TPU v7x, 32 devices: a whole 2x2x4 slice. The times are simulated.
32 devices in a mesh: vert: 8 (over z, x), tm: 4 (over y, core).
Axes of the slice: x: 2, y: 2, z: 4, core: 2. Of those that a mesh axis runs over, the one named last changes fastest.
Arguments:
- source: bfloat16 [10240, 512], P('vert', 'tm'), may hold values from -6 to 6
- band_taps: bfloat16 [2, 2, 65], replicated, may hold values from -0.75 to 0.75
- smooth_taps: bfloat16 [2, 65], replicated, may hold values from 0.0009 to 0.031
- parcel_ids: int32 [3, 10240], P(None, 'vert'), may hold values from 0 to 999, as said below
Outputs:
- envelope_coupling: float32 [4, 2, 1504, 1504], P('tm', None, 'vert')
Inputs may be any that keep to these rules, and one draw needn't show every extreme that they name: `parcel_ids`: row r = 0, 1, 2 gives each vertex's parcel in the atlas of 100, 400 or 1000 parcels (values below that count); every parcel of each atlas has at least one vertex.
All inputs are finite; a program needn't handle non-finite values.
Results may differ from a plain program's by a relative error of at most 0.0053.
Values may be sent and summed in bfloat16 or wider, within the bound.
No kernel may reach another device: no remote copies, remote signals or barrier semaphores. Data moves between devices by JAX's collectives and lax.ppermute only.
A program may use at most 64 MiB of HBM per device.

v0:
```python
from functools import partial
import math

import jax
import jax.numpy as jnp
from jax import lax
from jax.sharding import PartitionSpec as P

P1 = 100
P2 = 400
P3 = 1000
BANDS = 2
TAPS = 65
HALF = 32
LAG = 64
LAG_STEP = 1
NLAG = 129


EPSILON = 1e-05


def extended_2(cells, sides, width):
    for axis, dim in sides:
        count = lax.axis_size(axis)
        ends = count - 1
        head = lax.slice_in_dim(cells, 0, width, axis=dim)
        tail = lax.slice_in_dim(cells, cells.shape[dim] - width, cells.shape[dim], axis=dim)
        cells = jnp.concatenate(
            [
                lax.ppermute(tail, axis, [(i, (i + 1) % count) for i in range(ends)]),
                cells,
                lax.ppermute(head, axis, [((i + 1) % count, i) for i in range(ends)]),
            ],
            axis=dim,
        )
    return cells


def toeplitz_band(taps, n_out, n_in):
    period = jnp.concatenate([taps, jnp.zeros((n_in + 1 - taps.shape[0],), taps.dtype)])
    return jnp.tile(period, n_out)[: n_out * n_in].reshape(n_out, n_in)


def resolution_of(parcel):
    first = (parcel >= P1).astype(jnp.int32)
    second = (parcel >= P1 + P2).astype(jnp.int32)
    third = (parcel >= P1 + P2 + P3).astype(jnp.int32)
    return first + second + third


def centered_rows(extended, length):
    level_mean = jnp.mean(extended[:, :, LAG : LAG + length], axis=2, keepdims=True)
    centered = (extended - level_mean).astype(jnp.bfloat16)
    middle = centered[:, :, LAG : LAG + length]
    middle_wide = middle.astype(jnp.float32)
    spread = lax.rsqrt(jnp.mean(middle_wide * middle_wide, axis=2) + EPSILON)
    return (centered, middle, spread)


def make_fold(own_middle, own_spread, owner_start, par_dev, t_dev):
    kernel = own_middle.transpose(1, 0, 2).reshape(BANDS * par_dev, 1, t_dev)
    own_level = resolution_of(owner_start + lax.iota(jnp.int32, par_dev))

    def block_value(visiting, first):
        vis_middle = visiting[:, :, LAG : LAG + t_dev].astype(jnp.float32)
        vis_spread = lax.rsqrt(jnp.mean(vis_middle * vis_middle, axis=2) + EPSILON)
        inner = lax.conv_general_dilated(
            visiting,
            kernel,
            (LAG_STEP,),
            "VALID",
            dimension_numbers=("NCH", "OIH", "NCH"),
            feature_group_count=BANDS,
            preferred_element_type=jnp.float32,
        )
        inner = inner.reshape(par_dev, BANDS, par_dev, NLAG)
        energy = jnp.sum(inner * inner, axis=3).transpose(1, 2, 0)
        scale = own_spread.T[:, :, None] * vis_spread.T[:, None, :] / t_dev
        vis_level = resolution_of(first + lax.iota(jnp.int32, par_dev))
        same = ((own_level[:, None] == vis_level[None, :]) & (own_level[:, None] < 3)).astype(
            jnp.float32
        )
        return energy * scale * scale * same[None] / NLAG

    def guarded(visiting, first):
        result = block_value(visiting, first)
        return result

    def fold_rows(carry, piece, start):
        count = piece.shape[0] // par_dev

        def add_block(block_idx, total):
            first = block_idx * par_dev
            visiting = lax.dynamic_slice_in_dim(piece, block_idx * par_dev, par_dev, 0)
            slot = first // par_dev
            zero = jnp.int32(0)
            return lax.dynamic_update_slice(
                total, guarded(visiting, first)[None], (slot, zero, zero, zero)
            )

        return lax.fori_loop(0, count, add_block, carry)

    return fold_rows


def local(source, band_taps, smooth_taps, parcel_ids):
    vert_dev, t_dev = source.shape
    owners = lax.axis_size("vert")
    total_par = (P1 + P2 + P3 + owners - 1) // owners * owners
    par_dev = total_par // owners
    n_mid = t_dev + 2 * HALF
    n_in = t_dev + 4 * HALF
    first_rows = jax.vmap(partial(toeplitz_band, n_out=n_mid, n_in=n_in))(
        band_taps.reshape(2 * BANDS, TAPS)
    )
    first_mat = first_rows.transpose(2, 0, 1).reshape(n_in, 2 * BANDS * n_mid)
    second_rows = jax.vmap(partial(toeplitz_band, n_out=t_dev, n_in=n_mid))(smooth_taps)
    second_mat = second_rows.transpose(0, 2, 1)
    widened = extended_2(source, (("tm", 1),), 2 * HALF)
    block_rows = math.gcd(vert_dev, 128)

    def filter_block(block):
        wave = jnp.dot(block, first_mat, preferred_element_type=jnp.float32).reshape(
            block_rows, 2, BANDS, n_mid
        )
        power = (wave[:, 0] * wave[:, 0] + wave[:, 1] * wave[:, 1]).astype(jnp.bfloat16)
        return jnp.einsum(
            "vbu,but->vbt", power, second_mat, preferred_element_type=jnp.float32
        ).astype(jnp.bfloat16)

    envelope = lax.map(filter_block, widened.reshape(vert_dev // block_rows, block_rows, n_in))
    flat_env = envelope.reshape(vert_dev, BANDS * t_dev)
    offsets = jnp.array([0, P1, P1 + P2], dtype=jnp.int32)
    global_ids = parcel_ids + offsets[:, None]
    owner_start = lax.axis_index("vert") * par_dev
    empty = jnp.zeros((owners, BANDS, par_dev, par_dev), jnp.float32)

    def one_block(block_idx):
        wanted = block_idx * par_dev + lax.iota(jnp.int32, par_dev)
        hits = jnp.sum(
            (global_ids[:, None, :] == wanted[None, :, None]).astype(jnp.bfloat16), axis=0
        )
        return jnp.dot(hits, flat_env, preferred_element_type=jnp.float32)

    pooled = lax.map(
        one_block, jnp.arange(par_dev * lax.axis_size("vert") // par_dev, dtype=jnp.int32)
    )
    own_sums = lax.psum_scatter(
        pooled.reshape(par_dev * lax.axis_size("vert"), BANDS * t_dev),
        "vert",
        scatter_dimension=0,
        tiled=True,
    )
    own_env = own_sums.reshape(par_dev, BANDS, t_dev)
    own_ext = extended_2(own_env, (("tm", 2),), LAG)
    centered, own_middle, own_spread = centered_rows(own_ext, t_dev)
    fold_rows = make_fold(own_middle, own_spread, owner_start, par_dev, t_dev)
    blocks = fold_rows(empty, lax.all_gather(centered, "vert", axis=0, tiled=True), jnp.int32(0))
    coupling = blocks.transpose(1, 2, 0, 3).reshape(BANDS, par_dev, total_par)
    return coupling[None]


def solution(mesh):
    return jax.shard_map(
        local,
        mesh=mesh,
        in_specs=(P("vert", "tm"), P(), P(), P(None, "vert")),
        out_specs=P("tm", None, "vert", None),
        check_vma=False,
    )
```

profile of v0, /device:TPU:9, one launch (start us, length us, event | category | flops | bytes accessed | tf_op | source)
XLA Modules:
  0.0 351.6 jit_solution(13580460754429065313)
XLA Ops:
  6.5 2.0 fusion.27
  8.6 3.7 %collective-permute-start = (bf16[1280,64]{1,0:T(8,128)(2,1)}, bf16[1280,64]{1,0:T(8,128)(2,1)}, u32[]{:S(2)}, u32[]{:S(2)}) collective-permute-start(bf16[1280,64]{1,0:T(8,128)(2,1)} %get-tuple-element.348), channel_id=1, source_target_pairs={{0,1},{1,2},{2,3},{4,5},{5,6},{6,7},{8,9},{9,10},{10,11},{12,13},{... | collective-permute-start | bytes 491528 | tf_op jit(solution)/shard_map/ppermute | solution.py:31
  12.3 1.9 collective-permute-start.1
  18.3 2.7 collective-permute-done.1
  22.5 12.1 %while.38 = (s32[]{:T(128)}, bf16[10,128,2,128]{3,2,1,0:T(2,128)(2,1)}, bf16[10,128,256]{2,1,0:T(8,128)(2,1)S(1)}, bf16[256,768]{0,1:T(8,128)(2,1)S(1)}, bf16[2,192,128]{2,1,0:T(8,128)(2,1)S(1)}, /*index=5*/s32[]{:T(128)}) while((s32[]{:T(128)}, bf16[10,128,2,128]{3,2,1,0:T(2,128)(2,1)}, bf16[10,128,256]{2,1,0:T(8,128)(2,1)S(1)}, ...), condition=%wide.region_1.2_spmd, body=%wide.region_0.1_spmd.sunk | while | flops 63143936 | bytes 1540181 | solution.py:132
  35.7 15.7 %while.39 = (s32[]{:T(128)}, f32[8,188,256]{2,1,0:T(8,128)S(1)}, s32[3,1280]{1,0:T(4,128)S(1)}, s32[8]{0:T(128)S(1)}, bf16[1280,256]{1,0:T(8,128)(2,1)S(1)}, /*index=5*/s32[]{:T(128)}, s32[1]{0:T(128)}) while((s32[]{:T(128)}, f32[8,188,256]{2,1,0:T(8,128)S(1)}, s32[3,1280]{1,0:T(4,128)S(1)}, s32[8]{0:T(128)S(1)}, ...), condition=%wide.region_4.5_spmd, body=%wide.region_2.4_spmd.sunk | while | flops 125132992 | bytes 1841749 | solution.py:146
  51.6 33.5 %fusion.2 = f32[192,256]{1,0:T(8,128)S(1)} fusion(f32[1504,256]{1,0:T(8,128)S(1)} %reshape.143), kind=kCustom, calls=%all-reduce-scatter | all-reduce-scatter fusion | flops 393217 | bytes 1737216
  85.1 3.7 %collective-permute-start.4 = (f32[28,256]{1,0:T(8,128)S(1)}, f32[28,256]{1,0:T(8,128)S(1)}, u32[]{:S(2)}, u32[]{:S(2)}) collective-permute-start(f32[28,256]{1,0:T(8,128)S(1)} %slice.55), channel_id=1, source_target_pairs={{0,4},{4,8},{8,12},{12,16},{16,20},{20,24},{24,28},{1,5},{5,9},{9,... | collective-permute-start | bytes 86024
  91.7 5.5 %collective-permute-start.2 = (f32[188,2,64]{2,1,0:T(2,128)S(1)}, f32[188,2,64]{2,1,0:T(2,128)S(1)}, u32[]{:S(2)}, u32[]{:S(2)}) collective-permute-start(f32[188,2,64]{2,1,0:T(2,128)S(1)} %get-tuple-element.350), channel_id=1, source_target_pairs={{0,1},{1,2},{2,3},{4,5},{5,6},{6,7},{8,9},{9,10},{10,11},{12,13},{... | collective-permute-start | bytes 288776 | tf_op jit(solution)/shard_map/ppermute | solution.py:31
  97.2 1.9 collective-permute-start.3
  99.8 4.4 %collective-permute-done.3 = f32[188,2,64]{2,1,0:T(2,128)S(1)} collective-permute-done((f32[188,2,64]{2,1,0:T(2,128)S(1)}, f32[188,2,64]{2,1,0:T(2,128)S(1)}, u32[]{:S(2)}, u32[]{:S(2)}) %collective-permute-start.3) | collective-permute-done | bytes 96288 | tf_op jit(solution)/shard_map/ppermute | solution.py:33
  104.2 1.6 fusion.26
  109.2 39.0 %all-gather.2.cloned.1.call-done = bf16[1504,2,256]{2,1,0:T(2,128)(2,1)} async-done(((bf16[188,2,256]{2,1,0:T(2,128)(2,1)}), bf16[1504,2,256]{2,1,0:T(2,128)(2,1)}) %all-gather.2.cloned.1.call-update) | async-done | bytes 1540112 | tf_op jit(solution)/shard_map/all_gather | solution.py:159
  148.1 2.4 broadcast_in_dim.52
  150.6 187.7 %while.40 = (s32[]{:T(128)}, f32[8,2,188,188]{2,1,3,0:T(2,128)}, bf16[1504,2,256]{2,1,0:T(2,128)(2,1)}, bf16[376,1,128]{0,2,1:T(8,128)(2,1)S(1)}, f32[188,2]{0,1...) while((s32[]{:T(128)}, f32[8,2,188,188]{2,1,3,0:T(2,128)}, ...), condition=%wide.region_11.12_spmd.clone, body=%wide.region_8.11_spmd.clone.sunk | while | flops 4687840256 | bytes 2988515 | solution.py:102
  154.1 18.2 %multiply_reduce_fusion.5 = f32[188,376]{1,0:T(8,128)S(1)} fusion(bf16[188,2,256]{0,1,2:T(2,128)(2,1)S(1)} %copy.64, s32[376]{0:T(512)S(1)} %get-tuple-element.532, bf16[376,128]{0,1:T(8,128)(2,1)S(1)} %bitcast.102), kind=kOutput, calls=%fused_computation.18.clone.1 | convolution fusion | flops 4687160320 | bytes 573024 | tf_op jit(solution)/shard_map/while/body/eval_jaxpr/conv_general_dilated | solution.py:68
  177.5 18.2 %multiply_reduce_fusion.5 = f32[188,376]{1,0:T(8,128)S(1)} fusion(bf16[188,2,256]{0,1,2:T(2,128)(2,1)S(1)} %copy.64, s32[376]{0:T(512)S(1)} %get-tuple-element.532, bf16[376,128]{0,1:T(8,128)(2,1)S(1)} %bitcast.102), kind=kOutput, calls=%fused_computation.18.clone.1 | convolution fusion | flops 4687160320 | bytes 573024 | tf_op jit(solution)/shard_map/while/body/eval_jaxpr/conv_general_dilated | solution.py:68
  201.0 18.2 %multiply_reduce_fusion.5 = f32[188,376]{1,0:T(8,128)S(1)} fusion(bf16[188,2,256]{0,1,2:T(2,128)(2,1)S(1)} %copy.64, s32[376]{0:T(512)S(1)} %get-tuple-element.532, bf16[376,128]{0,1:T(8,128)(2,1)S(1)} %bitcast.102), kind=kOutput, calls=%fused_computation.18.clone.1 | convolution fusion | flops 4687160320 | bytes 573024 | tf_op jit(solution)/shard_map/while/body/eval_jaxpr/conv_general_dilated | solution.py:68
  224.4 18.2 %multiply_reduce_fusion.5 = f32[188,376]{1,0:T(8,128)S(1)} fusion(bf16[188,2,256]{0,1,2:T(2,128)(2,1)S(1)} %copy.64, s32[376]{0:T(512)S(1)} %get-tuple-element.532, bf16[376,128]{0,1:T(8,128)(2,1)S(1)} %bitcast.102), kind=kOutput, calls=%fused_computation.18.clone.1 | convolution fusion | flops 4687160320 | bytes 573024 | tf_op jit(solution)/shard_map/while/body/eval_jaxpr/conv_general_dilated | solution.py:68
  247.9 18.2 %multiply_reduce_fusion.5 = f32[188,376]{1,0:T(8,128)S(1)} fusion(bf16[188,2,256]{0,1,2:T(2,128)(2,1)S(1)} %copy.64, s32[376]{0:T(512)S(1)} %get-tuple-element.532, bf16[376,128]{0,1:T(8,128)(2,1)S(1)} %bitcast.102), kind=kOutput, calls=%fused_computation.18.clone.1 | convolution fusion | flops 4687160320 | bytes 573024 | tf_op jit(solution)/shard_map/while/body/eval_jaxpr/conv_general_dilated | solution.py:68
  271.4 18.2 %multiply_reduce_fusion.5 = f32[188,376]{1,0:T(8,128)S(1)} fusion(bf16[188,2,256]{0,1,2:T(2,128)(2,1)S(1)} %copy.64, s32[376]{0:T(512)S(1)} %get-tuple-element.532, bf16[376,128]{0,1:T(8,128)(2,1)S(1)} %bitcast.102), kind=kOutput, calls=%fused_computation.18.clone.1 | convolution fusion | flops 4687160320 | bytes 573024 | tf_op jit(solution)/shard_map/while/body/eval_jaxpr/conv_general_dilated | solution.py:68
  294.9 18.2 %multiply_reduce_fusion.5 = f32[188,376]{1,0:T(8,128)S(1)} fusion(bf16[188,2,256]{0,1,2:T(2,128)(2,1)S(1)} %copy.64, s32[376]{0:T(512)S(1)} %get-tuple-element.532, bf16[376,128]{0,1:T(8,128)(2,1)S(1)} %bitcast.102), kind=kOutput, calls=%fused_computation.18.clone.1 | convolution fusion | flops 4687160320 | bytes 573024 | tf_op jit(solution)/shard_map/while/body/eval_jaxpr/conv_general_dilated | solution.py:68
  318.3 18.2 %multiply_reduce_fusion.5 = f32[188,376]{1,0:T(8,128)S(1)} fusion(bf16[188,2,256]{0,1,2:T(2,128)(2,1)S(1)} %copy.64, s32[376]{0:T(512)S(1)} %get-tuple-element.532, bf16[376,128]{0,1:T(8,128)(2,1)S(1)} %bitcast.102), kind=kOutput, calls=%fused_computation.18.clone.1 | convolution fusion | flops 4687160320 | bytes 573024 | tf_op jit(solution)/shard_map/while/body/eval_jaxpr/conv_general_dilated | solution.py:68
  338.3 6.5 %copy.45 = f32[1,2,188,1504]{3,1,2,0:T(2,128)} copy(f32[1,2,188,1504]{2,1,3,0:T(2,128)} %bitcast.97) | data formatting | bytes 4524032 | tf_op jit(solution)/shard_map/broadcast_in_dim;reshape | solution.py:161
  (265 shorter events, 76.7 us)
Async XLA Ops:
  6.5 141.6 %all-gather.2.cloned.1.call-start = ((), (), s32[]{:S(2)}) async-start(), calls=%async_computation | async-start | bytes 1732608 | tf_op jit(solution)/shard_map/all_gather | solution.py:159
  8.6 9.7 %collective-permute-start = (bf16[1280,64]{1,0:T(8,128)(2,1)}, bf16[1280,64]{1,0:T(8,128)(2,1)}, u32[]{:S(2)}, u32[]{:S(2)}) collective-permute-start(bf16[1280,64]{1,0:T(8,128)(2,1)} %get-tuple-element.348), channel_id=1, source_target_pairs={{0,1},{1,2},{2,3},{4,5},{5,6},{6,7},{8,9},{9,10},{10,11},{12,13},{... | collective-permute-start | bytes 491528 | tf_op jit(solution)/shard_map/ppermute | solution.py:31
  12.3 8.7 %collective-permute-start.1 = (bf16[1280,64]{1,0:T(8,128)(2,1)}, bf16[1280,64]{1,0:T(8,128)(2,1)}, u32[]{:S(2)}, u32[]{:S(2)}) collective-permute-start(bf16[1280,64]{1,0:T(8,128)(2,1)} %get-tuple-element.349), channel_id=1, source_target_pairs={{1,0},{2,1},{3,2},{5,4},{6,5},{7,6},{9,8},{10,9},{11,10},{13,12},{... | collective-permute-start | bytes 491528 | tf_op jit(solution)/shard_map/ppermute | solution.py:33
  51.6 37.2 %copy-start.6 = (u32[32]{0:T(128)S(1)}, u32[32]{0:T(128)}, u32[]{:S(2)}) copy-start(u32[32]{0:T(128)} %constant.229) | copy-start | bytes 388
  85.1 5.6 %collective-permute-start.4 = (f32[28,256]{1,0:T(8,128)S(1)}, f32[28,256]{1,0:T(8,128)S(1)}, u32[]{:S(2)}, u32[]{:S(2)}) collective-permute-start(f32[28,256]{1,0:T(8,128)S(1)} %slice.55), channel_id=1, source_target_pairs={{0,4},{4,8},{8,12},{12,16},{16,20},{20,24},{24,28},{1,5},{5,9},{9,... | collective-permute-start | bytes 86024
  91.7 8.1 %collective-permute-start.2 = (f32[188,2,64]{2,1,0:T(2,128)S(1)}, f32[188,2,64]{2,1,0:T(2,128)S(1)}, u32[]{:S(2)}, u32[]{:S(2)}) collective-permute-start(f32[188,2,64]{2,1,0:T(2,128)S(1)} %get-tuple-element.350), channel_id=1, source_target_pairs={{0,1},{1,2},{2,3},{4,5},{5,6},{6,7},{8,9},{9,10},{10,11},{12,13},{... | collective-permute-start | bytes 288776 | tf_op jit(solution)/shard_map/ppermute | solution.py:31
  97.2 6.9 %collective-permute-start.3 = (f32[188,2,64]{2,1,0:T(2,128)S(1)}, f32[188,2,64]{2,1,0:T(2,128)S(1)}, u32[]{:S(2)}, u32[]{:S(2)}) collective-permute-start(f32[188,2,64]{2,1,0:T(2,128)S(1)} %get-tuple-element.351), channel_id=1, source_target_pairs={{1,0},{2,1},{3,2},{5,4},{6,5},{7,6},{9,8},{10,9},{11,10},{13,12},{... | collective-permute-start | bytes 288776 | tf_op jit(solution)/shard_map/ppermute | solution.py:33
  108.5 42.0 %copy-start.7 = (s32[376]{0:T(512)S(1)}, s32[376]{0:T(512)}, u32[]{:S(2)}) copy-start(s32[376]{0:T(512)} %constant.198.clone.2) | copy-start | bytes 4516
  154.1 18.7 %copy-start.5 = (pred[188]{0:T(512)(128)(4,1)S(1)}, pred[188]{0:T(512)(128)(4,1)}, u32[]{:S(2)}) copy-start(pred[188]{0:T(512)(128)(4,1)} %broadcast_compare_fusion.2) | copy-start | bytes 568 | tf_op jit(solution)/shard_map/while
  154.1 18.8 %copy-start.4 = (f32[188,2]{0,1:T(2,128)S(1)}, f32[188,2]{0,1:T(2,128)}, u32[]{:S(2)}) copy-start(f32[188,2]{0,1:T(2,128)} %get-tuple-element.524) | copy-start | bytes 4516 | tf_op jit(solution)/shard_map/while
  177.5 18.7 %copy-start.5 = (pred[188]{0:T(512)(128)(4,1)S(1)}, pred[188]{0:T(512)(128)(4,1)}, u32[]{:S(2)}) copy-start(pred[188]{0:T(512)(128)(4,1)} %broadcast_compare_fusion.2) | copy-start | bytes 568 | tf_op jit(solution)/shard_map/while
  177.5 18.8 %copy-start.4 = (f32[188,2]{0,1:T(2,128)S(1)}, f32[188,2]{0,1:T(2,128)}, u32[]{:S(2)}) copy-start(f32[188,2]{0,1:T(2,128)} %get-tuple-element.524) | copy-start | bytes 4516 | tf_op jit(solution)/shard_map/while
  201.0 18.7 %copy-start.5 = (pred[188]{0:T(512)(128)(4,1)S(1)}, pred[188]{0:T(512)(128)(4,1)}, u32[]{:S(2)}) copy-start(pred[188]{0:T(512)(128)(4,1)} %broadcast_compare_fusion.2) | copy-start | bytes 568 | tf_op jit(solution)/shard_map/while
  201.0 18.8 %copy-start.4 = (f32[188,2]{0,1:T(2,128)S(1)}, f32[188,2]{0,1:T(2,128)}, u32[]{:S(2)}) copy-start(f32[188,2]{0,1:T(2,128)} %get-tuple-element.524) | copy-start | bytes 4516 | tf_op jit(solution)/shard_map/while
  224.4 18.7 %copy-start.5 = (pred[188]{0:T(512)(128)(4,1)S(1)}, pred[188]{0:T(512)(128)(4,1)}, u32[]{:S(2)}) copy-start(pred[188]{0:T(512)(128)(4,1)} %broadcast_compare_fusion.2) | copy-start | bytes 568 | tf_op jit(solution)/shard_map/while
  224.4 18.8 %copy-start.4 = (f32[188,2]{0,1:T(2,128)S(1)}, f32[188,2]{0,1:T(2,128)}, u32[]{:S(2)}) copy-start(f32[188,2]{0,1:T(2,128)} %get-tuple-element.524) | copy-start | bytes 4516 | tf_op jit(solution)/shard_map/while
  247.9 18.7 %copy-start.5 = (pred[188]{0:T(512)(128)(4,1)S(1)}, pred[188]{0:T(512)(128)(4,1)}, u32[]{:S(2)}) copy-start(pred[188]{0:T(512)(128)(4,1)} %broadcast_compare_fusion.2) | copy-start | bytes 568 | tf_op jit(solution)/shard_map/while
  247.9 18.8 %copy-start.4 = (f32[188,2]{0,1:T(2,128)S(1)}, f32[188,2]{0,1:T(2,128)}, u32[]{:S(2)}) copy-start(f32[188,2]{0,1:T(2,128)} %get-tuple-element.524) | copy-start | bytes 4516 | tf_op jit(solution)/shard_map/while
  271.4 18.7 %copy-start.5 = (pred[188]{0:T(512)(128)(4,1)S(1)}, pred[188]{0:T(512)(128)(4,1)}, u32[]{:S(2)}) copy-start(pred[188]{0:T(512)(128)(4,1)} %broadcast_compare_fusion.2) | copy-start | bytes 568 | tf_op jit(solution)/shard_map/while
  271.4 18.8 %copy-start.4 = (f32[188,2]{0,1:T(2,128)S(1)}, f32[188,2]{0,1:T(2,128)}, u32[]{:S(2)}) copy-start(f32[188,2]{0,1:T(2,128)} %get-tuple-element.524) | copy-start | bytes 4516 | tf_op jit(solution)/shard_map/while
  294.9 18.7 %copy-start.5 = (pred[188]{0:T(512)(128)(4,1)S(1)}, pred[188]{0:T(512)(128)(4,1)}, u32[]{:S(2)}) copy-start(pred[188]{0:T(512)(128)(4,1)} %broadcast_compare_fusion.2) | copy-start | bytes 568 | tf_op jit(solution)/shard_map/while
  294.9 18.8 %copy-start.4 = (f32[188,2]{0,1:T(2,128)S(1)}, f32[188,2]{0,1:T(2,128)}, u32[]{:S(2)}) copy-start(f32[188,2]{0,1:T(2,128)} %get-tuple-element.524) | copy-start | bytes 4516 | tf_op jit(solution)/shard_map/while
  318.3 18.7 %copy-start.5 = (pred[188]{0:T(512)(128)(4,1)S(1)}, pred[188]{0:T(512)(128)(4,1)}, u32[]{:S(2)}) copy-start(pred[188]{0:T(512)(128)(4,1)} %broadcast_compare_fusion.2) | copy-start | bytes 568 | tf_op jit(solution)/shard_map/while
  318.3 18.8 %copy-start.4 = (f32[188,2]{0,1:T(2,128)S(1)}, f32[188,2]{0,1:T(2,128)}, u32[]{:S(2)}) copy-start(f32[188,2]{0,1:T(2,128)} %get-tuple-element.524) | copy-start | bytes 4516 | tf_op jit(solution)/shard_map/while
  (25 other events, 450.5 us)
Sparse Core Ops, SparseCore 0:
  105.9 42.2 all-gather.1
where the time goes:
time: 354 us; the launch traced here: 352 us
  matrix products  153 us (43%)
  waiting for transfers between devices  47.3 us (13%)
  local copies, waits for them, and re-layouts  45.9 us (13%)
  other arithmetic  34.8 us (10%)
  blocking collectives  33.5 us (9%)
  starting transfers between devices  16.7 us (5%)
  between operations  14.3 us (4%)
  loops' own time  6.47 us (2%)
    conv_general_dilated x8, matrix products, block_value(): lax.conv_general_dilated(visiting, kernel, (LAG_STEP,), 'VALID', dimensio...  145 us
    all_gather x1, waiting for transfers between devices, local(): lax.all_gather(centered, 'vert', axis=0, tiled=True)  39 us
    unnamed x1, blocking collectives  33.5 us
    dynamic_slice x16, local copies, waits for them, and re-layouts, add_block(): visiting = lax.dynamic_slice_in_dim(piece, block_idx * par_dev, par_dev, 0)  12.3 us
    dynamic_update_slice x8, other arithmetic, add_block(): lax.dynamic_update_slice(total, guarded(visiting, first)[None], (slot, ze...  9.41 us
    ppermute x2, starting transfers between devices, extended_2(): lax.ppermute(tail, axis, [(i, (i + 1) % count) for i in range(ends)])  9.2 us
    ppermute x2, waiting for transfers between devices, extended_2(): lax.ppermute(head, axis, [((i + 1) % count, i) for i in range(ends)])  7.1 us
  transfers between devices with their start and end apart: 6, of which 5 were waited for; matrix products, arithmetic and copies ran while one was open for 2% of the time, Pallas kernels for 0%

commit v1 on v0

--- a/solution.py
+++ b/solution.py
@@ -1,9 +1,13 @@
 from functools import partial
 import math
+
+import numpy as np
 
 import jax
 import jax.numpy as jnp
 from jax import lax
+from jax.experimental import pallas as pl
+from jax.experimental.pallas import tpu as pltpu
 from jax.sharding import PartitionSpec as P
 
 P1 = 100
@@ -58,50 +62,238 @@
     return (centered, middle, spread)
 
 
-def make_fold(own_middle, own_spread, owner_start, par_dev, t_dev):
-    kernel = own_middle.transpose(1, 0, 2).reshape(BANDS * par_dev, 1, t_dev)
-    own_level = resolution_of(owner_start + lax.iota(jnp.int32, par_dev))
-
-    def block_value(visiting, first):
-        vis_middle = visiting[:, :, LAG : LAG + t_dev].astype(jnp.float32)
-        vis_spread = lax.rsqrt(jnp.mean(vis_middle * vis_middle, axis=2) + EPSILON)
-        inner = lax.conv_general_dilated(
-            visiting,
-            kernel,
-            (LAG_STEP,),
-            "VALID",
-            dimension_numbers=("NCH", "OIH", "NCH"),
-            feature_group_count=BANDS,
-            preferred_element_type=jnp.float32,
+GROUP = (P1 + P2 + 127) // 128 * 128
+TILE = 256
+PERIOD = 127
+HIGH = lax.Precision.HIGHEST
+BF16 = jnp.bfloat16
+F32 = jnp.float32
+
+
+def fourier_constants():
+    n = 256
+    freq = np.arange(129)
+    angle = 2 * np.pi * np.outer(np.arange(n), freq) / n
+    cos, sin = np.cos(angle), np.sin(angle)
+    weight = np.full(129, 2.0 / n)
+    weight[[0, 128]] = 1.0 / n
+    lags = np.arange(128)
+    twice = np.where(lags == 0, 1.0, 2.0)
+    from_power = weight[:, None] * cos[lags].T * twice
+    real = (from_power @ cos[lags]) * weight
+    imag = -(from_power @ sin[lags]) * weight
+    to_weights = np.concatenate([real[:, :128], real[:, 128:], imag[:, 1:128]], axis=1)
+    inverse = np.concatenate([weight[:, None] * cos.T, -weight[:, None] * sin.T], axis=0)
+    packed = np.concatenate([cos[:, :128], cos[:, 128:], -sin[:, 1:128]], axis=1).T
+    near = packed * (np.arange(n) < 129)
+    factors = np.concatenate([near, packed], axis=0)
+    high = factors.astype(np.float32).astype(jnp.bfloat16)
+    low = (factors - high.astype(np.float64)).astype(np.float32).astype(jnp.bfloat16)
+    both = np.concatenate([high, low], axis=0)
+    forward = np.concatenate([cos, -sin], axis=1).astype(np.float32)
+    return forward, to_weights.astype(np.float32), inverse.astype(np.float32), both
+
+
+FORWARD, TO_WEIGHTS, INVERSE, FACTORS = fourier_constants()
+
+
+def lag_weights_kernel(rows, middle_ref, out_ref):
+    middle = middle_ref[...]
+    lane = lax.broadcasted_iota(jnp.int32, middle.shape, 1)
+    row = lax.broadcasted_iota(jnp.int32, (128, 128), 0)
+    col = lax.broadcasted_iota(jnp.int32, (128, 128), 1)
+
+    def one(d, turned):
+        further = pltpu.roll(turned, 127, 1)
+        partner = jnp.where(lane <= PERIOD - d, turned, further)
+        product = (middle * partner).astype(BF16)
+        keep = (row > col) & ((row <= PERIOD - d) == (col < PERIOD - d))
+        sums = jnp.dot(product, keep.astype(F32).astype(BF16), preferred_element_type=F32)
+        scale = jnp.where(d == 0, 1.0, 2.0).astype(F32)
+        out_ref[:, pl.ds(pl.multiple_of(d * 128, 128), 128)] = (sums * scale).astype(BF16)
+        return further
+
+    lax.fori_loop(0, 64, one, middle)
+
+
+def lag_weights(middle):
+    rows = middle.shape[0]
+    return pl.pallas_call(
+        partial(lag_weights_kernel, rows),
+        out_shape=jax.ShapeDtypeStruct((rows, 64 * 128), BF16),
+        in_specs=[pl.BlockSpec(memory_space=pltpu.VMEM)],
+        out_specs=pl.BlockSpec(memory_space=pltpu.VMEM),
+        compiler_params=pltpu.CompilerParams(vmem_limit_bytes=40 * 2**20),
+        name="lag_weights",
+    )(middle)
+
+
+def coupling_kernel(
+    par_dev,
+    bounds_ref,
+    lag_ref,
+    freq_ref,
+    edge_ref,
+    edge_sum_ref,
+    own_ref,
+    own_level_ref,
+    rows_ref,
+    mu_ref,
+    other_ref,
+    other_level_ref,
+    factor_ref,
+    out_ref,
+    result,
+    near,
+    far,
+    near_turn,
+    far_turn,
+    change,
+):
+    result[...] = jnp.zeros_like(result)
+    padded = result.shape[1]
+
+    def block(step, carry):
+        band = lax.rem(step, BANDS)
+        first = pl.multiple_of((step // BANDS) * TILE, TILE)
+        columns = rows_ref[band, pl.ds(first, TILE), :].astype(F32).T
+        narrow = columns.astype(BF16)
+        near[0:PERIOD] = columns[0:PERIOD]
+        near[PERIOD : PERIOD + 64] = columns[0:64]
+        far[0:PERIOD] = columns[129:256]
+        far[PERIOD : PERIOD + 64] = columns[129:193]
+        for r in range(16):
+            near_turn[r] = near[r : r + 176].astype(BF16)
+            far_turn[r] = far[r : r + 176].astype(BF16)
+        for d in range(64):
+            a, r = divmod(d, 16)
+            change[d * 128 : (d + 1) * 128] = (
+                far_turn[0, 0:128] * far_turn[r, 16 * a : 16 * a + 128]
+                - near_turn[0, 0:128] * near_turn[r, 16 * a : 16 * a + 128]
+            )
+        total = jnp.dot(lag_ref[band], change[...], preferred_element_type=F32)
+        spectra = jnp.dot(factor_ref[0:512], narrow, preferred_element_type=F32) + jnp.dot(
+            factor_ref[512:1024], narrow, preferred_element_type=F32
         )
-        inner = inner.reshape(par_dev, BANDS, par_dev, NLAG)
-        energy = jnp.sum(inner * inner, axis=3).transpose(1, 2, 0)
-        scale = own_spread.T[:, :, None] * vis_spread.T[:, None, :] / t_dev
-        vis_level = resolution_of(first + lax.iota(jnp.int32, par_dev))
-        same = ((own_level[:, None] == vis_level[None, :]) & (own_level[:, None] < 3)).astype(
-            jnp.float32
-        )
-        return energy * scale * scale * same[None] / NLAG
-
-    def guarded(visiting, first):
-        result = block_value(visiting, first)
-        return result
-
-    def fold_rows(carry, piece, start):
-        count = piece.shape[0] // par_dev
-
-        def add_block(block_idx, total):
-            first = block_idx * par_dev
-            visiting = lax.dynamic_slice_in_dim(piece, block_idx * par_dev, par_dev, 0)
-            slot = first // par_dev
-            zero = jnp.int32(0)
-            return lax.dynamic_update_slice(
-                total, guarded(visiting, first)[None], (slot, zero, zero, zero)
-            )
-
-        return lax.fori_loop(0, count, add_block, carry)
-
-    return fold_rows
+        low_a, high_a, low_c, high_c = (spectra[128 * k : 128 * (k + 1)] for k in range(4))
+        at_zero = lax.broadcasted_iota(jnp.int32, (128, TILE), 0) == 0
+        cross = high_a * high_c
+        real = low_a * low_c + jnp.where(at_zero, 0.0, cross)
+        imag = jnp.where(at_zero, cross, low_a * high_c - high_a * low_c)
+        both = jnp.concatenate([real, imag], axis=0)
+        big = both.astype(BF16)
+        small = (both - big.astype(F32)).astype(BF16)
+        weights = freq_ref[band]
+        total += jnp.dot(weights[:, 0:256], big, preferred_element_type=F32)
+        total += jnp.dot(weights[:, 256:512], big, preferred_element_type=F32)
+        total += jnp.dot(weights[:, 0:256], small, preferred_element_type=F32)
+        mixed = jnp.dot(edge_ref[band], narrow, preferred_element_type=F32)
+        mu = mu_ref[band, :, pl.ds(first, TILE)]
+        total += mu * (mu * edge_sum_ref[band] - 2.0 * mixed)
+        same = own_level_ref[...] == other_level_ref[:, pl.ds(first, TILE)]
+        scaled = total * own_ref[band] * other_ref[band, :, pl.ds(first, TILE)]
+        result[band, :, pl.ds(first, TILE)] = jnp.where(same, scaled, 0.0)
+        return carry
+
+    lax.fori_loop(bounds_ref[0] * BANDS, bounds_ref[1] * BANDS, block, 0)
+    split = P1 + P2
+    width = out_ref.shape[2]
+    for band in range(BANDS):
+        out_ref[band, :, 0:split] = result[band, 0:par_dev, 0:split]
+        out_ref[band, :, split:width] = result[band, 0:par_dev, GROUP : GROUP + width - split]
+
+
+def coupling_call(par_dev, total_par, bounds, *operands):
+    padded, width = operands[0].shape[1], operands[6].shape[1]
+    return pl.pallas_call(
+        partial(coupling_kernel, par_dev),
+        out_shape=jax.ShapeDtypeStruct((BANDS, par_dev, total_par), F32),
+        in_specs=[pl.BlockSpec(memory_space=pltpu.SMEM)]
+        + [pl.BlockSpec(memory_space=pltpu.VMEM)] * len(operands),
+        out_specs=pl.BlockSpec(memory_space=pltpu.VMEM),
+        scratch_shapes=[
+            pltpu.VMEM((BANDS, padded, width), F32),
+            pltpu.VMEM((192, TILE), F32),
+            pltpu.VMEM((192, TILE), F32),
+            pltpu.VMEM((16, 176, TILE), BF16),
+            pltpu.VMEM((16, 176, TILE), BF16),
+            pltpu.VMEM((64 * 128, TILE), BF16),
+        ],
+        compiler_params=pltpu.CompilerParams(vmem_limit_bytes=56 * 2**20),
+        name="coupling",
+    )(bounds, *operands)
+
+
+def grouped(cells, axis):
+    split, total = P1 + P2, cells.shape[axis]
+    end = GROUP + (total - split + TILE - 1) // TILE * TILE
+    pads = lambda n: [(0, n if k == axis else 0) for k in range(cells.ndim)]
+    return jnp.concatenate(
+        [
+            jnp.pad(lax.slice_in_dim(cells, 0, split, axis=axis), pads(GROUP - split)),
+            jnp.pad(
+                lax.slice_in_dim(cells, split, total, axis=axis), pads(end - GROUP - total + split)
+            ),
+        ],
+        axis=axis,
+    )
+
+
+def coupling_of(gathered, own_centered, owner_start, t_dev):
+    total_par, par_dev = gathered.shape[0], own_centered.shape[0]
+    padded = (par_dev + 15) // 16 * 16
+    window, windows = lax.axis_index("tm"), lax.axis_size("tm")
+    place = lax.iota(jnp.int32, t_dev + 2 * LAG)
+    outside = ((window == 0) & (place < LAG)) | ((window == windows - 1) & (place >= LAG + t_dev))
+
+    def scales(cells):
+        middle = cells[:, :, LAG : LAG + t_dev].astype(F32)
+        spread = lax.rsqrt(jnp.mean(middle * middle, axis=2) + EPSILON)
+        power = jnp.exp2(jnp.floor(jnp.log2(spread)))
+        rest = spread / power
+        return power, rest * rest
+
+    power, rest = scales(gathered)
+    mu = jnp.where(window == 0, -gathered[:, :, 0].astype(F32), 0.0)
+    mu = jnp.where(window == windows - 1, -gathered[:, :, -1].astype(F32), mu) * power
+    inner = jnp.where(outside, 0.0, gathered.astype(F32)) * power[:, :, None]
+    rows = grouped(inner.astype(BF16).transpose(1, 0, 2), 1)
+    other_mu = grouped(mu.T[:, None, :], 2)
+    other = grouped(rest.T[:, None, :], 2)
+    other_level = grouped(resolution_of(lax.iota(jnp.int32, total_par))[None, :] - 3, 1) + 3
+
+    own_power, own_rest = scales(own_centered)
+    middle = own_centered[:, :, LAG : LAG + t_dev].astype(F32) * own_power[:, :, None]
+    middle = jnp.pad(middle.transpose(1, 0, 2), ((0, 0), (0, padded - par_dev), (0, 0)))
+    own = jnp.pad(own_rest.T / (t_dev * t_dev * NLAG), ((0, 0), (0, padded - par_dev)))[:, :, None]
+    own_level = resolution_of(owner_start + lax.iota(jnp.int32, padded))
+    own_level = jnp.where(own_level < 3, own_level, -1)[:, None]
+
+    flat = middle.reshape(BANDS * padded, t_dev)
+    lag = lag_weights(flat).reshape(BANDS, padded, 64 * 128)
+    spectrum = jnp.dot(flat, FORWARD[:t_dev], precision=HIGH)
+    power_spectrum = spectrum[:, :129] ** 2 + spectrum[:, 129:] ** 2
+    weights = jnp.dot(power_spectrum, TO_WEIGHTS, precision=HIGH).reshape(BANDS, padded, 256)
+    big = weights.astype(BF16)
+    freq = jnp.concatenate([big, (weights - big.astype(F32)).astype(BF16)], axis=2)
+    step = lax.iota(jnp.int32, t_dev)[:, None] + lax.iota(jnp.int32, NLAG)[None, :]
+    sums = jnp.dot(flat, jnp.take(outside, step).astype(F32), precision=HIGH)
+    edge_sum = jnp.sum(sums * sums, axis=1).reshape(BANDS, padded, 1)
+    sums_spectrum = jnp.dot(sums, FORWARD[:NLAG], precision=HIGH)
+    (a, b), (c, d) = ((x[:, :129], x[:, 129:]) for x in (sums_spectrum, spectrum))
+    turned = jnp.concatenate([a * c - b * d, a * d + b * c], axis=1)
+    edge = jnp.dot(turned, INVERSE, precision=HIGH).astype(BF16).reshape(BANDS, padded, 256)
+
+    level_first = resolution_of(owner_start)
+    level_last = resolution_of(jnp.minimum(owner_start + par_dev, P1 + P2 + P3) - 1)
+    end = rows.shape[1] // TILE
+    lo = jnp.where(level_first < 2, 0, GROUP // TILE)
+    hi = jnp.where(level_last < 2, GROUP // TILE, end)
+    bounds = jnp.stack([lo, hi]).astype(jnp.int32)
+    return coupling_call(
+        par_dev, total_par, bounds, lag, freq, edge, edge_sum, own, own_level,
+        rows, other_mu, other, other_level, jnp.asarray(FACTORS),
+    )
 
 
 def local(source, band_taps, smooth_taps, parcel_ids):
@@ -134,7 +326,6 @@
     offsets = jnp.array([0, P1, P1 + P2], dtype=jnp.int32)
     global_ids = parcel_ids + offsets[:, None]
     owner_start = lax.axis_index("vert") * par_dev
-    empty = jnp.zeros((owners, BANDS, par_dev, par_dev), jnp.float32)
 
     def one_block(block_idx):
         wanted = block_idx * par_dev + lax.iota(jnp.int32, par_dev)
@@ -155,9 +346,8 @@
     own_env = own_sums.reshape(par_dev, BANDS, t_dev)
     own_ext = extended_2(own_env, (("tm", 2),), LAG)
     centered, own_middle, own_spread = centered_rows(own_ext, t_dev)
-    fold_rows = make_fold(own_middle, own_spread, owner_start, par_dev, t_dev)
-    blocks = fold_rows(empty, lax.all_gather(centered, "vert", axis=0, tiled=True), jnp.int32(0))
-    coupling = blocks.transpose(1, 2, 0, 3).reshape(BANDS, par_dev, total_par)
+    gathered = lax.all_gather(centered, "vert", axis=0, tiled=True)
+    coupling = coupling_of(gathered, centered, owner_start, t_dev)
     return coupling[None]
 
 

time: 354 us -> 278 us (0.79)
  matrix products: 153 us -> 12.3 us
  local copies, waits for them, and re-layouts: 45.9 us -> 125 us
  Pallas kernels: 0 us -> 43 us
  waiting for transfers between devices: 47.3 us -> 6.41 us
  other arithmetic: 34.8 us -> 18.1 us
    conv_general_dilated x8 -> x0, matrix products: 145 us -> none  [block_value(): lax.conv_general_dilated(visiting, kernel, (LAG_STEP,), 'VALID', dimensio...]
    gather x0 -> x2, local copies, waits for them, and re-layouts: none -> 91.9 us  [coupling_of(): sums = jnp.dot(flat, jnp.take(outside, step).astype(F32), precision=HIGH)]
    pallas_call x0 -> x2, Pallas kernels: none -> 43 us  [the longest x1 27.2 us: coupling_call(): pl.pallas_call(partial(coupling_kernel, par_dev), out_shape=jax.ShapeDtyp...]
    all_gather x1, waiting for transfers between devices: 39 us -> 0.01 us  [local(): gathered = lax.all_gather(centered, 'vert', axis=0, tiled=True)]
    dynamic_slice x16 -> x0, local copies, waits for them, and re-layouts: 12.3 us -> none  [add_block(): visiting = lax.dynamic_slice_in_dim(piece, block_idx * par_dev, par_dev, 0)]
    dynamic_update_slice x8 -> x0, other arithmetic: 9.41 us -> none  [add_block(): lax.dynamic_update_slice(total, guarded(visiting, first)[None], (slot, ze...]
    another operation x1 -> x0, local copies, waits for them, and re-layouts: 6.5 us -> none  [local(): return coupling[None]]
    rsqrt x9 -> x0, other arithmetic: 5.33 us -> none  [the longest x8 4.72 us: block_value(): vis_spread = lax.rsqrt(jnp.mean(vis_middle * vis_middle, axis=2) + EPSILON)]
  transfers between devices with their start and end apart: 6 -> 6, of which waited for: 5 -> 3; matrix products, arithmetic and copies ran while one was open for 2% -> 39% of each run, Pallas kernels for 0% -> 6%
where the time goes in v1:
time: 278 us
  local copies, waits for them, and re-layouts  125 us (45%)
  Pallas kernels  43 us (15%)
  blocking collectives  35.4 us (13%)
  other arithmetic  18.1 us (7%)
  starting transfers between devices  16.7 us (6%)
  between operations  14.6 us (5%)
  matrix products  12.3 us (4%)
  waiting for transfers between devices  6.41 us (2%)
  loops' own time  5.69 us (2%)
    gather x2, local copies, waits for them, and re-layouts, coupling_of(): sums = jnp.dot(flat, jnp.take(outside, step).astype(F32), precision=HIGH)  91.9 us
    unnamed x1, blocking collectives  35.4 us
    pallas_call x1, Pallas kernels, coupling_call(): pl.pallas_call(partial(coupling_kernel, par_dev), out_shape=jax.ShapeDtyp...  27.2 us
    pallas_call x1, Pallas kernels, lag_weights(): pl.pallas_call(partial(lag_weights_kernel, rows), out_shape=jax.ShapeDtyp...  15.8 us
    ppermute x2, starting transfers between devices, extended_2(): lax.ppermute(tail, axis, [(i, (i + 1) % count) for i in range(ends)])  9.03 us
    dynamic_update_slice x10, local copies, waits for them, and re-layouts, local(): lax.map(filter_block, widened.reshape(vert_dev // block_rows, block_rows,...  7.04 us
    unnamed x35, local copies, waits for them, and re-layouts  6.72 us
    ppermute x2, waiting for transfers between devices, extended_2(): lax.ppermute(head, axis, [((i + 1) % count, i) for i in range(ends)])  5.96 us
  transfers between devices with their start and end apart: 6, of which 3 were waited for; matrix products, arithmetic and copies ran while one was open for 39% of the time, Pallas kernels for 6%

profile of v1, /device:TPU:9, one launch (start us, length us, event | category | flops | bytes accessed | tf_op | source)
XLA Modules:
  0.0 277.7 jit_solution(13026772931433035603)
XLA Ops:
  6.5 2.1 fusion.65
  8.6 3.7 %collective-permute-start = (bf16[1280,64]{1,0:T(8,128)(2,1)}, bf16[1280,64]{1,0:T(8,128)(2,1)}, u32[]{:S(2)}, u32[]{:S(2)}) collective-permute-start(bf16[1280,64]{1,0:T(8,128)(2,1)} %get-tuple-element.153), channel_id=1, source_target_pairs={{0,1},{1,2},{2,3},{4,5},{5,6},{6,7},{8,9},{9,10},{10,11},{12,13},{... | collective-permute-start | bytes 491528 | tf_op jit(solution)/shard_map/ppermute | solution.py:35
  12.4 1.9 collective-permute-start.1
  19.5 1.6 collective-permute-done.1
  21.1 1.5 pad_maximum_fusion
  22.5 12.1 %while.22 = (s32[]{:T(128)}, bf16[10,128,2,128]{3,2,1,0:T(2,128)(2,1)}, bf16[10,128,256]{2,1,0:T(8,128)(2,1)S(1)}, bf16[256,768]{0,1:T(8,128)(2,1)S(1)}, bf16[2,192,128]{2,1,0:T(8,128)(2,1)S(1)}, /*index=5*/s32[]{:T(128)}) while((s32[]{:T(128)}, bf16[10,128,2,128]{3,2,1,0:T(2,128)(2,1)}, bf16[10,128,256]{2,1,0:T(8,128)(2,1)S(1)}, ...), condition=%wide.region_1.2_spmd, body=%wide.region_0.1_spmd.sunk | while | flops 63143936 | bytes 1540181 | solution.py:324
  34.6 1.2 copy.106
  35.8 15.7 %while.23 = (s32[]{:T(128)}, f32[8,188,256]{2,1,0:T(8,128)S(1)}, s32[3,1280]{1,0:T(4,128)S(1)}, s32[8]{0:T(128)S(1)}, bf16[1280,256]{1,0:T(8,128)(2,1)S(1)}, /*index=5*/s32[]{:T(128)}, s32[1]{0:T(128)}) while((s32[]{:T(128)}, f32[8,188,256]{2,1,0:T(8,128)S(1)}, s32[3,1280]{1,0:T(4,128)S(1)}, s32[8]{0:T(128)S(1)}, ...), condition=%wide.region_4.5_spmd, body=%wide.region_2.4_spmd.sunk | while | flops 125132992 | bytes 1841749 | solution.py:337
  51.7 35.4 %fusion = f32[192,256]{1,0:T(8,128)S(1)} fusion(f32[1504,256]{1,0:T(8,128)S(1)} %reshape.245), kind=kCustom, calls=%all-reduce-scatter | all-reduce-scatter fusion | flops 393217 | bytes 1737216
  87.1 3.7 %collective-permute-start.4 = (f32[28,256]{1,0:T(8,128)S(1)}, f32[28,256]{1,0:T(8,128)S(1)}, u32[]{:S(2)}, u32[]{:S(2)}) collective-permute-start(f32[28,256]{1,0:T(8,128)S(1)} %slice.129), channel_id=1, source_target_pairs={{0,4},{4,8},{8,12},{12,16},{16,20},{20,24},{24,28},{1,5},{5,9},{9,... | collective-permute-start | bytes 86024
  93.7 5.3 %collective-permute-start.2 = (f32[188,2,64]{2,1,0:T(2,128)S(1)}, f32[188,2,64]{2,1,0:T(2,128)S(1)}, u32[]{:S(2)}, u32[]{:S(2)}) collective-permute-start(f32[188,2,64]{2,1,0:T(2,128)S(1)} %get-tuple-element.155), channel_id=1, source_target_pairs={{0,1},{1,2},{2,3},{4,5},{5,6},{6,7},{8,9},{9,10},{10,11},{12,13},{... | collective-permute-start | bytes 288776 | tf_op jit(solution)/shard_map/ppermute | solution.py:35
  99.1 2.1 collective-permute-start.3
  101.6 4.4 %collective-permute-done.3 = f32[188,2,64]{2,1,0:T(2,128)S(1)} collective-permute-done((f32[188,2,64]{2,1,0:T(2,128)S(1)}, f32[188,2,64]{2,1,0:T(2,128)S(1)}, u32[]{:S(2)}, u32[]{:S(2)}) %collective-permute-start.3) | collective-permute-done | bytes 96288 | tf_op jit(solution)/shard_map/ppermute | solution.py:37
  106.0 1.5 fusion.16
  107.6 91.5 %gather_fusion = pred[16512]{0:T(1024)(128)(4,1)S(1)} fusion(pred[256]{0:T(512)(128)(4,1)S(1)} %and_or_fusion, s32[17408]{0:T(1024)S(1)} %pad_clamp_fusion), kind=kCustom, calls=%fused_computation | custom fusion | bytes 99072 | tf_op jit(solution)/shard_map/jit(_take)/gather | solution.py:280
  201.3 15.8 %lag_weights.1 = bf16[384,8192]{1,0:T(8,128)(2,1)S(1)} custom-call(f32[384,128]{1,0:T(8,128)S(1)} %bitcast.98), custom_call_target="tpu_custom_call" | custom-call | tf_op jit(solution)/shard_map/lag_weights/pallas_call | solution.py:121
  217.1 2.6 copy-done
  225.9 1.6 fusion.15
  227.5 4.8 %multiply_reduce_fusion = f32[1504,2]{1,0:T(8,128)S(1)} fusion(bf16[1504,2,256]{2,1,0:T(2,128)(2,1)} %all-gather.2.cloned.1.call-done), kind=kLoop, calls=%fused_computation.23 | loop fusion | flops 1152064 | bytes 782080 | tf_op jit(solution)/shard_map/reduce_sum | solution.py:251
  232.5 1.4 fusion.64
  234.0 0.9 copy.89
  237.0 1.2 fusion.13.rows_ref
  238.8 27.2 %coupling.1 = f32[2,188,1504]{2,1,0:T(8,128)} custom-call(s32[2]{0:T(128)} %pad_add_fusion.1.bounds_ref, bf16[2,192,8192]{2,1,0:T(8,128)(2,1)} %bitcast.97, bf16[2,192,512]{2,1,0:T(8,128)(2,1)} %pad_maximum_fusion.1.freq_ref, bf16[2,192,256]{2,1,0:T(8,128)(2,1)} %bitcast.108, f32[2,192,1]{2,1,0:T(8,128)} %reshape.262.edge_sum_ref, ...), custom_call_target="tpu_custom_call" | custom-call | tf_op jit(solution)/shard_map/coupling/pallas_call | solution.py:208
  266.1 4.8 %copy.85 = f32[1,2,188,1504]{3,1,2,0:T(2,128)} copy(f32[1,2,188,1504]{3,2,1,0:T(8,128)} %bitcast.104) | data formatting | bytes 4524032 | tf_op jit(solution)/shard_map/broadcast_in_dim | solution.py:351
  (157 shorter events, 41.1 us)
Async XLA Ops:
  6.5 220.9 %all-gather.2.cloned.1.call-start = ((), (), s32[]{:S(2)}) async-start(), calls=%async_computation | async-start | bytes 1732608 | tf_op jit(solution)/shard_map/all_gather | solution.py:349
  8.6 10.8 %collective-permute-start = (bf16[1280,64]{1,0:T(8,128)(2,1)}, bf16[1280,64]{1,0:T(8,128)(2,1)}, u32[]{:S(2)}, u32[]{:S(2)}) collective-permute-start(bf16[1280,64]{1,0:T(8,128)(2,1)} %get-tuple-element.153), channel_id=1, source_target_pairs={{0,1},{1,2},{2,3},{4,5},{5,6},{6,7},{8,9},{9,10},{10,11},{12,13},{... | collective-permute-start | bytes 491528 | tf_op jit(solution)/shard_map/ppermute | solution.py:35
  12.4 8.7 %collective-permute-start.1 = (bf16[1280,64]{1,0:T(8,128)(2,1)}, bf16[1280,64]{1,0:T(8,128)(2,1)}, u32[]{:S(2)}, u32[]{:S(2)}) collective-permute-start(bf16[1280,64]{1,0:T(8,128)(2,1)} %get-tuple-element.154), channel_id=1, source_target_pairs={{1,0},{2,1},{3,2},{5,4},{6,5},{7,6},{9,8},{10,9},{11,10},{13,12},{... | collective-permute-start | bytes 491528 | tf_op jit(solution)/shard_map/ppermute | solution.py:37
  17.6 1.2 copy-start.9
  17.7 1.2 copy-start.12
  17.7 3.4 %copy-start.2 = (bf16[1280,128]{1,0:T(8,128)(2,1)S(1)}, bf16[1280,128]{1,0:T(8,128)(2,1)}, u32[]{:S(2)}) copy-start(bf16[1280,128]{1,0:T(8,128)(2,1)} %param.14) | copy-start | bytes 983044
  51.7 39.8 %copy-start.11 = (u32[32]{0:T(128)S(1)}, u32[32]{0:T(128)}, u32[]{:S(2)}) copy-start(u32[32]{0:T(128)} %constant.172) | copy-start | bytes 388
  87.1 5.6 %collective-permute-start.4 = (f32[28,256]{1,0:T(8,128)S(1)}, f32[28,256]{1,0:T(8,128)S(1)}, u32[]{:S(2)}, u32[]{:S(2)}) collective-permute-start(f32[28,256]{1,0:T(8,128)S(1)} %slice.129), channel_id=1, source_target_pairs={{0,4},{4,8},{8,12},{12,16},{16,20},{20,24},{24,28},{1,5},{5,9},{9,... | collective-permute-start | bytes 86024
  93.7 7.9 %collective-permute-start.2 = (f32[188,2,64]{2,1,0:T(2,128)S(1)}, f32[188,2,64]{2,1,0:T(2,128)S(1)}, u32[]{:S(2)}, u32[]{:S(2)}) collective-permute-start(f32[188,2,64]{2,1,0:T(2,128)S(1)} %get-tuple-element.155), channel_id=1, source_target_pairs={{0,1},{1,2},{2,3},{4,5},{5,6},{6,7},{8,9},{9,10},{10,11},{12,13},{... | collective-permute-start | bytes 288776 | tf_op jit(solution)/shard_map/ppermute | solution.py:35
  99.1 6.9 %collective-permute-start.3 = (f32[188,2,64]{2,1,0:T(2,128)S(1)}, f32[188,2,64]{2,1,0:T(2,128)S(1)}, u32[]{:S(2)}, u32[]{:S(2)}) collective-permute-start(f32[188,2,64]{2,1,0:T(2,128)S(1)} %get-tuple-element.156), channel_id=1, source_target_pairs={{1,0},{2,1},{3,2},{5,4},{6,5},{7,6},{9,8},{10,9},{11,10},{13,12},{... | collective-permute-start | bytes 288776 | tf_op jit(solution)/shard_map/ppermute | solution.py:37
  107.6 92.6 %copy-start.3 = (bf16[188,2,256]{2,1,0:T(2,128)(2,1)S(1)}, bf16[188,2,256]{2,1,0:T(2,128)(2,1)}, u32[]{:S(2)}) copy-start(bf16[188,2,256]{2,1,0:T(2,128)(2,1)} %fusion.16) | copy-start | bytes 577540
  201.3 20.5 %copy-start.5 = (f32[128,258]{1,0:T(8,128)S(1)}, f32[128,258]{1,0:T(8,128)}, u32[]{:S(2)}) copy-start(f32[128,258]{1,0:T(8,128)} %constant.147.clone) | copy-start | bytes 396292
  217.1 2.6 copy-start
  219.7 2.7 copy-start.7
  221.8 2.4 copy-start.4
  222.5 2.6 copy-start.8
  223.3 2.6 copy-start.6
  227.5 5.1 %copy-start.1 = (bf16[1504,2,256]{2,1,0:T(2,128)(2,1)S(1)}, bf16[1504,2,256]{2,1,0:T(2,128)(2,1)}, u32[]{:S(2)}) copy-start(bf16[1504,2,256]{2,1,0:T(2,128)(2,1)} %all-gather.2.cloned.1.call-done) | copy-start | bytes 4620292
  234.0 2.1 copy-start.10
Sparse Core Ops, SparseCore 0:
  107.7 41.7 all-gather.1

commit v2 on v0

v2 whole, which is shorter than its diff:
```python
from functools import partial

import numpy as np

import jax
import jax.numpy as jnp
from jax import lax
from jax.experimental import pallas as pl
from jax.experimental.pallas import tpu as pltpu
from jax.sharding import PartitionSpec as P

P1 = 100
P2 = 400
P3 = 1000
BANDS = 2
TAPS = 65
HALF = 32
LAG = 64
NLAG = 129
EPSILON = 1e-05
SPLIT = P1 + P2
GROUP = (SPLIT + 127) // 128 * 128
TILE = 256
PERIOD = 127
HIGH = lax.Precision.HIGHEST
BF16 = jnp.bfloat16
F32 = jnp.float32
VMEM = pl.BlockSpec(memory_space=pltpu.VMEM)


def fourier_constants():
    n = 256
    freq = np.arange(129)
    angle = 2 * np.pi * np.outer(np.arange(n), freq) / n
    cos, sin = np.cos(angle), np.sin(angle)
    weight = np.full(129, 2.0 / n)
    weight[[0, 128]] = 1.0 / n
    packed = np.concatenate([cos[:, :128], cos[:, 128:], -sin[:, 1:128]], axis=1)
    lags = np.arange(128)
    twice = np.where(lags == 0, 1.0, 2.0)
    from_power = weight[:, None] * cos[lags].T * twice
    scale = np.concatenate([weight[:128], weight[128:], weight[1:128]])
    to_weights = np.zeros((n, n))
    to_weights[:129] = (from_power @ packed[lags]) * scale
    order = np.concatenate([np.arange(64, 192), np.arange(0, 64), np.arange(192, 256)])
    inverse = (packed * scale).T[:, order]
    forward = packed * (np.arange(n) < NLAG)[:, None]
    near = forward.T[:, order]
    factors = np.concatenate([near, packed.T[:, order]], axis=0)
    high = factors.astype(np.float32).astype(jnp.bfloat16)
    low = (factors - high.astype(np.float64)).astype(np.float32).astype(jnp.bfloat16)
    f32 = lambda cells: cells.astype(np.float32)
    return f32(forward), f32(to_weights), f32(inverse), np.concatenate([high, low], axis=0)


FORWARD, TO_WEIGHTS, INVERSE, FACTORS = fourier_constants()


def params(mib):
    return pltpu.CompilerParams(vmem_limit_bytes=mib * 2**20)


def cost(flops, moved):
    return pl.CostEstimate(flops=flops, bytes_accessed=moved, transcendentals=0)


def iota(shape, dim):
    return lax.broadcasted_iota(jnp.int32, shape, dim)


class Rows:
    def __init__(self, par_dev):
        self.rows = par_dev
        self.padded = (par_dev + 15) // 16 * 16
        self.extra = (par_dev + 63) // 64
        self.height = (par_dev + 2 * self.extra + 15) // 16 * 16
        self.tail = par_dev // 16 * 16


def level_of(parcel):
    first = (parcel >= P1).astype(jnp.int32)
    second = (parcel >= SPLIT).astype(jnp.int32)
    third = (parcel >= SPLIT + P3).astype(jnp.int32)
    return first + second + third


def put_tail(form, tail, above, mean_rows):
    tail[...] = jnp.zeros_like(tail)
    tail[0 : form.rows - form.tail] = above
    high = mean_rows.astype(BF16).astype(F32)
    at = form.rows - form.tail
    tail[at : at + form.extra] = high
    tail[at + form.extra : at + 2 * form.extra] = mean_rows - high
    return tail[...].astype(BF16)


def front_kernel(
    form, owners, orders, middle_ref, left_ref, right_ref, taps_ref, smooth_ref, ids_ref, *rest
):
    outs, (env, tail) = rest[: 2 * BANDS], rest[2 * BANDS :]
    me = lax.axis_index("vert")
    shape = (256, 256)
    filters = [
        pltpu.roll(jnp.broadcast_to(taps_ref[k], shape), 192, 1, stride=1, stride_axis=0).astype(BF16)
        for k in range(2 * BANDS)
    ]
    smooths = [
        pltpu.roll(
            jnp.broadcast_to(smooth_ref[k], (128, 256)), 0, 1, stride=1, stride_axis=0
        ).astype(BF16)
        for k in range(BANDS)
    ]
    turned = (((1,), (1,)), ((), ()))
    vertices = middle_ref.shape[0]
    step = 256
    for at in range(0, vertices, step):
        cut = slice(at, at + step)
        wide = jnp.concatenate([middle_ref[cut], right_ref[cut], left_ref[cut]], axis=1)
        for band in range(BANDS):
            one = lax.dot_general(wide, filters[band], turned, preferred_element_type=F32)
            two = lax.dot_general(wide, filters[BANDS + band], turned, preferred_element_type=F32)
            power = (one * one + two * two).astype(BF16)
            smooth = lax.dot_general(power, smooths[band], turned, preferred_element_type=F32)
            env[cut, band * 128 : (band + 1) * 128] = smooth.astype(BF16)
    offsets = (0, P1, SPLIT)
    ids = [ids_ref[r : r + 1] + offsets[r] for r in range(3)]
    height = form.padded
    lane = iota((64, 128), 1)
    row = iota((64, 128), 0)
    diagonal = lax.rem(lane, 64) == row
    for k in range(owners):
        owner = me ^ k
        wanted = iota((height, 1), 0) + owner * form.rows
        hits = (wanted == ids[0]) | (wanted == ids[1]) | (wanted == ids[2])
        hits = jnp.where(hits, 1.0, 0.0).astype(BF16)
        sums = jnp.dot(hits, env[...], preferred_element_type=F32)
        for band in range(BANDS):
            cells = sums[:, band * 128 : (band + 1) * 128]
            mean = jnp.mean(cells, axis=1, keepdims=True)
            change = cells - mean
            means = jnp.concatenate(
                [
                    jnp.sum(
                        jnp.where(
                            diagonal[: min(64, height - 64 * e)], mean[64 * e : 64 * e + 64], 0.0
                        ),
                        axis=0,
                        keepdims=True,
                    )
                    for e in range(form.extra)
                ],
                axis=0,
            )
            p = place(k, orders[band][::-1])
            half = owners // 2
            out = outs[2 * band + p // half]
            out[p % half, 0 : form.tail] = change[0 : form.tail].astype(BF16)
            out[p % half, form.tail : form.height] = put_tail(
                form, tail, change[form.tail : form.rows], means
            )


def place(k, order):
    return sum((1 if k & bit else 0) << j for j, bit in enumerate(order))


def front(form, owners, orders, middle, left, right, taps, smooths, ids):
    shape = jax.ShapeDtypeStruct((owners // 2, form.height, 128), BF16)
    operands = (middle, left, right, taps, smooths, ids)
    return pl.pallas_call(
        partial(front_kernel, form, owners, orders),
        out_shape=[shape] * (2 * BANDS),
        in_specs=[VMEM] * len(operands),
        out_specs=[VMEM] * (2 * BANDS),
        scratch_shapes=[
            pltpu.VMEM((middle.shape[0], BANDS * 128), BF16),
            pltpu.VMEM((form.height - form.tail, 128), F32),
        ],
        compiler_params=params(40),
        cost_estimate=cost(3 * 10**9, 2 * 10**6),
        name="envelope_sums",
    )(*operands)


def merge_kernel(form, halves, count, *refs):
    ins, outs, tail = refs[: 2 * count], refs[2 * count : -1], refs[-1]
    blocks = ins[0].shape[0]
    at = form.rows - form.tail
    for pair in range(count):
        for n in range(blocks):
            whole = ins[2 * pair][n].astype(F32) + ins[2 * pair + 1][n].astype(F32)
            if halves == "own":
                put = outs[0].at[n]
            elif halves == "joined":
                put = outs[n].at[pair]
            else:
                put = outs[n // (blocks // 2)].at[n % (blocks // 2)]
            put[0 : form.tail] = whole[0 : form.tail].astype(BF16)
            tail[...] = whole[form.tail :]
            means = tail[at : at + form.extra] + tail[at + form.extra : at + 2 * form.extra]
            put[form.tail :] = put_tail(form, tail, whole[form.tail : form.rows], means)


def merge(form, pairs, halves):
    operands = [cells for pair in pairs for cells in pair]
    blocks = operands[0].shape[0]
    size = (form.height, 128)
    if halves == "own":
        shapes = [(blocks, *size)]
    elif halves == "joined":
        shapes = [(len(pairs), *size)] * 2
    else:
        shapes = [(blocks // 2, *size)] * 2
    return pl.pallas_call(
        partial(merge_kernel, form, halves, len(pairs)),
        out_shape=[jax.ShapeDtypeStruct(shape, BF16) for shape in shapes],
        in_specs=[VMEM] * len(operands),
        out_specs=[VMEM] * len(shapes),
        scratch_shapes=[pltpu.VMEM((form.height - form.tail, 128), F32)],
        cost_estimate=cost(10**6, 10**6),
        name="add_arrived",
    )(*operands)


def scales_of(middle):
    spread = lax.rsqrt(jnp.mean(middle * middle, axis=1, keepdims=True) + EPSILON)
    power = jnp.exp2(jnp.floor(jnp.log2(spread)))
    rest = spread / power
    return power, rest * rest


def own_rows(form, own_ref, band):
    middle = own_ref[band, 0 : form.padded].astype(F32)
    middle = jnp.where(iota(middle.shape, 0) < form.rows, middle, 0.0)
    power, rest = scales_of(middle)
    return middle * power, rest


def lag_sums_kernel(form, own_ref, out_ref):
    middle = jnp.concatenate([own_rows(form, own_ref, band)[0] for band in range(BANDS)], axis=0)
    lane = iota((1, 128), 1)
    row = iota((128, 128), 0)
    col = iota((128, 128), 1)

    def several(step, turned):
        for k in range(8):
            d = step * 8 + k
            further = pltpu.roll(turned, 127, 1)
            partner = jnp.where(lane <= PERIOD - d, turned, further)
            product = (middle * partner).astype(BF16)
            keep = (row > col) & ((row <= PERIOD - d) == (col < PERIOD - d))
            scale = jnp.where(d == 0, 1.0, 2.0).astype(F32)
            keep = jnp.where(keep, scale, 0.0).astype(BF16)
            sums = jnp.dot(product, keep, preferred_element_type=F32).astype(BF16)
            put = pl.ds(pl.multiple_of(d * 128, 128), 128)
            for band in range(BANDS):
                out_ref[band, :, put] = sums[band * form.padded : (band + 1) * form.padded]
            turned = further
        return turned

    lax.fori_loop(0, 8, several, middle)


def lag_sums(form, own):
    return pl.pallas_call(
        partial(lag_sums_kernel, form),
        out_shape=jax.ShapeDtypeStruct((BANDS, form.padded, 64 * 128), BF16),
        in_specs=[VMEM],
        out_specs=VMEM,
        compiler_params=params(40),
        cost_estimate=cost(5 * 10**9, 6 * 10**6),
        name="lag_sums",
    )(own)


def spectra_kernel(form, own_ref, forward_ref, to_weights_ref, inverse_ref, freq_ref, edge_ref, column_ref):
    window, windows = lax.axis_index("tm"), lax.axis_size("tm")
    rows = [own_rows(form, own_ref, band) for band in range(BANDS)]
    middle = jnp.concatenate([cells for cells, _ in rows], axis=0)
    rest = jnp.concatenate([left for _, left in rows], axis=0)
    dot = partial(jnp.dot, precision=HIGH, preferred_element_type=F32)
    forward = forward_ref[...]
    spectrum = dot(middle, forward_ref[0:128])
    low, high = spectrum[:, :128], spectrum[:, 128:]
    lane = iota(low.shape, 1)
    inner = jnp.where(lane == 0, 0.0, high)
    last = jnp.where(lane == 0, high, 0.0)
    strength = jnp.concatenate([low * low + inner * inner, last * last], axis=1)
    weights = dot(strength, to_weights_ref[...])
    place_in = iota((128, 256), 0) + iota((128, 256), 1)
    count = iota((128, 256), 1)
    outside = ((window == 0) & (place_in < LAG)) | (
        (window == windows - 1) & (place_in >= LAG + 128) & (count < NLAG)
    )
    outside = jnp.where(outside, 1.0, 0.0).astype(BF16)
    sums = jnp.dot(middle.astype(BF16), outside, preferred_element_type=F32)
    edge_sum = jnp.sum(sums * sums, axis=1, keepdims=True)
    other = dot(sums, forward)
    other_low, other_high = other[:, :128], other[:, 128:]
    cross = other_high * high
    real = other_low * low - jnp.where(lane == 0, 0.0, cross)
    imag = jnp.where(lane == 0, cross, other_low * high + other_high * low)
    edge = dot(jnp.concatenate([real, imag], axis=1), inverse_ref[...])
    factor = rest * (1.0 / (128 * 128 * NLAG))
    column = jnp.where(lane == 0, edge_sum, jnp.where(lane == 1, factor, 0.0))
    for band in range(BANDS):
        cut = slice(band * form.padded, (band + 1) * form.padded)
        big = weights[cut].astype(BF16)
        freq_ref[band, :, 0:256] = big
        freq_ref[band, :, 256:512] = (weights[cut] - big.astype(F32)).astype(BF16)
        edge_ref[band] = edge[cut].astype(BF16)
        column_ref[band] = column[cut]


def spectra(form, own):
    shapes = [((BANDS, form.padded, 512), BF16), ((BANDS, form.padded, 256), BF16), ((BANDS, form.padded, 128), F32)]
    return pl.pallas_call(
        partial(spectra_kernel, form),
        out_shape=[jax.ShapeDtypeStruct(*shape) for shape in shapes],
        in_specs=[VMEM] * 4,
        out_specs=[VMEM] * 3,
        compiler_params=params(40),
        cost_estimate=cost(2 * 10**9, 2 * 10**6),
        name="row_spectra",
    )(own, jnp.asarray(FORWARD), jnp.asarray(TO_WEIGHTS), jnp.asarray(INVERSE))


def mean_column(form, block):
    shape = (form.padded, form.height - form.tail)
    row, col = iota(shape, 0), iota(shape, 1) - (form.rows - form.tail)
    pick = (col == row // 64) | (col - form.extra == row // 64)
    pick = jnp.where(pick, 1.0, 0.0).astype(BF16)
    spread = jnp.dot(pick, block[form.tail :], preferred_element_type=F32)
    own = iota(spread.shape, 1) == lax.rem(iota(spread.shape, 0), 64)
    return jnp.sum(jnp.where(own, spread, 0.0), axis=1, keepdims=True)


def coupling_kernel(
    form, owners, order, band, final, lag_ref, freq_ref, edge_ref, column_ref, near_half, far_half,
    left_ref, right_ref, factor_ref, *rest
):
    if final:
        before_ref, out_ref, *scratch = rest
        result = scratch.pop(0)
    else:
        result, *scratch = rest
    blocks, rows, near, far, near_turn, far_turn, change = scratch
    me = lax.axis_index("vert")
    window, windows = lax.axis_index("tm"), lax.axis_size("tm")
    half = owners // 2
    blocks[0:half] = near_half[...]
    blocks[half:owners] = far_half[...]
    result[...] = jnp.zeros_like(result)
    rows[...] = jnp.zeros_like(rows)
    lane = iota((1, 128), 1)
    is_left = lane < LAG
    first_window, last_window = window == 0, window == windows - 1
    outside = (first_window & is_left) | (last_window & ~is_left)
    for owner in range(owners):
        k = me ^ owner
        p = sum(lax.rem(k // bit, 2) << j for j, bit in enumerate(order))
        block = blocks[p]
        middle = block[0 : form.padded].astype(F32)
        mean = mean_column(form, block)
        left, right = left_ref[p], right_ref[p]
        margins = jnp.concatenate([left, right], axis=1)
        around = margins[0 : form.padded].astype(F32)
        shift_left = mean_column(form, left) - mean
        shift_right = mean_column(form, right) - mean
        around = (around + jnp.where(is_left, shift_left, shift_right)).astype(BF16).astype(F32)
        around = jnp.where(outside, 0.0, around)
        power, left_over = scales_of(middle)
        mu = jnp.where(first_window | last_window, mean.astype(BF16).astype(F32) * power, 0.0)
        extra = jnp.where(lane == 0, mu, jnp.where(lane == 1, left_over, 0.0))
        begin = owner * form.rows
        for lo, hi, gap in ((0, SPLIT, 0), (SPLIT, owners * form.rows, GROUP - SPLIT)):
            start, stop = max(lo, begin), min(hi, begin + form.rows)
            if start < stop:
                cut = slice(start - begin, stop - begin)
                put = slice(start + gap, stop + gap)
                rows[put, 0:128] = (middle * power)[cut]
                rows[put, 128:256] = (around * power)[cut]
                rows[put, 256:384] = extra[cut]

    own_parcel = iota((form.padded, 1), 0) + me * form.rows
    own_level = level_of(own_parcel)
    own_level = jnp.where(own_level < 3, own_level, -1)
    factors = column_ref[band]
    edge_sum, own_factor = factors[:, 0:1], factors[:, 1:2]

    def tile(n, carry):
        first = pl.multiple_of(n * TILE, TILE)
        columns = rows[pl.ds(first, TILE), :].T
        narrow = columns[0:256].astype(BF16)
        near[0:64] = columns[128:192]
        near[64:127] = columns[0:63]
        near[127:191] = columns[128:192]
        far[0:63] = columns[65:128]
        far[63:127] = columns[192:256]
        far[127:190] = columns[65:128]
        far[190:191] = columns[192:193]
        for r in range(16):
            near_turn[r] = near[r : r + 176].astype(BF16)
            far_turn[r] = far[r : r + 176].astype(BF16)
        for d in range(64):
            a, r = divmod(d, 16)
            change[d * 128 : (d + 1) * 128] = (
                far_turn[0, 0:128] * far_turn[r, 16 * a : 16 * a + 128]
                - near_turn[0, 0:128] * near_turn[r, 16 * a : 16 * a + 128]
            )
        total = jnp.dot(lag_ref[band], change[...], preferred_element_type=F32)
        spectra = jnp.dot(factor_ref[0:512], narrow, preferred_element_type=F32) + jnp.dot(
            factor_ref[512:1024], narrow, preferred_element_type=F32
        )
        low_a, high_a, low_c, high_c = (spectra[128 * k : 128 * (k + 1)] for k in range(4))
        at_zero = iota((128, TILE), 0) == 0
        cross = high_a * high_c
        real = low_a * low_c + jnp.where(at_zero, 0.0, cross)
        imag = jnp.where(at_zero, cross, low_a * high_c - high_a * low_c)
        both = jnp.concatenate([real, imag], axis=0)
        big = both.astype(BF16)
        small = (both - big.astype(F32)).astype(BF16)
        weights = freq_ref[band]
        total += jnp.dot(weights[:, 0:256], big, preferred_element_type=F32)
        total += jnp.dot(weights[:, 256:512], big, preferred_element_type=F32)
        total += jnp.dot(weights[:, 0:256], small, preferred_element_type=F32)
        mixed = jnp.dot(edge_ref[band], narrow, preferred_element_type=F32)
        mu, other_factor = columns[256:257], columns[257:258]
        total += mu * (mu * edge_sum - 2.0 * mixed)
        column = iota((1, TILE), 1) + first
        parcel = jnp.where(column < GROUP, column, column - (GROUP - SPLIT))
        gap = (column >= SPLIT) & (column < GROUP)
        other_level = jnp.where(gap, 3, level_of(parcel))
        scaled = total * own_factor * other_factor
        result[:, pl.ds(first, TILE)] = jnp.where(own_level == other_level, scaled, 0.0)
        return carry

    begin = me * form.rows
    end = jnp.minimum(begin + form.rows, SPLIT + P3)
    tiles = result.shape[1] // TILE
    lax.fori_loop(
        jnp.where(begin < SPLIT, 0, GROUP // TILE),
        jnp.where(end <= SPLIT, GROUP // TILE, tiles),
        tile,
        0,
    )
    if final:
        total = owners * form.rows
        for k, cells in ((1 - band, before_ref), (band, result)):
            out_ref[:, k, 0:SPLIT] = cells[0 : form.rows, 0:SPLIT]
            out_ref[:, k, SPLIT:total] = cells[0 : form.rows, GROUP : GROUP + total - SPLIT]


def coupling(form, owners, order, band, before, *operands):
    total = owners * form.rows
    width = GROUP + (total - SPLIT + TILE - 1) // TILE * TILE
    final = before is not None
    operands = (*operands, jnp.asarray(FACTORS), *((before,) if final else ()))
    result = (form.padded, width)
    out = (form.rows, BANDS, total) if final else result
    return pl.pallas_call(
        partial(coupling_kernel, form, owners, order, band, final),
        out_shape=jax.ShapeDtypeStruct(out, F32),
        in_specs=[VMEM] * len(operands),
        out_specs=VMEM,
        scratch_shapes=([pltpu.VMEM(result, F32)] if final else [])
        + [
            pltpu.VMEM((owners, form.height, 128), BF16),
            pltpu.VMEM((width, 384), F32),
            pltpu.VMEM((192, TILE), F32),
            pltpu.VMEM((192, TILE), F32),
            pltpu.VMEM((16, 176, TILE), BF16),
            pltpu.VMEM((16, 176, TILE), BF16),
            pltpu.VMEM((64 * 128, TILE), BF16),
        ],
        compiler_params=params(56),
        cost_estimate=cost(8 * 10**9, 10**7),
        name="coupling",
    )(*operands)


def swap(cells, owners, bit):
    return lax.ppermute(cells, "vert", [(i, i ^ bit) for i in range(owners)])


def local(source, band_taps, smooth_taps, parcel_ids):
    vert_dev, t_dev = source.shape
    owners, windows = lax.axis_size("vert"), lax.axis_size("tm")
    form = Rows((P1 + P2 + P3 + owners - 1) // owners)
    bits = [1 << k for k in range(owners.bit_length() - 1)]
    orders = [bits, [bits[1], bits[0], *bits[2:]]]
    up = [(i, i + 1) for i in range(windows - 1)]
    down = [(i + 1, i) for i in range(windows - 1)]
    left = lax.ppermute(source[:, t_dev - 2 * HALF :], "tm", up)
    right = lax.ppermute(source[:, : 2 * HALF], "tm", down)
    taps = jnp.pad(band_taps.astype(F32).reshape(2 * BANDS, 1, TAPS), ((0, 0), (0, 0), (0, 256 - TAPS)))
    smooths = jnp.pad(smooth_taps.astype(F32)[:, None, :], ((0, 0), (0, 0), (0, 256 - TAPS)))
    parts = front(form, owners, orders, source, left, right, taps, smooths, parcel_ids)
    parts = [parts[0:2], parts[2:4]]
    for step in range(len(bits) - 1):
        arrived = [swap(parts[b][1], owners, orders[b][step]) for b in range(BANDS)]
        pairs = [(parts[b][0], arrived[b]) for b in range(BANDS)]
        if step < len(bits) - 2:
            parts = [merge(form, [pair], "halves") for pair in pairs]
        else:
            kept, sent = merge(form, pairs, "joined")
    arrived = swap(sent, owners, bits[-1])
    (own,) = merge(form, [(kept, arrived)], "own")

    lag = lag_sums(form, own)
    freq, edge, column = spectra(form, own)
    arrived = swap(own, owners, bits[-1])
    held = [jnp.stack([own[b], arrived[b]]) for b in range(BANDS)]
    halves = [None, None]
    for step in range(len(bits) - 2, -1, -1):
        arrived = [swap(held[b], owners, orders[b][step]) for b in range(BANDS)]
        halves = [(held[b], arrived[b]) for b in range(BANDS)]
        if step:
            held = [jnp.concatenate(pair, axis=0) for pair in halves]
    done = None
    for b in range(BANDS):
        whole = jnp.concatenate(halves[b], axis=0)
        left = lax.ppermute(whole[:, :, t_dev - LAG :], "tm", up)
        right = lax.ppermute(whole[:, :, :LAG], "tm", down)
        done = coupling(form, owners, orders[b][::-1], b, done, lag, freq, edge, column, *halves[b], left, right)
    return done.transpose(1, 0, 2)[None]


def solution(mesh):
    return jax.shard_map(
        local,
        mesh=mesh,
        in_specs=(P("vert", "tm"), P(), P(), P(None, "vert")),
        out_specs=P("tm", None, "vert", None),
        check_vma=False,
    )
```

time: 354 us -> 123 us (0.35)
  matrix products: 153 us -> 0 us
  Pallas kernels: 0 us -> 56.1 us
  other arithmetic: 34.8 us -> 0.18 us
  blocking collectives: 33.5 us -> 0 us
  waiting for transfers between devices: 47.3 us -> 16 us
  local copies, waits for them, and re-layouts: 45.9 us -> 14.8 us
  starting transfers between devices: 16.7 us -> 34.8 us
  between operations: 14.3 us -> 0.35 us
  loops' own time: 6.47 us -> 0 us
    conv_general_dilated x8 -> x0, matrix products: 145 us -> none  [block_value(): lax.conv_general_dilated(visiting, kernel, (LAG_STEP,), 'VALID', dimensio...]
    pallas_call x0 -> x9, Pallas kernels: none -> 56.1 us  [the longest x2 35.5 us: coupling(): pl.pallas_call(partial(coupling_kernel, form, owners, order, band, final)...]
    all_gather x1 -> x0, waiting for transfers between devices: 39 us -> none  [local(): lax.all_gather(centered, 'vert', axis=0, tiled=True)]
    unnamed x1 -> x0, blocking collectives: 33.5 us -> none
    ppermute x4 -> x16, starting transfers between devices: 13 us -> 34.8 us  [the longest x2 11.3 us: local(): left = lax.ppermute(whole[:, :, t_dev - LAG:], 'tm', up)]
    dynamic_slice x24 -> x0, local copies, waits for them, and re-layouts: 17 us -> none  [the longest x16 12.3 us: add_block(): visiting = lax.dynamic_slice_in_dim(piece, block_idx * par_dev, par_dev, 0)]
    dynamic_update_slice x8 -> x0, other arithmetic: 9.41 us -> none  [add_block(): lax.dynamic_update_slice(total, guarded(visiting, first)[None], (slot, ze...]
    unnamed x14 -> x50, local copies, waits for them, and re-layouts: 2.44 us -> 11.8 us
  transfers between devices with their start and end apart: 6 -> 16, of which waited for: 5 -> 7; matrix products, arithmetic and copies ran while one was open for 2% -> 2% of each run, Pallas kernels for 0% -> 24%
where the time goes in v2:
time: 123 us; the launch traced here: 122 us
  Pallas kernels  56.1 us (46%)
  starting transfers between devices  34.8 us (28%)
  waiting for transfers between devices  16 us (13%)
  local copies, waits for them, and re-layouts  14.8 us (12%)
    pallas_call x2, Pallas kernels, coupling(): pl.pallas_call(partial(coupling_kernel, form, owners, order, band, final)...  35.5 us
    ppermute x10, waiting for transfers between devices, swap(): return lax.ppermute(cells, 'vert', [(i, i ^ bit) for i in range(owners)])  13.4 us
    unnamed x50, local copies, waits for them, and re-layouts  11.8 us
    ppermute x2, starting transfers between devices, local(): left = lax.ppermute(whole[:, :, t_dev - LAG:], 'tm', up)  11.3 us
    ppermute x10, starting transfers between devices, swap(): return lax.ppermute(cells, 'vert', [(i, i ^ bit) for i in range(owners)])  11.1 us
    pallas_call x4, Pallas kernels, merge(): pl.pallas_call(partial(merge_kernel, form, halves, len(pairs)), out_shape...  6.95 us
    ppermute x2, starting transfers between devices, local(): right = lax.ppermute(whole[:, :, :LAG], 'tm', down)  6.81 us
    pallas_call x1, Pallas kernels, lag_sums(): pl.pallas_call(partial(lag_sums_kernel, form), out_shape=jax.ShapeDtypeSt...  6.1 us
  transfers between devices with their start and end apart: 16, of which 7 were waited for; matrix products, arithmetic and copies ran while one was open for 2% of the time, Pallas kernels for 24%

profile of v2, /device:TPU:9, one launch (start us, length us, event | category | flops | bytes accessed | tf_op | source)
XLA Modules:
  0.0 122.3 jit_solution(10476485598812027113)
XLA Ops:
  0.0 1.3 %fusion.2 = (bf16[1280,64]{1,0:T(8,128)(2,1)S(1)}, bf16[1280,64]{1,0:T(8,128)(2,1)S(1)}) fusion(bf16[1280,128]{1,0:T(8,128)(2,1)} %middle_ref.1), kind=kLoop, calls=%fused_computation.10 | loop fusion | bytes 655360 | tf_op jit(solution)/shard_map/slice | solution.py:495
  1.3 2.6 %collective-permute-start.1 = (bf16[1280,64]{1,0:T(8,128)(2,1)S(1)}, bf16[1280,64]{1,0:T(8,128)(2,1)S(1)}, u32[]{:S(2)}, u32[]{:S(2)}) collective-permute-start(bf16[1280,64]{1,0:T(8,128)(2,1)S(1)} %get-tuple-element.35), channel_id=1, source_target_pairs={{1,0},{2,1},{3,2},{5,4},{6,5},{7,6},{9,8},{10,9},{11,10},{13,12},{... | collective-permute-start | bytes 491528 | tf_op jit(solution)/shard_map/ppermute | solution.py:495
  3.9 3.0 %collective-permute-start = (bf16[1280,64]{1,0:T(8,128)(2,1)S(1)}, bf16[1280,64]{1,0:T(8,128)(2,1)S(1)}, u32[]{:S(2)}, u32[]{:S(2)}) collective-permute-start(bf16[1280,64]{1,0:T(8,128)(2,1)S(1)} %get-tuple-element.36), channel_id=1, source_target_pairs={{0,1},{1,2},{2,3},{4,5},{5,6},{6,7},{8,9},{9,10},{10,11},{12,13},{... | collective-permute-start | bytes 491528 | tf_op jit(solution)/shard_map/ppermute | solution.py:494
  8.3 1.5 %collective-permute-done.1.right_ref = bf16[1280,64]{1,0:T(8,128)(2,1)S(1)} collective-permute-done((bf16[1280,64]{1,0:T(8,128)(2,1)S(1)}, bf16[1280,64]{1,0:T(8,128)(2,1)S(1)}, u32[]{:S(2)}, u32[]{:S(2)}) %collective-permute-start.1) | collective-permute-done | bytes 163872 | tf_op jit(solution)/shard_map/ppermute | solution.py:495
  12.7 4.8 %envelope_sums.1 = (bf16[4,208,128]{2,1,0:T(8,128)(2,1)S(1)}, bf16[4,208,128]{2,1,0:T(8,128)(2,1)S(1)}, bf16[4,208,128]{2,1,0:T(8,128)(2,1)S(1)}, bf16[4,208,128]{2,1,0:T(8,128)(2,1)S(1)}) custom-call(bf16[1280,128]{1,0:T(8,128)(2,1)S(1)} %copy-done, bf16[1280,64]{1,0:T(8,128)(2,1)S(1)} %collective-permute-done.left_ref, ...), custom_call_target="tpu_custom_call" | custom-call | flops 3000000000 | bytes 2000000 | tf_op jit(solution)/shard_map/envelope_sums/pallas_call | solution.py:170
  20.2 3.3 %collective-permute-done.2.refs_1_ = bf16[4,208,128]{2,1,0:T(8,128)(2,1)S(1)} collective-permute-done((bf16[4,208,128]{2,1,0:T(8,128)(2,1)S(1)}, bf16[4,208,128]{2,1,0:T(8,128)(2,1)S(1)}, u32[]{:S(2)}, u32[]{:S(2)}) %collective-permute-start.2) | collective-permute-done | bytes 213024 | tf_op jit(solution)/shard_map/ppermute | solution.py:483
  24.2 1.8 %add_arrived.4 = (bf16[2,208,128]{2,1,0:T(8,128)(2,1)}, bf16[2,208,128]{2,1,0:T(8,128)(2,1)}) custom-call(bf16[4,208,128]{2,1,0:T(8,128)(2,1)} %copy-done.3, bf16[4,208,128]{2,1,0:T(8,128)(2,1)} %copy-done.15), custom_call_target="tpu_custom_call" | custom-call | flops 1000000 | bytes 1000000 | tf_op jit(solution)/shard_map/add_arrived/pallas_call | solution.py:214
  26.9 1.8 %add_arrived.5 = (bf16[2,208,128]{2,1,0:T(8,128)(2,1)}, bf16[2,208,128]{2,1,0:T(8,128)(2,1)}) custom-call(bf16[4,208,128]{2,1,0:T(8,128)(2,1)} %copy-done.2, bf16[4,208,128]{2,1,0:T(8,128)(2,1)} %copy-done.14), custom_call_target="tpu_custom_call" | custom-call | flops 1000000 | bytes 1000000 | tf_op jit(solution)/shard_map/add_arrived/pallas_call | solution.py:214
  30.1 2.3 %collective-permute-done.5.refs_3_ = bf16[2,208,128]{2,1,0:T(8,128)(2,1)S(1)} collective-permute-done((bf16[2,208,128]{2,1,0:T(8,128)(2,1)}, bf16[2,208,128]{2,1,0:T(8,128)(2,1)S(1)}, u32[]{:S(2)}, u32[]{:S(2)}) %collective-permute-start.5) | collective-permute-done | bytes 106528 | tf_op jit(solution)/shard_map/ppermute | solution.py:483
  33.0 1.8 %add_arrived.6 = (bf16[2,208,128]{2,1,0:T(8,128)(2,1)}, bf16[2,208,128]{2,1,0:T(8,128)(2,1)}) custom-call(bf16[2,208,128]{2,1,0:T(8,128)(2,1)} %get-tuple-element.20.refs_0_, bf16[2,208,128]{2,1,0:T(8,128)(2,1)} %copy-done.19, bf16[2,208,128]{2,1,0:T(8,128)(2,1)} %get-tuple-element.24.refs_2_, bf16[2,208,128]{2,1,0:T(8,128)(2,1)} %copy-done.20), custom_call_target="tpu_custom_call" | custom-call | flops 1000000 | bytes 1000000 | tf_op jit(solution)/shard_map/add_arrived/pallas_call | solution.py:214
  34.8 2.3 %collective-permute-start.6 = (bf16[2,208,128]{2,1,0:T(8,128)(2,1)}, bf16[2,208,128]{2,1,0:T(8,128)(2,1)S(1)}, u32[]{:S(2)}, u32[]{:S(2)}) collective-permute-start(bf16[2,208,128]{2,1,0:T(8,128)(2,1)} %get-tuple-element.27), channel_id=1, source_target_pairs={{0,16},{4,20},{8,24},{12,28},{16,0},{20,4},{24,8},{28,12},{1,17},{... | collective-permute-start | bytes 319496 | tf_op jit(solution)/shard_map/ppermute | solution.py:483
  37.1 5.2 %collective-permute-done.6.refs_1_ = bf16[2,208,128]{2,1,0:T(8,128)(2,1)S(1)} collective-permute-done((bf16[2,208,128]{2,1,0:T(8,128)(2,1)}, bf16[2,208,128]{2,1,0:T(8,128)(2,1)S(1)}, u32[]{:S(2)}, u32[]{:S(2)}) %collective-permute-start.6) | collective-permute-done | bytes 106528 | tf_op jit(solution)/shard_map/ppermute | solution.py:483
  43.0 1.6 %add_arrived.7.own_ref = bf16[2,208,128]{2,1,0:T(8,128)(2,1)} custom-call(bf16[2,208,128]{2,1,0:T(8,128)(2,1)} %get-tuple-element.26.refs_0_, bf16[2,208,128]{2,1,0:T(8,128)(2,1)} %copy-done.18), custom_call_target="tpu_custom_call" | custom-call | flops 1000000 | bytes 1000000 | tf_op jit(solution)/shard_map/add_arrived/pallas_call | solution.py:214
  44.6 2.8 %collective-permute-start.7 = (bf16[2,208,128]{2,1,0:T(8,128)(2,1)}, bf16[2,208,128]{2,1,0:T(8,128)(2,1)S(1)}, u32[]{:S(2)}, u32[]{:S(2)}) collective-permute-start(bf16[2,208,128]{2,1,0:T(8,128)(2,1)} %add_arrived.7.own_ref), channel_id=1, source_target_pairs={{0,16},{4,20},{8,24},{12,28},{16,0},{20,4},{24,8},{28,12},{1,17},{... | collective-permute-start | bytes 319496 | tf_op jit(solution)/shard_map/ppermute | solution.py:483
  48.4 6.1 %lag_sums.1.lag_ref = bf16[2,192,8192]{2,1,0:T(8,128)(2,1)S(1)} custom-call(bf16[2,208,128]{2,1,0:T(8,128)(2,1)S(1)} %copy-done.1), custom_call_target="tpu_custom_call" | custom-call | flops 5000000000 | bytes 6000000 | tf_op jit(solution)/shard_map/lag_sums/pallas_call | solution.py:265
  54.5 2.7 %copy-done.8 = bf16[2,192,8192]{2,1,0:T(8,128)(2,1)} copy-done((bf16[2,192,8192]{2,1,0:T(8,128)(2,1)}, bf16[2,192,8192]{2,1,0:T(8,128)(2,1)S(1)}, u32[]{:S(2)}) %copy-start.8) | copy-done | bytes 6291480
  58.6 2.3 %collective-permute-done.12 = bf16[2,208,128]{2,1,0:T(8,128)(2,1)S(1)} collective-permute-done((bf16[2,208,128]{2,1,0:T(8,128)(2,1)S(1)}, bf16[2,208,128]{2,1,0:T(8,128)(2,1)S(1)}, u32[]{:S(2)}, u32[]{:S(2)}) %collective-permute-start.12) | collective-permute-done | bytes 106528 | tf_op jit(solution)/shard_map/ppermute | solution.py:483
  62.1 2.7 %row_spectra.1 = (bf16[2,192,512]{2,1,0:T(8,128)(2,1)S(1)}, bf16[2,192,256]{2,1,0:T(8,128)(2,1)S(1)}, f32[2,192,128]{2,1,0:T(8,128)S(1)}) custom-call(bf16[2,208,128]{2,1,0:T(8,128)(2,1)S(1)} %copy-done.1, f32[256,256]{1,0:T(8,128)S(1)} %copy-done.7, f32[256,256]{1,0:T(8,128)S(1)} %copy-done.6, f32[256,256]{1,0:T(8,128)S(1)} %copy-done.5), custom_call_target="tpu_custom_call" | custom-call | flops 2000000000 | bytes 2000000 | tf_op jit(solution)/shard_map/row_spectra/pallas_call | solution.py:317
  65.9 4.9 %collective-permute-start.15 = (bf16[8,208,64]{2,1,0:T(8,128)(2,1)S(1)}, bf16[8,208,64]{2,1,0:T(8,128)(2,1)S(1)}, u32[]{:S(2)}, u32[]{:S(2)}) collective-permute-start(bf16[8,208,64]{2,1,0:T(8,128)(2,1)S(1)} %get-tuple-element.31), channel_id=1, source_target_pairs={{1,0},{2,1},{3,2},{5,4},{6,5},{7,6},{9,8},{10,9},{11,10},{13,12},{... | collective-permute-start | bytes 638984 | tf_op jit(solution)/shard_map/ppermute | solution.py:524
  70.8 7.6 %collective-permute-start.14 = (bf16[8,208,64]{2,1,0:T(8,128)(2,1)S(1)}, bf16[8,208,64]{2,1,0:T(8,128)(2,1)S(1)}, u32[]{:S(2)}, u32[]{:S(2)}) collective-permute-start(bf16[8,208,64]{2,1,0:T(8,128)(2,1)S(1)} %get-tuple-element.32), channel_id=1, source_target_pairs={{0,1},{1,2},{2,3},{4,5},{5,6},{6,7},{8,9},{9,10},{10,11},{12,13},{... | collective-permute-start | bytes 638984 | tf_op jit(solution)/shard_map/ppermute | solution.py:523
  78.7 1.9 %collective-permute-start.11 = (bf16[8,208,64]{2,1,0:T(8,128)(2,1)S(1)}, bf16[8,208,64]{2,1,0:T(8,128)(2,1)S(1)}, u32[]{:S(2)}, u32[]{:S(2)}) collective-permute-start(bf16[8,208,64]{2,1,0:T(8,128)(2,1)S(1)} %get-tuple-element.33), channel_id=1, source_target_pairs={{1,0},{2,1},{3,2},{5,4},{6,5},{7,6},{9,8},{10,9},{11,10},{13,12},{... | collective-permute-start | bytes 638984 | tf_op jit(solution)/shard_map/ppermute | solution.py:524
  80.6 3.6 %collective-permute-start.10 = (bf16[8,208,64]{2,1,0:T(8,128)(2,1)S(1)}, bf16[8,208,64]{2,1,0:T(8,128)(2,1)S(1)}, u32[]{:S(2)}, u32[]{:S(2)}) collective-permute-start(bf16[8,208,64]{2,1,0:T(8,128)(2,1)S(1)} %get-tuple-element.34), channel_id=1, source_target_pairs={{0,1},{1,2},{2,3},{4,5},{5,6},{6,7},{8,9},{9,10},{10,11},{12,13},{... | collective-permute-start | bytes 638984 | tf_op jit(solution)/shard_map/ppermute | solution.py:523
  85.2 17.3 %coupling.2.rest_0_ = f32[192,1536]{1,0:T(8,128)} custom-call(bf16[2,192,8192]{2,1,0:T(8,128)(2,1)} %copy-done.8, bf16[2,192,512]{2,1,0:T(8,128)(2,1)} %copy-done.9, bf16[2,192,256]{2,1,0:T(8,128)(2,1)} %copy-done.10, f32[2,192,128]{2,1,0:T(8,128)} %copy-done.11, bf16[4,208,128]{2,1,0:T(8,128)(2,1)} %copy-done.13, bf16[4,208,128]{2,1,0:T(8,128)(2,1)} %copy-done.17, ...), custom_call_target="tpu_custom_call" | custom-call | flops 8000000000 | bytes 10000000 | tf_op jit(solution)/shard_map/coupling/pallas_call | solution.py:461
  104.0 18.3 %coupling.3 = f32[188,2,1504]{2,1,0:T(2,128)} custom-call(bf16[2,192,8192]{2,1,0:T(8,128)(2,1)} %copy-done.8, bf16[2,192,512]{2,1,0:T(8,128)(2,1)} %copy-done.9, bf16[2,192,256]{2,1,0:T(8,128)(2,1)} %copy-done.10, f32[2,192,128]{2,1,0:T(8,128)} %copy-done.11, bf16[4,208,128]{2,1,0:T(8,128)(2,1)} %copy-done.12, bf16[4,208,128]{2,1,0:T(8,128)(2,1)} %copy-done.16, ...), custom_call_target="tpu_custom_call" | custom-call | flops 8000000000 | bytes 10000000 | tf_op jit(solution)/shard_map/coupling/pallas_call | solution.py:461
  (82 shorter events, 18.5 us)
Async XLA Ops:
  1.3 8.5 %collective-permute-start.1 = (bf16[1280,64]{1,0:T(8,128)(2,1)S(1)}, bf16[1280,64]{1,0:T(8,128)(2,1)S(1)}, u32[]{:S(2)}, u32[]{:S(2)}) collective-permute-start(bf16[1280,64]{1,0:T(8,128)(2,1)S(1)} %get-tuple-element.35), channel_id=1, source_target_pairs={{1,0},{2,1},{3,2},{5,4},{6,5},{7,6},{9,8},{10,9},{11,10},{13,12},{... | collective-permute-start | bytes 491528 | tf_op jit(solution)/shard_map/ppermute | solution.py:495
  3.9 7.1 %collective-permute-start = (bf16[1280,64]{1,0:T(8,128)(2,1)S(1)}, bf16[1280,64]{1,0:T(8,128)(2,1)S(1)}, u32[]{:S(2)}, u32[]{:S(2)}) collective-permute-start(bf16[1280,64]{1,0:T(8,128)(2,1)S(1)} %get-tuple-element.36), channel_id=1, source_target_pairs={{0,1},{1,2},{2,3},{4,5},{5,6},{6,7},{8,9},{9,10},{10,11},{12,13},{... | collective-permute-start | bytes 491528 | tf_op jit(solution)/shard_map/ppermute | solution.py:494
  18.8 4.7 %collective-permute-start.2 = (bf16[4,208,128]{2,1,0:T(8,128)(2,1)S(1)}, bf16[4,208,128]{2,1,0:T(8,128)(2,1)S(1)}, u32[]{:S(2)}, u32[]{:S(2)}) collective-permute-start(bf16[4,208,128]{2,1,0:T(8,128)(2,1)S(1)} %get-tuple-element.19), channel_id=1, source_target_pairs={{0,4},{4,0},{8,12},{12,8},{16,20},{20,16},{24,28},{28,24},{1,5},{5... | collective-permute-start | bytes 638984 | tf_op jit(solution)/shard_map/ppermute | solution.py:483
  20.0 6.1 %collective-permute-start.4 = (bf16[4,208,128]{2,1,0:T(8,128)(2,1)S(1)}, bf16[4,208,128]{2,1,0:T(8,128)(2,1)S(1)}, u32[]{:S(2)}, u32[]{:S(2)}) collective-permute-start(bf16[4,208,128]{2,1,0:T(8,128)(2,1)S(1)} %get-tuple-element.23), channel_id=1, source_target_pairs={{0,8},{4,12},{8,0},{12,4},{16,24},{20,28},{24,16},{28,20},{1,9},{5... | collective-permute-start | bytes 638984 | tf_op jit(solution)/shard_map/ppermute | solution.py:483
  26.0 4.1 %collective-permute-start.3 = (bf16[2,208,128]{2,1,0:T(8,128)(2,1)}, bf16[2,208,128]{2,1,0:T(8,128)(2,1)S(1)}, u32[]{:S(2)}, u32[]{:S(2)}) collective-permute-start(bf16[2,208,128]{2,1,0:T(8,128)(2,1)} %get-tuple-element.21), channel_id=1, source_target_pairs={{0,8},{4,12},{8,0},{12,4},{16,24},{20,28},{24,16},{28,20},{1,9},{5... | collective-permute-start | bytes 319496 | tf_op jit(solution)/shard_map/ppermute | solution.py:483
  28.6 3.8 %collective-permute-start.5 = (bf16[2,208,128]{2,1,0:T(8,128)(2,1)}, bf16[2,208,128]{2,1,0:T(8,128)(2,1)S(1)}, u32[]{:S(2)}, u32[]{:S(2)}) collective-permute-start(bf16[2,208,128]{2,1,0:T(8,128)(2,1)} %get-tuple-element.25), channel_id=1, source_target_pairs={{0,4},{4,0},{8,12},{12,8},{16,20},{20,16},{24,28},{28,24},{1,5},{5... | collective-permute-start | bytes 319496 | tf_op jit(solution)/shard_map/ppermute | solution.py:483
  34.8 7.5 %collective-permute-start.6 = (bf16[2,208,128]{2,1,0:T(8,128)(2,1)}, bf16[2,208,128]{2,1,0:T(8,128)(2,1)S(1)}, u32[]{:S(2)}, u32[]{:S(2)}) collective-permute-start(bf16[2,208,128]{2,1,0:T(8,128)(2,1)} %get-tuple-element.27), channel_id=1, source_target_pairs={{0,16},{4,20},{8,24},{12,28},{16,0},{20,4},{24,8},{28,12},{1,17},{... | collective-permute-start | bytes 319496 | tf_op jit(solution)/shard_map/ppermute | solution.py:483
  44.6 12.6 %collective-permute-start.7 = (bf16[2,208,128]{2,1,0:T(8,128)(2,1)}, bf16[2,208,128]{2,1,0:T(8,128)(2,1)S(1)}, u32[]{:S(2)}, u32[]{:S(2)}) collective-permute-start(bf16[2,208,128]{2,1,0:T(8,128)(2,1)} %add_arrived.7.own_ref), channel_id=1, source_target_pairs={{0,16},{4,20},{8,24},{12,28},{16,0},{20,4},{24,8},{28,12},{1,17},{... | collective-permute-start | bytes 319496 | tf_op jit(solution)/shard_map/ppermute | solution.py:483
  48.4 13.8 %copy-start.5 = (f32[256,256]{1,0:T(8,128)S(1)}, f32[256,256]{1,0:T(8,128)}, u32[]{:S(2)}) copy-start(f32[256,256]{1,0:T(8,128)} %constant.14.clone.inverse_ref) | copy-start | bytes 786436
  48.4 13.8 %copy-start.6 = (f32[256,256]{1,0:T(8,128)S(1)}, f32[256,256]{1,0:T(8,128)}, u32[]{:S(2)}) copy-start(f32[256,256]{1,0:T(8,128)} %constant.13.clone.to_weights_ref) | copy-start | bytes 786436
  48.4 13.8 %copy-start.7 = (f32[256,256]{1,0:T(8,128)S(1)}, f32[256,256]{1,0:T(8,128)}, u32[]{:S(2)}) copy-start(f32[256,256]{1,0:T(8,128)} %constant.12.clone.forward_ref) | copy-start | bytes 786436
  57.2 3.6 %collective-permute-start.12 = (bf16[2,208,128]{2,1,0:T(8,128)(2,1)S(1)}, bf16[2,208,128]{2,1,0:T(8,128)(2,1)S(1)}, u32[]{:S(2)}, u32[]{:S(2)}) collective-permute-start(bf16[2,208,128]{2,1,0:T(8,128)(2,1)S(1)} %pad_maximum_fusion.5), channel_id=1, source_target_pairs={{0,8},{4,12},{8,0},{12,4},{16,24},{20,28},{24,16},{28,20},{1,9},{5... | collective-permute-start | bytes 319496 | tf_op jit(solution)/shard_map/ppermute | solution.py:483
  57.3 7.6 %collective-permute-start.8 = (bf16[2,208,128]{2,1,0:T(8,128)(2,1)S(1)}, bf16[2,208,128]{2,1,0:T(8,128)(2,1)S(1)}, u32[]{:S(2)}, u32[]{:S(2)}) collective-permute-start(bf16[2,208,128]{2,1,0:T(8,128)(2,1)S(1)} %pad_maximum_fusion.4), channel_id=1, source_target_pairs={{0,4},{4,0},{8,12},{12,8},{16,20},{20,16},{24,28},{28,24},{1,5},{5... | collective-permute-start | bytes 319496 | tf_op jit(solution)/shard_map/ppermute | solution.py:483
  60.9 4.8 %collective-permute-start.13 = (bf16[4,208,128]{2,1,0:T(8,128)(2,1)S(1)}, bf16[4,208,128]{2,1,0:T(8,128)(2,1)S(1)}, u32[]{:S(2)}, u32[]{:S(2)}) collective-permute-start(bf16[4,208,128]{2,1,0:T(8,128)(2,1)S(1)} %pad_maximum_fusion.3.near_half), channel_id=1, source_target_pairs={{0,4},{4,0},{8,12},{12,8},{16,20},{20,16},{24,28},{28,24},{1,5},{5... | collective-permute-start | bytes 638984 | tf_op jit(solution)/shard_map/ppermute | solution.py:483
  64.8 13.8 %copy-start.9 = (bf16[2,192,512]{2,1,0:T(8,128)(2,1)}, bf16[2,192,512]{2,1,0:T(8,128)(2,1)S(1)}, u32[]{:S(2)}) copy-start(bf16[2,192,512]{2,1,0:T(8,128)(2,1)S(1)} %get-tuple-element.28.freq_ref) | copy-start | bytes 1179652
  64.9 13.8 %copy-start.10 = (bf16[2,192,256]{2,1,0:T(8,128)(2,1)}, bf16[2,192,256]{2,1,0:T(8,128)(2,1)S(1)}, u32[]{:S(2)}) copy-start(bf16[2,192,256]{2,1,0:T(8,128)(2,1)S(1)} %get-tuple-element.29.edge_ref) | copy-start | bytes 589828
  64.9 13.8 %copy-start.11 = (f32[2,192,128]{2,1,0:T(8,128)}, f32[2,192,128]{2,1,0:T(8,128)S(1)}, u32[]{:S(2)}) copy-start(f32[2,192,128]{2,1,0:T(8,128)S(1)} %get-tuple-element.30.column_ref) | copy-start | bytes 589828
  64.9 13.7 %copy-start.12 = (bf16[4,208,128]{2,1,0:T(8,128)(2,1)}, bf16[4,208,128]{2,1,0:T(8,128)(2,1)S(1)}, u32[]{:S(2)}) copy-start(bf16[4,208,128]{2,1,0:T(8,128)(2,1)S(1)} %pad_maximum_fusion.2.near_half) | copy-start | bytes 638980
  64.9 13.4 %collective-permute-start.9 = (bf16[4,208,128]{2,1,0:T(8,128)(2,1)S(1)}, bf16[4,208,128]{2,1,0:T(8,128)(2,1)S(1)}, u32[]{:S(2)}, u32[]{:S(2)}) collective-permute-start(bf16[4,208,128]{2,1,0:T(8,128)(2,1)S(1)} %pad_maximum_fusion.2.near_half), channel_id=1, source_target_pairs={{0,8},{4,12},{8,0},{12,4},{16,24},{20,28},{24,16},{28,20},{1,9},{5... | collective-permute-start | bytes 638984 | tf_op jit(solution)/shard_map/ppermute | solution.py:483
  65.9 18.4 %collective-permute-start.15 = (bf16[8,208,64]{2,1,0:T(8,128)(2,1)S(1)}, bf16[8,208,64]{2,1,0:T(8,128)(2,1)S(1)}, u32[]{:S(2)}, u32[]{:S(2)}) collective-permute-start(bf16[8,208,64]{2,1,0:T(8,128)(2,1)S(1)} %get-tuple-element.31), channel_id=1, source_target_pairs={{1,0},{2,1},{3,2},{5,4},{6,5},{7,6},{9,8},{10,9},{11,10},{13,12},{... | collective-permute-start | bytes 638984 | tf_op jit(solution)/shard_map/ppermute | solution.py:524
  70.8 13.5 %collective-permute-start.14 = (bf16[8,208,64]{2,1,0:T(8,128)(2,1)S(1)}, bf16[8,208,64]{2,1,0:T(8,128)(2,1)S(1)}, u32[]{:S(2)}, u32[]{:S(2)}) collective-permute-start(bf16[8,208,64]{2,1,0:T(8,128)(2,1)S(1)} %get-tuple-element.32), channel_id=1, source_target_pairs={{0,1},{1,2},{2,3},{4,5},{5,6},{6,7},{8,9},{9,10},{10,11},{12,13},{... | collective-permute-start | bytes 638984 | tf_op jit(solution)/shard_map/ppermute | solution.py:523
  78.4 24.1 %copy-start.16 = (bf16[4,208,128]{2,1,0:T(8,128)(2,1)}, bf16[4,208,128]{2,1,0:T(8,128)(2,1)S(1)}, u32[]{:S(2)}) copy-start(bf16[4,208,128]{2,1,0:T(8,128)(2,1)S(1)} %collective-permute-done.9.far_half) | copy-start | bytes 638980
  78.7 23.8 %collective-permute-start.11 = (bf16[8,208,64]{2,1,0:T(8,128)(2,1)S(1)}, bf16[8,208,64]{2,1,0:T(8,128)(2,1)S(1)}, u32[]{:S(2)}, u32[]{:S(2)}) collective-permute-start(bf16[8,208,64]{2,1,0:T(8,128)(2,1)S(1)} %get-tuple-element.33), channel_id=1, source_target_pairs={{1,0},{2,1},{3,2},{5,4},{6,5},{7,6},{9,8},{10,9},{11,10},{13,12},{... | collective-permute-start | bytes 638984 | tf_op jit(solution)/shard_map/ppermute | solution.py:524
  80.6 21.9 %collective-permute-start.10 = (bf16[8,208,64]{2,1,0:T(8,128)(2,1)S(1)}, bf16[8,208,64]{2,1,0:T(8,128)(2,1)S(1)}, u32[]{:S(2)}, u32[]{:S(2)}) collective-permute-start(bf16[8,208,64]{2,1,0:T(8,128)(2,1)S(1)} %get-tuple-element.34), channel_id=1, source_target_pairs={{0,1},{1,2},{2,3},{4,5},{5,6},{6,7},{8,9},{9,10},{10,11},{12,13},{... | collective-permute-start | bytes 638984 | tf_op jit(solution)/shard_map/ppermute | solution.py:523
  (17 other events, 32.0 us)

commit v3 on v2

--- a/solution.py
+++ b/solution.py
@@ -73,8 +73,10 @@
         self.rows = par_dev
         self.padded = (par_dev + 15) // 16 * 16
         self.extra = (par_dev + 63) // 64
-        self.height = (par_dev + 2 * self.extra + 15) // 16 * 16
         self.tail = par_dev // 16 * 16
+        self.first = par_dev - self.tail
+        self.height = self.tail + 32
+        assert 0 < self.first <= 16 - self.extra
 
 
 def level_of(parcel):
@@ -86,16 +88,16 @@
 
 def put_tail(form, tail, above, mean_rows):
     tail[...] = jnp.zeros_like(tail)
-    tail[0 : form.rows - form.tail] = above
+    tail[0 : form.first] = above
     high = mean_rows.astype(BF16).astype(F32)
-    at = form.rows - form.tail
+    at = form.first
     tail[at : at + form.extra] = high
-    tail[at + form.extra : at + 2 * form.extra] = mean_rows - high
+    tail[at + 16 : at + 16 + form.extra] = mean_rows - high
     return tail[...].astype(BF16)
 
 
 def front_kernel(
-    form, owners, orders, middle_ref, left_ref, right_ref, taps_ref, smooth_ref, ids_ref, *rest
+    form, owners, orders, middle_ref, first_ref, second_ref, taps_ref, smooth_ref, ids_ref, *rest
 ):
     outs, (env, tail) = rest[: 2 * BANDS], rest[2 * BANDS :]
     me = lax.axis_index("vert")
@@ -113,9 +115,13 @@
     turned = (((1,), (1,)), ((), ()))
     vertices = middle_ref.shape[0]
     step = 256
+    odd = lax.rem(lax.axis_index("tm"), 2) == 1
     for at in range(0, vertices, step):
         cut = slice(at, at + step)
-        wide = jnp.concatenate([middle_ref[cut], right_ref[cut], left_ref[cut]], axis=1)
+        first, second = first_ref[cut], second_ref[cut]
+        right = jnp.where(odd, second, first)[:, 0:64]
+        left = jnp.where(odd, first, second)[:, 64:128]
+        wide = jnp.concatenate([middle_ref[cut], right, left], axis=1)
         for band in range(BANDS):
             one = lax.dot_general(wide, filters[band], turned, preferred_element_type=F32)
             two = lax.dot_general(wide, filters[BANDS + band], turned, preferred_element_type=F32)
@@ -164,9 +170,9 @@
     return sum((1 if k & bit else 0) << j for j, bit in enumerate(order))
 
 
-def front(form, owners, orders, middle, left, right, taps, smooths, ids):
+def front(form, owners, orders, middle, first, second, taps, smooths, ids):
     shape = jax.ShapeDtypeStruct((owners // 2, form.height, 128), BF16)
-    operands = (middle, left, right, taps, smooths, ids)
+    operands = (middle, first, second, taps, smooths, ids)
     return pl.pallas_call(
         partial(front_kernel, form, owners, orders),
         out_shape=[shape] * (2 * BANDS),
@@ -176,50 +182,21 @@
             pltpu.VMEM((middle.shape[0], BANDS * 128), BF16),
             pltpu.VMEM((form.height - form.tail, 128), F32),
         ],
-        compiler_params=params(40),
+        compiler_params=params(16),
         cost_estimate=cost(3 * 10**9, 2 * 10**6),
         name="envelope_sums",
     )(*operands)
 
 
-def merge_kernel(form, halves, count, *refs):
-    ins, outs, tail = refs[: 2 * count], refs[2 * count : -1], refs[-1]
-    blocks = ins[0].shape[0]
-    at = form.rows - form.tail
-    for pair in range(count):
-        for n in range(blocks):
-            whole = ins[2 * pair][n].astype(F32) + ins[2 * pair + 1][n].astype(F32)
-            if halves == "own":
-                put = outs[0].at[n]
-            elif halves == "joined":
-                put = outs[n].at[pair]
-            else:
-                put = outs[n // (blocks // 2)].at[n % (blocks // 2)]
-            put[0 : form.tail] = whole[0 : form.tail].astype(BF16)
-            tail[...] = whole[form.tail :]
-            means = tail[at : at + form.extra] + tail[at + form.extra : at + 2 * form.extra]
-            put[form.tail :] = put_tail(form, tail, whole[form.tail : form.rows], means)
-
-
-def merge(form, pairs, halves):
-    operands = [cells for pair in pairs for cells in pair]
-    blocks = operands[0].shape[0]
-    size = (form.height, 128)
-    if halves == "own":
-        shapes = [(blocks, *size)]
-    elif halves == "joined":
-        shapes = [(len(pairs), *size)] * 2
-    else:
-        shapes = [(blocks // 2, *size)] * 2
-    return pl.pallas_call(
-        partial(merge_kernel, form, halves, len(pairs)),
-        out_shape=[jax.ShapeDtypeStruct(shape, BF16) for shape in shapes],
-        in_specs=[VMEM] * len(operands),
-        out_specs=[VMEM] * len(shapes),
-        scratch_shapes=[pltpu.VMEM((form.height - form.tail, 128), F32)],
-        cost_estimate=cost(10**6, 10**6),
-        name="add_arrived",
-    )(*operands)
+def added(form, kept, arrived):
+    whole = kept.astype(F32) + arrived.astype(F32)
+    high, low = whole[:, form.tail : form.tail + 16], whole[:, form.tail + 16 :]
+    row = lax.broadcasted_iota(jnp.int32, high.shape, 1)
+    holds = (row >= form.first) & (row < form.first + form.extra)
+    mean = high + low
+    big = lax.reduce_precision(mean, 8, 7)
+    parts = [whole[:, : form.tail], jnp.where(holds, big, high), jnp.where(holds, mean - big, 0.0)]
+    return jnp.concatenate([part.astype(BF16) for part in parts], axis=1)
 
 
 def scales_of(middle):
@@ -267,7 +244,7 @@
         out_shape=jax.ShapeDtypeStruct((BANDS, form.padded, 64 * 128), BF16),
         in_specs=[VMEM],
         out_specs=VMEM,
-        compiler_params=params(40),
+        compiler_params=params(12),
         cost_estimate=cost(5 * 10**9, 6 * 10**6),
         name="lag_sums",
     )(own)
@@ -319,7 +296,7 @@
         out_shape=[jax.ShapeDtypeStruct(*shape) for shape in shapes],
         in_specs=[VMEM] * 4,
         out_specs=[VMEM] * 3,
-        compiler_params=params(40),
+        compiler_params=params(12),
         cost_estimate=cost(2 * 10**9, 2 * 10**6),
         name="row_spectra",
     )(own, jnp.asarray(FORWARD), jnp.asarray(TO_WEIGHTS), jnp.asarray(INVERSE))
@@ -327,8 +304,8 @@
 
 def mean_column(form, block):
     shape = (form.padded, form.height - form.tail)
-    row, col = iota(shape, 0), iota(shape, 1) - (form.rows - form.tail)
-    pick = (col == row // 64) | (col - form.extra == row // 64)
+    row, col = iota(shape, 0), iota(shape, 1) - form.first
+    pick = (col == row // 64) | (col - 16 == row // 64)
     pick = jnp.where(pick, 1.0, 0.0).astype(BF16)
     spread = jnp.dot(pick, block[form.tail :], preferred_element_type=F32)
     own = iota(spread.shape, 1) == lax.rem(iota(spread.shape, 0), 64)
@@ -336,61 +313,60 @@
 
 
 def coupling_kernel(
-    form, owners, order, band, final, lag_ref, freq_ref, edge_ref, column_ref, near_half, far_half,
-    left_ref, right_ref, factor_ref, *rest
+    form, owners, orders, lag_ref, freq_ref, edge_ref, column_ref, near_0, far_0, near_1, far_1,
+    first_ref, second_ref, factor_ref, out_ref, result, blocks, rows, near, far, near_turn, far_turn, change
 ):
-    if final:
-        before_ref, out_ref, *scratch = rest
-        result = scratch.pop(0)
-    else:
-        result, *scratch = rest
-    blocks, rows, near, far, near_turn, far_turn, change = scratch
     me = lax.axis_index("vert")
     window, windows = lax.axis_index("tm"), lax.axis_size("tm")
+    odd = lax.rem(window, 2) == 1
     half = owners // 2
-    blocks[0:half] = near_half[...]
-    blocks[half:owners] = far_half[...]
+    for band, (low, high) in enumerate(((near_0, far_0), (near_1, far_1))):
+        blocks[band, 0:half] = low[...]
+        blocks[band, half:owners] = high[...]
     result[...] = jnp.zeros_like(result)
-    rows[...] = jnp.zeros_like(rows)
+    gaps = ((SPLIT, GROUP), (GROUP + owners * form.rows - SPLIT, rows.shape[1]))
+    for start, stop in gaps:
+        rows[:, start:stop] = jnp.zeros((BANDS, stop - start, 384), F32)
     lane = iota((1, 128), 1)
     is_left = lane < LAG
     first_window, last_window = window == 0, window == windows - 1
     outside = (first_window & is_left) | (last_window & ~is_left)
-    for owner in range(owners):
-        k = me ^ owner
-        p = sum(lax.rem(k // bit, 2) << j for j, bit in enumerate(order))
-        block = blocks[p]
-        middle = block[0 : form.padded].astype(F32)
-        mean = mean_column(form, block)
-        left, right = left_ref[p], right_ref[p]
-        margins = jnp.concatenate([left, right], axis=1)
-        around = margins[0 : form.padded].astype(F32)
-        shift_left = mean_column(form, left) - mean
-        shift_right = mean_column(form, right) - mean
-        around = (around + jnp.where(is_left, shift_left, shift_right)).astype(BF16).astype(F32)
-        around = jnp.where(outside, 0.0, around)
-        power, left_over = scales_of(middle)
-        mu = jnp.where(first_window | last_window, mean.astype(BF16).astype(F32) * power, 0.0)
-        extra = jnp.where(lane == 0, mu, jnp.where(lane == 1, left_over, 0.0))
-        begin = owner * form.rows
-        for lo, hi, gap in ((0, SPLIT, 0), (SPLIT, owners * form.rows, GROUP - SPLIT)):
-            start, stop = max(lo, begin), min(hi, begin + form.rows)
-            if start < stop:
-                cut = slice(start - begin, stop - begin)
-                put = slice(start + gap, stop + gap)
-                rows[put, 0:128] = (middle * power)[cut]
-                rows[put, 128:256] = (around * power)[cut]
-                rows[put, 256:384] = extra[cut]
+    for band in range(BANDS):
+        for owner in range(owners):
+            k = me ^ owner
+            p = sum(lax.rem(k // bit, 2) << j for j, bit in enumerate(orders[band]))
+            block = blocks[band, p]
+            middle = block[0 : form.padded].astype(F32)
+            mean = mean_column(form, block)
+            one, two = first_ref[band, p], second_ref[band, p]
+            left, right = jnp.where(odd, one, two), jnp.where(odd, two, one)
+            margins = jnp.concatenate([left, right], axis=1)
+            around = margins[0 : form.padded].astype(F32)
+            shift_left = mean_column(form, left) - mean
+            shift_right = mean_column(form, right) - mean
+            around = (around + jnp.where(is_left, shift_left, shift_right)).astype(BF16).astype(F32)
+            around = jnp.where(outside, 0.0, around)
+            power, left_over = scales_of(middle)
+            mu = jnp.where(first_window | last_window, mean.astype(BF16).astype(F32) * power, 0.0)
+            extra = jnp.where(lane == 0, mu, jnp.where(lane == 1, left_over, 0.0))
+            begin = owner * form.rows
+            for lo, hi, gap in ((0, SPLIT, 0), (SPLIT, owners * form.rows, GROUP - SPLIT)):
+                start, stop = max(lo, begin), min(hi, begin + form.rows)
+                if start < stop:
+                    cut = slice(start - begin, stop - begin)
+                    put = slice(start + gap, stop + gap)
+                    rows[band, put, 0:128] = (middle * power)[cut]
+                    rows[band, put, 128:256] = (around * power)[cut]
+                    rows[band, put, 256:384] = extra[cut]
 
     own_parcel = iota((form.padded, 1), 0) + me * form.rows
     own_level = level_of(own_parcel)
     own_level = jnp.where(own_level < 3, own_level, -1)
-    factors = column_ref[band]
-    edge_sum, own_factor = factors[:, 0:1], factors[:, 1:2]
-
-    def tile(n, carry):
-        first = pl.multiple_of(n * TILE, TILE)
-        columns = rows[pl.ds(first, TILE), :].T
+
+    def tile(step, carry):
+        band = lax.rem(step, BANDS)
+        first = pl.multiple_of((step // BANDS) * TILE, TILE)
+        columns = rows[band, pl.ds(first, TILE), :].T
         narrow = columns[0:256].astype(BF16)
         near[0:64] = columns[128:192]
         near[64:127] = columns[0:63]
@@ -426,55 +402,53 @@
         total += jnp.dot(weights[:, 0:256], small, preferred_element_type=F32)
         mixed = jnp.dot(edge_ref[band], narrow, preferred_element_type=F32)
         mu, other_factor = columns[256:257], columns[257:258]
+        factors = column_ref[band]
+        edge_sum, own_factor = factors[:, 0:1], factors[:, 1:2]
         total += mu * (mu * edge_sum - 2.0 * mixed)
         column = iota((1, TILE), 1) + first
         parcel = jnp.where(column < GROUP, column, column - (GROUP - SPLIT))
         gap = (column >= SPLIT) & (column < GROUP)
         other_level = jnp.where(gap, 3, level_of(parcel))
         scaled = total * own_factor * other_factor
-        result[:, pl.ds(first, TILE)] = jnp.where(own_level == other_level, scaled, 0.0)
+        result[band, :, pl.ds(first, TILE)] = jnp.where(own_level == other_level, scaled, 0.0)
         return carry
 
     begin = me * form.rows
     end = jnp.minimum(begin + form.rows, SPLIT + P3)
-    tiles = result.shape[1] // TILE
+    tiles = result.shape[2] // TILE
     lax.fori_loop(
-        jnp.where(begin < SPLIT, 0, GROUP // TILE),
-        jnp.where(end <= SPLIT, GROUP // TILE, tiles),
+        jnp.where(begin < SPLIT, 0, GROUP // TILE) * BANDS,
+        jnp.where(end <= SPLIT, GROUP // TILE, tiles) * BANDS,
         tile,
         0,
     )
-    if final:
-        total = owners * form.rows
-        for k, cells in ((1 - band, before_ref), (band, result)):
-            out_ref[:, k, 0:SPLIT] = cells[0 : form.rows, 0:SPLIT]
-            out_ref[:, k, SPLIT:total] = cells[0 : form.rows, GROUP : GROUP + total - SPLIT]
-
-
-def coupling(form, owners, order, band, before, *operands):
+    total = owners * form.rows
+    for band in range(BANDS):
+        out_ref[:, band, 0:SPLIT] = result[band, 0 : form.rows, 0:SPLIT]
+        out_ref[:, band, SPLIT:total] = result[band, 0 : form.rows, GROUP : GROUP + total - SPLIT]
+
+
+def coupling(form, owners, orders, *operands):
     total = owners * form.rows
     width = GROUP + (total - SPLIT + TILE - 1) // TILE * TILE
-    final = before is not None
-    operands = (*operands, jnp.asarray(FACTORS), *((before,) if final else ()))
-    result = (form.padded, width)
-    out = (form.rows, BANDS, total) if final else result
+    operands = (*operands, jnp.asarray(FACTORS))
     return pl.pallas_call(
-        partial(coupling_kernel, form, owners, order, band, final),
-        out_shape=jax.ShapeDtypeStruct(out, F32),
+        partial(coupling_kernel, form, owners, orders),
+        out_shape=jax.ShapeDtypeStruct((form.rows, BANDS, total), F32),
         in_specs=[VMEM] * len(operands),
         out_specs=VMEM,
-        scratch_shapes=([pltpu.VMEM(result, F32)] if final else [])
-        + [
-            pltpu.VMEM((owners, form.height, 128), BF16),
-            pltpu.VMEM((width, 384), F32),
+        scratch_shapes=[
+            pltpu.VMEM((BANDS, form.padded, width), F32),
+            pltpu.VMEM((BANDS, owners, form.height, 128), BF16),
+            pltpu.VMEM((BANDS, width, 384), F32),
             pltpu.VMEM((192, TILE), F32),
             pltpu.VMEM((192, TILE), F32),
             pltpu.VMEM((16, 176, TILE), BF16),
             pltpu.VMEM((16, 176, TILE), BF16),
             pltpu.VMEM((64 * 128, TILE), BF16),
         ],
-        compiler_params=params(56),
-        cost_estimate=cost(8 * 10**9, 10**7),
+        compiler_params=params(40),
+        cost_estimate=cost(16 * 10**9, 10**7),
         name="coupling",
     )(*operands)
 
@@ -489,23 +463,21 @@
     form = Rows((P1 + P2 + P3 + owners - 1) // owners)
     bits = [1 << k for k in range(owners.bit_length() - 1)]
     orders = [bits, [bits[1], bits[0], *bits[2:]]]
-    up = [(i, i + 1) for i in range(windows - 1)]
-    down = [(i + 1, i) for i in range(windows - 1)]
-    left = lax.ppermute(source[:, t_dev - 2 * HALF :], "tm", up)
-    right = lax.ppermute(source[:, : 2 * HALF], "tm", down)
+    window = lax.axis_index("tm")
+    odd = lax.rem(window, 2) == 1
+    meet = [[p for i in range(k, windows - 1, 2) for p in ((i, i + 1), (i + 1, i))] for k in range(2)]
+    first, second = (lax.ppermute(source, "tm", pairs) for pairs in meet)
     taps = jnp.pad(band_taps.astype(F32).reshape(2 * BANDS, 1, TAPS), ((0, 0), (0, 0), (0, 256 - TAPS)))
     smooths = jnp.pad(smooth_taps.astype(F32)[:, None, :], ((0, 0), (0, 0), (0, 256 - TAPS)))
-    parts = front(form, owners, orders, source, left, right, taps, smooths, parcel_ids)
+    parts = front(form, owners, orders, source, first, second, taps, smooths, parcel_ids)
     parts = [parts[0:2], parts[2:4]]
     for step in range(len(bits) - 1):
         arrived = [swap(parts[b][1], owners, orders[b][step]) for b in range(BANDS)]
-        pairs = [(parts[b][0], arrived[b]) for b in range(BANDS)]
-        if step < len(bits) - 2:
-            parts = [merge(form, [pair], "halves") for pair in pairs]
-        else:
-            kept, sent = merge(form, pairs, "joined")
-    arrived = swap(sent, owners, bits[-1])
-    (own,) = merge(form, [(kept, arrived)], "own")
+        sums = [added(form, parts[b][0], arrived[b]) for b in range(BANDS)]
+        half = sums[0].shape[0] // 2
+        parts = [(cells[:half], cells[half:]) for cells in sums]
+    kept, sent = (jnp.concatenate([parts[b][k] for b in range(BANDS)], axis=0) for k in range(2))
+    own = added(form, kept, swap(sent, owners, bits[-1]))
 
     lag = lag_sums(form, own)
     freq, edge, column = spectra(form, own)
@@ -517,12 +489,12 @@
         halves = [(held[b], arrived[b]) for b in range(BANDS)]
         if step:
             held = [jnp.concatenate(pair, axis=0) for pair in halves]
-    done = None
-    for b in range(BANDS):
-        whole = jnp.concatenate(halves[b], axis=0)
-        left = lax.ppermute(whole[:, :, t_dev - LAG :], "tm", up)
-        right = lax.ppermute(whole[:, :, :LAG], "tm", down)
-        done = coupling(form, owners, orders[b][::-1], b, done, lag, freq, edge, column, *halves[b], left, right)
+    whole = jnp.stack([jnp.concatenate(pair, axis=0) for pair in halves])
+    early, late = whole[..., :LAG], whole[..., t_dev - LAG :]
+    first = lax.ppermute(jnp.where(odd, early, late), "tm", meet[0])
+    second = lax.ppermute(jnp.where(odd, late, early), "tm", meet[1])
+    turned = [order[::-1] for order in orders]
+    done = coupling(form, owners, turned, lag, freq, edge, column, *halves[0], *halves[1], first, second)
     return done.transpose(1, 0, 2)[None]
 
 

time: 123 us -> 106 us (0.86)
  Pallas kernels: 56.1 us -> 40.7 us
  starting transfers between devices: 34.8 us -> 21.5 us
  waiting for transfers between devices: 16 us -> 24.5 us
  other arithmetic: 0.18 us -> 2.06 us
    pallas_call x6 -> x1, Pallas kernels: 42.5 us -> 27.1 us  [coupling(): pl.pallas_call(partial(coupling_kernel, form, owners, orders), out_shape=...]
    ppermute x6 -> x4, starting transfers between devices: 23.7 us -> 10.4 us  [the longest x1 6.74 us: local(): second = lax.ppermute(jnp.where(odd, late, early), 'tm', meet[1])]
    ppermute x10, waiting for transfers between devices: 13.4 us -> 20.3 us  [swap(): return lax.ppermute(cells, 'vert', [(i, i ^ bit) for i in range(owners)])]
    ppermute x0 -> x2, local copies, waits for them, and re-layouts: none -> 2.93 us  [the longest x1 1.49 us: local(): first = lax.ppermute(jnp.where(odd, early, late), 'tm', meet[0])]
    unnamed x50 -> x24, local copies, waits for them, and re-layouts: 11.8 us -> 8.99 us
    select_n x0 -> x2, local copies, waits for them, and re-layouts: none -> 2.61 us  [the longest x1 1.47 us: local(): second = lax.ppermute(jnp.where(odd, late, early), 'tm', meet[1])]
    ppermute x6 -> x4, waiting for transfers between devices: 2.65 us -> 4.2 us  [the longest x2 4.2 us: local(): first, second = (lax.ppermute(source, 'tm', pairs) for pairs in meet)]
    slice x3 -> x9, local copies, waits for them, and re-layouts: 1.66 us -> 0.13 us  [the longest x5 0.1 us: added(): whole[:, :form.tail]]
  transfers between devices with their start and end apart: 16 -> 14, of which waited for: 7 -> 11; matrix products, arithmetic and copies ran while one was open for 2% -> 3% of each run, Pallas kernels for 24% -> 8%
where the time goes in v3:
time: 106 us; the launch traced here: 105 us
  Pallas kernels  40.7 us (38%)
  waiting for transfers between devices  24.5 us (23%)
  starting transfers between devices  21.5 us (20%)
  local copies, waits for them, and re-layouts  16 us (15%)
  other arithmetic  2.06 us (2%)
    pallas_call x1, Pallas kernels, coupling(): pl.pallas_call(partial(coupling_kernel, form, owners, orders), out_shape=...  27.1 us
    ppermute x10, waiting for transfers between devices, swap(): return lax.ppermute(cells, 'vert', [(i, i ^ bit) for i in range(owners)])  20.3 us
    ppermute x10, starting transfers between devices, swap(): return lax.ppermute(cells, 'vert', [(i, i ^ bit) for i in range(owners)])  11.1 us
    unnamed x24, local copies, waits for them, and re-layouts  8.99 us
    ppermute x1, starting transfers between devices, local(): second = lax.ppermute(jnp.where(odd, late, early), 'tm', meet[1])  6.74 us
    pallas_call x1, Pallas kernels, lag_sums(): pl.pallas_call(partial(lag_sums_kernel, form), out_shape=jax.ShapeDtypeSt...  6.09 us
    pallas_call x1, Pallas kernels, front(): pl.pallas_call(partial(front_kernel, form, owners, orders), out_shape=[sh...  4.78 us
    ppermute x2, waiting for transfers between devices, local(): first, second = (lax.ppermute(source, 'tm', pairs) for pairs in meet)  4.2 us
  transfers between devices with their start and end apart: 14, of which 11 were waited for; matrix products, arithmetic and copies ran while one was open for 3% of the time, Pallas kernels for 8%

profile of v3, /device:TPU:9, one launch (start us, length us, event | category | flops | bytes accessed | tf_op | source)
XLA Modules:
  0.0 105.1 jit_solution(5987627111029955189)
XLA Ops:
  0.7 3.0 %collective-permute-start.1 = (bf16[1280,128]{1,0:T(8,128)(2,1)}, bf16[1280,128]{1,0:T(8,128)(2,1)S(1)}, u32[]{:S(2)}, u32[]{:S(2)}) collective-permute-start(bf16[1280,128]{1,0:T(8,128)(2,1)} %middle_ref.1), channel_id=1, source_target_pairs={{1,2},{2,1},{5,6},{6,5},{9,10},{10,9},{13,14},{14,13},{17,18},{18,... | collective-permute-start | bytes 983048 | tf_op jit(solution)/shard_map/ppermute | solution.py:469
  5.1 4.2 %collective-permute-done.1.second_ref = bf16[1280,128]{1,0:T(8,128)(2,1)S(1)} collective-permute-done((bf16[1280,128]{1,0:T(8,128)(2,1)}, bf16[1280,128]{1,0:T(8,128)(2,1)S(1)}, u32[]{:S(2)}, u32[]{:S(2)}) %collective-permute-start.1) | collective-permute-done | bytes 327712 | tf_op jit(solution)/shard_map/ppermute | solution.py:469
  11.0 4.8 %envelope_sums.1 = (bf16[4,208,128]{2,1,0:T(8,128)(2,1)S(1)}, bf16[4,208,128]{2,1,0:T(8,128)(2,1)S(1)}, bf16[4,208,128]{2,1,0:T(8,128)(2,1)S(1)}, bf16[4,208,128]{2,1,0:T(8,128)(2,1)S(1)}) custom-call(bf16[1280,128]{1,0:T(8,128)(2,1)S(1)} %copy-done, bf16[1280,128]{1,0:T(8,128)(2,1)S(1)} %collective-permute-done.first_ref, ...), custom_call_target="tpu_custom_call" | custom-call | flops 3000000000 | bytes 2000000 | tf_op jit(solution)/shard_map/envelope_sums/pallas_call | solution.py:176
  17.2 3.8 %collective-permute-done.2 = bf16[4,208,128]{2,1,0:T(8,128)(2,1)S(1)} collective-permute-done((bf16[4,208,128]{2,1,0:T(8,128)(2,1)S(1)}, bf16[4,208,128]{2,1,0:T(8,128)(2,1)S(1)}, u32[]{:S(2)}, u32[]{:S(2)}) %collective-permute-start.2) | collective-permute-done | bytes 213024 | tf_op jit(solution)/shard_map/ppermute | solution.py:457
  21.1 1.8 %collective-permute-done.4 = bf16[4,208,128]{2,1,0:T(8,128)(2,1)S(1)} collective-permute-done((bf16[4,208,128]{2,1,0:T(8,128)(2,1)S(1)}, bf16[4,208,128]{2,1,0:T(8,128)(2,1)S(1)}, u32[]{:S(2)}, u32[]{:S(2)}) %collective-permute-start.4) | collective-permute-done | bytes 213024 | tf_op jit(solution)/shard_map/ppermute | solution.py:457
  23.7 3.0 %collective-permute-done.3 = bf16[2,208,128]{2,1,0:T(8,128)(2,1)S(1)} collective-permute-done((bf16[2,208,128]{2,1,0:T(8,128)(2,1)S(1)}, bf16[2,208,128]{2,1,0:T(8,128)(2,1)S(1)}, u32[]{:S(2)}, u32[]{:S(2)}) %collective-permute-start.3) | collective-permute-done | bytes 106528 | tf_op jit(solution)/shard_map/ppermute | solution.py:457
  27.5 2.4 %collective-permute-start.6 = (bf16[2,208,128]{2,1,0:T(8,128)(2,1)S(1)}, bf16[2,208,128]{2,1,0:T(8,128)(2,1)S(1)}, u32[]{:S(2)}, u32[]{:S(2)}) collective-permute-start(bf16[2,208,128]{2,1,0:T(8,128)(2,1)S(1)} %pad_maximum_fusion.7), channel_id=1, source_target_pairs={{0,16},{4,20},{8,24},{12,28},{16,0},{20,4},{24,8},{28,12},{1,17},{... | collective-permute-start | bytes 319496 | tf_op jit(solution)/shard_map/ppermute | solution.py:457
  29.9 2.2 %collective-permute-done.6 = bf16[2,208,128]{2,1,0:T(8,128)(2,1)S(1)} collective-permute-done((bf16[2,208,128]{2,1,0:T(8,128)(2,1)S(1)}, bf16[2,208,128]{2,1,0:T(8,128)(2,1)S(1)}, u32[]{:S(2)}, u32[]{:S(2)}) %collective-permute-start.6) | collective-permute-done | bytes 106528 | tf_op jit(solution)/shard_map/ppermute | solution.py:457
  32.3 4.6 %collective-permute-start.7 = (bf16[2,208,128]{2,1,0:T(8,128)(2,1)S(1)}, bf16[2,208,128]{2,1,0:T(8,128)(2,1)S(1)}, u32[]{:S(2)}, u32[]{:S(2)}) collective-permute-start(bf16[2,208,128]{2,1,0:T(8,128)(2,1)S(1)} %pad_maximum_fusion.8.own_ref), channel_id=1, source_target_pairs={{0,16},{4,20},{8,24},{12,28},{16,0},{20,4},{24,8},{28,12},{1,17},{... | collective-permute-start | bytes 319496 | tf_op jit(solution)/shard_map/ppermute | solution.py:457
  36.9 2.2 %collective-permute-done.7 = bf16[2,208,128]{2,1,0:T(8,128)(2,1)S(1)} collective-permute-done((bf16[2,208,128]{2,1,0:T(8,128)(2,1)S(1)}, bf16[2,208,128]{2,1,0:T(8,128)(2,1)S(1)}, u32[]{:S(2)}, u32[]{:S(2)}) %collective-permute-start.7) | collective-permute-done | bytes 106528 | tf_op jit(solution)/shard_map/ppermute | solution.py:457
  39.1 1.9 %collective-permute-start.8 = (bf16[2,208,128]{2,1,0:T(8,128)(2,1)S(1)}, bf16[2,208,128]{2,1,0:T(8,128)(2,1)S(1)}, u32[]{:S(2)}, u32[]{:S(2)}) collective-permute-start(bf16[2,208,128]{2,1,0:T(8,128)(2,1)S(1)} %pad_maximum_fusion.9), channel_id=1, source_target_pairs={{0,8},{4,12},{8,0},{12,4},{16,24},{20,28},{24,16},{28,20},{1,9},{5... | collective-permute-start | bytes 319496 | tf_op jit(solution)/shard_map/ppermute | solution.py:457
  41.1 2.0 %collective-permute-done.8 = bf16[2,208,128]{2,1,0:T(8,128)(2,1)S(1)} collective-permute-done((bf16[2,208,128]{2,1,0:T(8,128)(2,1)S(1)}, bf16[2,208,128]{2,1,0:T(8,128)(2,1)S(1)}, u32[]{:S(2)}, u32[]{:S(2)}) %collective-permute-start.8) | collective-permute-done | bytes 106528 | tf_op jit(solution)/shard_map/ppermute | solution.py:457
  43.2 2.9 %collective-permute-done.10 = bf16[2,208,128]{2,1,0:T(8,128)(2,1)S(1)} collective-permute-done((bf16[2,208,128]{2,1,0:T(8,128)(2,1)S(1)}, bf16[2,208,128]{2,1,0:T(8,128)(2,1)S(1)}, u32[]{:S(2)}, u32[]{:S(2)}) %collective-permute-start.10) | collective-permute-done | bytes 106528 | tf_op jit(solution)/shard_map/ppermute | solution.py:457
  46.2 2.7 %row_spectra.1 = (bf16[2,192,512]{2,1,0:T(8,128)(2,1)S(1)}, bf16[2,192,256]{2,1,0:T(8,128)(2,1)S(1)}, f32[2,192,128]{2,1,0:T(8,128)S(1)}) custom-call(bf16[2,208,128]{2,1,0:T(8,128)(2,1)S(1)} %pad_maximum_fusion.8.own_ref, f32[256,256]{1,0:T(8,128)S(1)} %copy-done.5, f32[256,256]{1,0:T(8,128)S(1)} %copy-done.4, f32[256,256]{1,0:T(8,128)S(1)} %copy-done.3), custom_call_target="tpu_custom_call" | custom-call | flops 2000000000 | bytes 2000000 | tf_op jit(solution)/shard_map/row_spectra/pallas_call | solution.py:294
  49.2 1.7 %collective-permute-done.11.far_1 = bf16[4,208,128]{2,1,0:T(8,128)(2,1)S(1)} collective-permute-done((bf16[4,208,128]{2,1,0:T(8,128)(2,1)S(1)}, bf16[4,208,128]{2,1,0:T(8,128)(2,1)S(1)}, u32[]{:S(2)}, u32[]{:S(2)}) %collective-permute-start.11) | collective-permute-done | bytes 213024 | tf_op jit(solution)/shard_map/ppermute | solution.py:457
  50.9 1.4 %broadcast_select_fusion = (bf16[2,8,208,64]{3,2,1,0:T(8,128)(2,1)}, bf16[2,8,208,64]{3,2,1,0:T(8,128)(2,1)S(1)}) fusion(pred[]{:T(512)S(6)} %eq.3, bf16[1,8,208,128]{3,2,1,0:T(8,128)(2,1)S(1)} %maximum_bitcast_fusion.1, bf16[1,8,208,128]{3,2,1,0:T(8,128)(2,1)S(1)} %maximum_bitcast_fusion), kind=kLoop, calls=%fused_computation.2 | loop fusion | flops 2981888 | bytes 1703937 | tf_op jit(solution)/shard_map/jit(_where)/select_n | solution.py:495
  52.3 1.5 %copy.14 = bf16[2,8,208,64]{2,3,1,0:T(8,128)(2,1)S(1)} copy(bf16[2,8,208,64]{3,2,1,0:T(8,128)(2,1)} %get-tuple-element.19) | data formatting | bytes 851968 | tf_op jit(solution)/shard_map/jit(_where)/select_n | solution.py:495
  55.0 6.7 %collective-permute-start.13 = (bf16[2,8,208,64]{2,3,1,0:T(8,128)(2,1)S(1)}, bf16[2,8,208,64]{2,3,1,0:T(8,128)(2,1)}, u32[]{:S(2)}, u32[]{:S(2)}) collective-permute-start(bf16[2,8,208,64]{2,3,1,0:T(8,128)(2,1)S(1)} %copy.14), channel_id=1, source_target_pairs={{1,2},{2,1},{5,6},{6,5},{9,10},{10,9},{13,14},{14,13},{17,18},{18,... | collective-permute-start | bytes 1277960 | tf_op jit(solution)/shard_map/ppermute | solution.py:495
  61.7 6.1 %lag_sums.1.lag_ref = bf16[2,192,8192]{2,1,0:T(8,128)(2,1)S(1)} custom-call(bf16[2,208,128]{2,1,0:T(8,128)(2,1)S(1)} %pad_maximum_fusion.8.own_ref), custom_call_target="tpu_custom_call" | custom-call | flops 5000000000 | bytes 6000000 | tf_op jit(solution)/shard_map/lag_sums/pallas_call | solution.py:242
  67.8 2.6 %copy-done.6 = bf16[2,192,8192]{2,1,0:T(8,128)(2,1)} copy-done((bf16[2,192,8192]{2,1,0:T(8,128)(2,1)}, bf16[2,192,8192]{2,1,0:T(8,128)(2,1)S(1)}, u32[]{:S(2)}) %copy-start.6) | copy-done | bytes 6291480
  70.4 1.5 %copy.15.first_ref = bf16[2,8,208,64]{3,2,1,0:T(8,128)(2,1)S(1)} copy(bf16[2,8,208,64]{2,3,1,0:T(8,128)(2,1)} %collective-permute-done.12) | data formatting | bytes 851968 | tf_op jit(solution)/shard_map/ppermute | solution.py:494
  71.9 1.4 %copy.16.second_ref = bf16[2,8,208,64]{3,2,1,0:T(8,128)(2,1)S(1)} copy(bf16[2,8,208,64]{2,3,1,0:T(8,128)(2,1)} %collective-permute-done.13) | data formatting | bytes 851968 | tf_op jit(solution)/shard_map/ppermute | solution.py:495
  73.4 2.8 %copy-done.7 = bf16[2,192,8192]{2,1,0:T(8,128)(2,1)S(1)} copy-done((bf16[2,192,8192]{2,1,0:T(8,128)(2,1)S(1)}, bf16[2,192,8192]{2,1,0:T(8,128)(2,1)}, u32[]{:S(2)}) %copy-start.7) | copy-done | bytes 6291480
  78.0 27.1 %coupling.1 = f32[188,2,1504]{2,1,0:T(2,128)} custom-call(bf16[2,192,8192]{2,1,0:T(8,128)(2,1)S(1)} %copy-done.7, bf16[2,192,512]{2,1,0:T(8,128)(2,1)S(1)} %get-tuple-element.16.freq_ref, bf16[2,192,256]{2,1,0:T(8,128)(2,1)S(1)} %copy-done.9, f32[2,192,128]{2,1,0:T(8,128)S(1)} %copy-done.11, bf16[4,208,128]{2,1,0:T(8,128)(2,1)S(1)} %pad_maximum_fusion.3.near_0, ...), custom_call_target="tpu_custom_call" | custom-call | flops 16000000000 | bytes 10000000 | tf_op jit(solution)/shard_map/coupling/pallas_call | solution.py:435
  (72 shorter events, 10.5 us)
Async XLA Ops:
  0.0 5.1 %collective-permute-start = (bf16[1280,128]{1,0:T(8,128)(2,1)}, bf16[1280,128]{1,0:T(8,128)(2,1)S(1)}, u32[]{:S(2)}, u32[]{:S(2)}) collective-permute-start(bf16[1280,128]{1,0:T(8,128)(2,1)} %middle_ref.1), channel_id=1, source_target_pairs={{0,1},{1,0},{2,3},{3,2},{4,5},{5,4},{6,7},{7,6},{8,9},{9,8},{10,11... | collective-permute-start | bytes 983048 | tf_op jit(solution)/shard_map/ppermute | solution.py:469
  0.7 8.6 %collective-permute-start.1 = (bf16[1280,128]{1,0:T(8,128)(2,1)}, bf16[1280,128]{1,0:T(8,128)(2,1)S(1)}, u32[]{:S(2)}, u32[]{:S(2)}) collective-permute-start(bf16[1280,128]{1,0:T(8,128)(2,1)} %middle_ref.1), channel_id=1, source_target_pairs={{1,2},{2,1},{5,6},{6,5},{9,10},{10,9},{13,14},{14,13},{17,18},{18,... | collective-permute-start | bytes 983048 | tf_op jit(solution)/shard_map/ppermute | solution.py:469
  9.3 1.0 copy-start
  15.8 5.2 %collective-permute-start.2 = (bf16[4,208,128]{2,1,0:T(8,128)(2,1)S(1)}, bf16[4,208,128]{2,1,0:T(8,128)(2,1)S(1)}, u32[]{:S(2)}, u32[]{:S(2)}) collective-permute-start(bf16[4,208,128]{2,1,0:T(8,128)(2,1)S(1)} %get-tuple-element.13), channel_id=1, source_target_pairs={{0,4},{4,0},{8,12},{12,8},{16,20},{20,16},{24,28},{28,24},{1,5},{5... | collective-permute-start | bytes 638984 | tf_op jit(solution)/shard_map/ppermute | solution.py:457
  17.0 5.8 %collective-permute-start.4 = (bf16[4,208,128]{2,1,0:T(8,128)(2,1)S(1)}, bf16[4,208,128]{2,1,0:T(8,128)(2,1)S(1)}, u32[]{:S(2)}, u32[]{:S(2)}) collective-permute-start(bf16[4,208,128]{2,1,0:T(8,128)(2,1)S(1)} %get-tuple-element.15), channel_id=1, source_target_pairs={{0,8},{4,12},{8,0},{12,4},{16,24},{20,28},{24,16},{28,20},{1,9},{5... | collective-permute-start | bytes 638984 | tf_op jit(solution)/shard_map/ppermute | solution.py:457
  23.1 3.6 %collective-permute-start.3 = (bf16[2,208,128]{2,1,0:T(8,128)(2,1)S(1)}, bf16[2,208,128]{2,1,0:T(8,128)(2,1)S(1)}, u32[]{:S(2)}, u32[]{:S(2)}) collective-permute-start(bf16[2,208,128]{2,1,0:T(8,128)(2,1)S(1)} %slice.125), channel_id=1, source_target_pairs={{0,8},{4,12},{8,0},{12,4},{16,24},{20,28},{24,16},{28,20},{1,9},{5... | collective-permute-start | bytes 319496 | tf_op jit(solution)/shard_map/ppermute | solution.py:457
  23.4 3.9 %collective-permute-start.5 = (bf16[2,208,128]{2,1,0:T(8,128)(2,1)S(1)}, bf16[2,208,128]{2,1,0:T(8,128)(2,1)S(1)}, u32[]{:S(2)}, u32[]{:S(2)}) collective-permute-start(bf16[2,208,128]{2,1,0:T(8,128)(2,1)S(1)} %slice.134), channel_id=1, source_target_pairs={{0,4},{4,0},{8,12},{12,8},{16,20},{20,16},{24,28},{28,24},{1,5},{5... | collective-permute-start | bytes 319496 | tf_op jit(solution)/shard_map/ppermute | solution.py:457
  27.5 18.7 %copy-start.3 = (f32[256,256]{1,0:T(8,128)S(1)}, f32[256,256]{1,0:T(8,128)}, u32[]{:S(2)}) copy-start(f32[256,256]{1,0:T(8,128)} %constant.32.clone.inverse_ref) | copy-start | bytes 786436
  27.5 18.7 %copy-start.4 = (f32[256,256]{1,0:T(8,128)S(1)}, f32[256,256]{1,0:T(8,128)}, u32[]{:S(2)}) copy-start(f32[256,256]{1,0:T(8,128)} %constant.31.clone.to_weights_ref) | copy-start | bytes 786436
  27.5 18.7 %copy-start.5 = (f32[256,256]{1,0:T(8,128)S(1)}, f32[256,256]{1,0:T(8,128)}, u32[]{:S(2)}) copy-start(f32[256,256]{1,0:T(8,128)} %constant.30.clone.forward_ref) | copy-start | bytes 786436
  27.5 4.6 %collective-permute-start.6 = (bf16[2,208,128]{2,1,0:T(8,128)(2,1)S(1)}, bf16[2,208,128]{2,1,0:T(8,128)(2,1)S(1)}, u32[]{:S(2)}, u32[]{:S(2)}) collective-permute-start(bf16[2,208,128]{2,1,0:T(8,128)(2,1)S(1)} %pad_maximum_fusion.7), channel_id=1, source_target_pairs={{0,16},{4,20},{8,24},{12,28},{16,0},{20,4},{24,8},{28,12},{1,17},{... | collective-permute-start | bytes 319496 | tf_op jit(solution)/shard_map/ppermute | solution.py:457
  32.3 6.8 %collective-permute-start.7 = (bf16[2,208,128]{2,1,0:T(8,128)(2,1)S(1)}, bf16[2,208,128]{2,1,0:T(8,128)(2,1)S(1)}, u32[]{:S(2)}, u32[]{:S(2)}) collective-permute-start(bf16[2,208,128]{2,1,0:T(8,128)(2,1)S(1)} %pad_maximum_fusion.8.own_ref), channel_id=1, source_target_pairs={{0,16},{4,20},{8,24},{12,28},{16,0},{20,4},{24,8},{28,12},{1,17},{... | collective-permute-start | bytes 319496 | tf_op jit(solution)/shard_map/ppermute | solution.py:457
  39.1 4.0 %collective-permute-start.8 = (bf16[2,208,128]{2,1,0:T(8,128)(2,1)S(1)}, bf16[2,208,128]{2,1,0:T(8,128)(2,1)S(1)}, u32[]{:S(2)}, u32[]{:S(2)}) collective-permute-start(bf16[2,208,128]{2,1,0:T(8,128)(2,1)S(1)} %pad_maximum_fusion.9), channel_id=1, source_target_pairs={{0,8},{4,12},{8,0},{12,4},{16,24},{20,28},{24,16},{28,20},{1,9},{5... | collective-permute-start | bytes 319496 | tf_op jit(solution)/shard_map/ppermute | solution.py:457
  41.0 5.1 %collective-permute-start.10 = (bf16[2,208,128]{2,1,0:T(8,128)(2,1)S(1)}, bf16[2,208,128]{2,1,0:T(8,128)(2,1)S(1)}, u32[]{:S(2)}, u32[]{:S(2)}) collective-permute-start(bf16[2,208,128]{2,1,0:T(8,128)(2,1)S(1)} %pad_maximum_fusion.10), channel_id=1, source_target_pairs={{0,4},{4,0},{8,12},{12,8},{16,20},{20,16},{24,28},{28,24},{1,5},{5... | collective-permute-start | bytes 319496 | tf_op jit(solution)/shard_map/ppermute | solution.py:457
  43.1 6.0 %collective-permute-start.9 = (bf16[4,208,128]{2,1,0:T(8,128)(2,1)S(1)}, bf16[4,208,128]{2,1,0:T(8,128)(2,1)S(1)}, u32[]{:S(2)}, u32[]{:S(2)}) collective-permute-start(bf16[4,208,128]{2,1,0:T(8,128)(2,1)S(1)} %pad_maximum_fusion.3.near_0), channel_id=1, source_target_pairs={{0,4},{4,0},{8,12},{12,8},{16,20},{20,16},{24,28},{28,24},{1,5},{5... | collective-permute-start | bytes 638984 | tf_op jit(solution)/shard_map/ppermute | solution.py:457
  46.1 4.8 %collective-permute-start.11 = (bf16[4,208,128]{2,1,0:T(8,128)(2,1)S(1)}, bf16[4,208,128]{2,1,0:T(8,128)(2,1)S(1)}, u32[]{:S(2)}, u32[]{:S(2)}) collective-permute-start(bf16[4,208,128]{2,1,0:T(8,128)(2,1)S(1)} %pad_maximum_fusion.4.near_1), channel_id=1, source_target_pairs={{0,8},{4,12},{8,0},{12,4},{16,24},{20,28},{24,16},{28,20},{1,9},{5... | collective-permute-start | bytes 638984 | tf_op jit(solution)/shard_map/ppermute | solution.py:457
  48.9 3.4 %copy-start.8 = (bf16[2,192,256]{2,1,0:T(8,128)(2,1)}, bf16[2,192,256]{2,1,0:T(8,128)(2,1)S(1)}, u32[]{:S(2)}) copy-start(bf16[2,192,256]{2,1,0:T(8,128)(2,1)S(1)} %get-tuple-element.17.edge_ref) | copy-start | bytes 589828
  49.0 3.4 %copy-start.10 = (f32[2,192,128]{2,1,0:T(8,128)}, f32[2,192,128]{2,1,0:T(8,128)S(1)}, u32[]{:S(2)}) copy-start(f32[2,192,128]{2,1,0:T(8,128)S(1)} %get-tuple-element.18.column_ref) | copy-start | bytes 589828
  54.9 15.5 %collective-permute-start.12 = (bf16[2,8,208,64]{2,3,1,0:T(8,128)(2,1)}, bf16[2,8,208,64]{2,3,1,0:T(8,128)(2,1)}, u32[]{:S(2)}, u32[]{:S(2)}) collective-permute-start(bf16[2,8,208,64]{2,3,1,0:T(8,128)(2,1)} %copy.13), channel_id=1, source_target_pairs={{0,1},{1,0},{2,3},{3,2},{4,5},{5,4},{6,7},{7,6},{8,9},{9,8},{10,11... | collective-permute-start | bytes 1277960 | tf_op jit(solution)/shard_map/ppermute | solution.py:494
  55.0 17.0 %collective-permute-start.13 = (bf16[2,8,208,64]{2,3,1,0:T(8,128)(2,1)S(1)}, bf16[2,8,208,64]{2,3,1,0:T(8,128)(2,1)}, u32[]{:S(2)}, u32[]{:S(2)}) collective-permute-start(bf16[2,8,208,64]{2,3,1,0:T(8,128)(2,1)S(1)} %copy.14), channel_id=1, source_target_pairs={{1,2},{2,1},{5,6},{6,5},{9,10},{10,9},{13,14},{14,13},{17,18},{18,... | collective-permute-start | bytes 1277960 | tf_op jit(solution)/shard_map/ppermute | solution.py:495
  67.8 2.6 %copy-start.6 = (bf16[2,192,8192]{2,1,0:T(8,128)(2,1)}, bf16[2,192,8192]{2,1,0:T(8,128)(2,1)S(1)}, u32[]{:S(2)}) copy-start(bf16[2,192,8192]{2,1,0:T(8,128)(2,1)S(1)} %lag_sums.1.lag_ref) | copy-start | bytes 18874372
  70.4 2.9 %copy-start.2 = (bf16[1024,256]{1,0:T(8,128)(2,1)S(1)}, bf16[1024,256]{1,0:T(8,128)(2,1)}, u32[]{:S(2)}) copy-start(bf16[1024,256]{1,0:T(8,128)(2,1)} %constant.33.clone.factor_ref) | copy-start | bytes 1572868
  73.4 2.8 %copy-start.7 = (bf16[2,192,8192]{2,1,0:T(8,128)(2,1)S(1)}, bf16[2,192,8192]{2,1,0:T(8,128)(2,1)}, u32[]{:S(2)}) copy-start(bf16[2,192,8192]{2,1,0:T(8,128)(2,1)} %copy-done.6) | copy-start | bytes 18874372
  76.2 0.9 copy-start.9
  (2 other events, 1.7 us)

commit v4 on v3

--- a/solution.py
+++ b/solution.py
@@ -213,39 +213,31 @@
     return middle * power, rest
 
 
-def lag_sums_kernel(form, own_ref, out_ref):
-    middle = jnp.concatenate([own_rows(form, own_ref, band)[0] for band in range(BANDS)], axis=0)
+def lag_sums_kernel(form, band, own_ref, out_ref):
+    middle = own_rows(form, own_ref, band)[0]
     lane = iota((1, 128), 1)
     row = iota((128, 128), 0)
     col = iota((128, 128), 1)
-
-    def several(step, turned):
-        for k in range(8):
-            d = step * 8 + k
-            further = pltpu.roll(turned, 127, 1)
-            partner = jnp.where(lane <= PERIOD - d, turned, further)
-            product = (middle * partner).astype(BF16)
-            keep = (row > col) & ((row <= PERIOD - d) == (col < PERIOD - d))
-            scale = jnp.where(d == 0, 1.0, 2.0).astype(F32)
-            keep = jnp.where(keep, scale, 0.0).astype(BF16)
-            sums = jnp.dot(product, keep, preferred_element_type=F32).astype(BF16)
-            put = pl.ds(pl.multiple_of(d * 128, 128), 128)
-            for band in range(BANDS):
-                out_ref[band, :, put] = sums[band * form.padded : (band + 1) * form.padded]
-            turned = further
-        return turned
-
-    lax.fori_loop(0, 8, several, middle)
-
-
-def lag_sums(form, own):
+    turned = middle
+    for d in range(64):
+        further = pltpu.roll(middle, PERIOD - d, 1)
+        partner = jnp.where(lane <= PERIOD - d, turned, further)
+        product = (middle * partner).astype(BF16)
+        keep = (row > col) & ((row <= PERIOD - d) == (col < PERIOD - d))
+        keep = jnp.where(keep, 2.0 if d else 1.0, 0.0).astype(BF16)
+        sums = jnp.dot(product, keep, preferred_element_type=F32)
+        out_ref[:, d * 128 : (d + 1) * 128] = sums.astype(BF16)
+        turned = further
+
+
+def lag_sums(form, band, own):
     return pl.pallas_call(
-        partial(lag_sums_kernel, form),
-        out_shape=jax.ShapeDtypeStruct((BANDS, form.padded, 64 * 128), BF16),
+        partial(lag_sums_kernel, form, band),
+        out_shape=jax.ShapeDtypeStruct((form.padded, 64 * 128), BF16),
         in_specs=[VMEM],
         out_specs=VMEM,
         compiler_params=params(12),
-        cost_estimate=cost(5 * 10**9, 6 * 10**6),
+        cost_estimate=cost(2 * 10**9, 3 * 10**6),
         name="lag_sums",
     )(own)
 
@@ -302,18 +294,43 @@
     )(own, jnp.asarray(FORWARD), jnp.asarray(TO_WEIGHTS), jnp.asarray(INVERSE))
 
 
-def mean_column(form, block):
+def mean_column(form, block, at=0):
     shape = (form.padded, form.height - form.tail)
     row, col = iota(shape, 0), iota(shape, 1) - form.first
     pick = (col == row // 64) | (col - 16 == row // 64)
     pick = jnp.where(pick, 1.0, 0.0).astype(BF16)
     spread = jnp.dot(pick, block[form.tail :], preferred_element_type=F32)
-    own = iota(spread.shape, 1) == lax.rem(iota(spread.shape, 0), 64)
+    own = iota(spread.shape, 1) == lax.rem(iota(spread.shape, 0), 64) + at
     return jnp.sum(jnp.where(own, spread, 0.0), axis=1, keepdims=True)
 
 
+def margins_kernel(form, owners, *refs):
+    halves, outs = refs[: 2 * BANDS], refs[2 * BANDS :]
+    odd = lax.rem(lax.axis_index("tm"), 2) == 1
+    is_low = iota((1, 128), 1) < LAG
+    half = owners // 2
+    for n in range(owners):
+        zero, one = (halves[2 * band + n // half][n % half].astype(F32) for band in range(BANDS))
+        early = jnp.where(is_low, zero, pltpu.roll(one, 64, 1)).astype(BF16)
+        late = jnp.where(is_low, pltpu.roll(zero, 64, 1), one).astype(BF16)
+        outs[0][n] = jnp.where(odd, early, late)
+        outs[1][n] = jnp.where(odd, late, early)
+
+
+def margins(form, owners, *halves):
+    return pl.pallas_call(
+        partial(margins_kernel, form, owners),
+        out_shape=[jax.ShapeDtypeStruct((owners, form.height, 128), BF16)] * 2,
+        in_specs=[VMEM] * len(halves),
+        out_specs=[VMEM] * 2,
+        compiler_params=params(8),
+        cost_estimate=cost(10**6, 2 * 10**6),
+        name="margins",
+    )(*halves)
+
+
 def coupling_kernel(
-    form, owners, orders, lag_ref, freq_ref, edge_ref, column_ref, near_0, far_0, near_1, far_1,
+    form, owners, orders, lag_0, lag_1, freq_ref, edge_ref, column_ref, near_0, far_0, near_1, far_1,
     first_ref, second_ref, factor_ref, out_ref, result, blocks, rows, near, far, near_turn, far_turn, change
 ):
     me = lax.axis_index("vert")
@@ -338,12 +355,16 @@
             block = blocks[band, p]
             middle = block[0 : form.padded].astype(F32)
             mean = mean_column(form, block)
-            one, two = first_ref[band, p], second_ref[band, p]
+            one, two = first_ref[p], second_ref[p]
             left, right = jnp.where(odd, one, two), jnp.where(odd, two, one)
-            margins = jnp.concatenate([left, right], axis=1)
-            around = margins[0 : form.padded].astype(F32)
-            shift_left = mean_column(form, left) - mean
-            shift_right = mean_column(form, right) - mean
+            shift_left = mean_column(form, left, band * 64) - mean
+            shift_right = mean_column(form, right, band * 64) - mean
+            left, right = (cells[0 : form.padded].astype(F32) for cells in (left, right))
+            if band == 0:
+                right = pltpu.roll(right, 64, 1)
+            else:
+                left = pltpu.roll(left, 64, 1)
+            around = jnp.where(is_left, left, right)
             around = (around + jnp.where(is_left, shift_left, shift_right)).astype(BF16).astype(F32)
             around = jnp.where(outside, 0.0, around)
             power, left_over = scales_of(middle)
@@ -363,9 +384,10 @@
     own_level = level_of(own_parcel)
     own_level = jnp.where(own_level < 3, own_level, -1)
 
-    def tile(step, carry):
-        band = lax.rem(step, BANDS)
-        first = pl.multiple_of((step // BANDS) * TILE, TILE)
+    def tile(band, start, height, step, carry):
+        lag_ref = (lag_0, lag_1)[band]
+        rows_of = slice(start, start + height)
+        first = pl.multiple_of(step * TILE, TILE)
         columns = rows[band, pl.ds(first, TILE), :].T
         narrow = columns[0:256].astype(BF16)
         near[0:64] = columns[128:192]
@@ -384,7 +406,7 @@
                 far_turn[0, 0:128] * far_turn[r, 16 * a : 16 * a + 128]
                 - near_turn[0, 0:128] * near_turn[r, 16 * a : 16 * a + 128]
             )
-        total = jnp.dot(lag_ref[band], change[...], preferred_element_type=F32)
+        total = jnp.dot(lag_ref[rows_of], change[...], preferred_element_type=F32)
         spectra = jnp.dot(factor_ref[0:512], narrow, preferred_element_type=F32) + jnp.dot(
             factor_ref[512:1024], narrow, preferred_element_type=F32
         )
@@ -396,13 +418,13 @@
         both = jnp.concatenate([real, imag], axis=0)
         big = both.astype(BF16)
         small = (both - big.astype(F32)).astype(BF16)
-        weights = freq_ref[band]
+        weights = freq_ref[band, rows_of]
         total += jnp.dot(weights[:, 0:256], big, preferred_element_type=F32)
         total += jnp.dot(weights[:, 256:512], big, preferred_element_type=F32)
         total += jnp.dot(weights[:, 0:256], small, preferred_element_type=F32)
-        mixed = jnp.dot(edge_ref[band], narrow, preferred_element_type=F32)
+        mixed = jnp.dot(edge_ref[band, rows_of], narrow, preferred_element_type=F32)
         mu, other_factor = columns[256:257], columns[257:258]
-        factors = column_ref[band]
+        factors = column_ref[band, rows_of]
         edge_sum, own_factor = factors[:, 0:1], factors[:, 1:2]
         total += mu * (mu * edge_sum - 2.0 * mixed)
         column = iota((1, TILE), 1) + first
@@ -410,18 +432,27 @@
         gap = (column >= SPLIT) & (column < GROUP)
         other_level = jnp.where(gap, 3, level_of(parcel))
         scaled = total * own_factor * other_factor
-        result[band, :, pl.ds(first, TILE)] = jnp.where(own_level == other_level, scaled, 0.0)
+        same = own_level[rows_of] == other_level
+        result[band, rows_of, pl.ds(first, TILE)] = jnp.where(same, scaled, 0.0)
         return carry
 
     begin = me * form.rows
     end = jnp.minimum(begin + form.rows, SPLIT + P3)
     tiles = result.shape[2] // TILE
-    lax.fori_loop(
-        jnp.where(begin < SPLIT, 0, GROUP // TILE) * BANDS,
-        jnp.where(end <= SPLIT, GROUP // TILE, tiles) * BANDS,
-        tile,
-        0,
-    )
+    fold = GROUP // TILE
+    coarse, fine = begin < SPLIT, end > SPLIT
+    for band in range(BANDS):
+        run = lambda lo, hi, start, height: lax.fori_loop(
+            lo, hi, partial(tile, band, start, height), 0
+        )
+        low, high = jnp.where(coarse, 0, fold), jnp.where(fine, tiles, fold)
+        cut = SPLIT % form.rows
+        if form.padded - 128 <= cut <= 128:
+            mixed = coarse & fine
+            run(0, jnp.where(mixed, fold, 0), 0, 128)
+            run(jnp.where(mixed, fold, tiles), tiles, form.padded - 128, 128)
+            low = jnp.where(mixed, high, low)
+        run(low, high, 0, form.padded)
     total = owners * form.rows
     for band in range(BANDS):
         out_ref[:, band, 0:SPLIT] = result[band, 0 : form.rows, 0:SPLIT]
@@ -447,7 +478,7 @@
             pltpu.VMEM((16, 176, TILE), BF16),
             pltpu.VMEM((64 * 128, TILE), BF16),
         ],
-        compiler_params=params(40),
+        compiler_params=params(24),
         cost_estimate=cost(16 * 10**9, 10**7),
         name="coupling",
     )(*operands)
@@ -463,8 +494,6 @@
     form = Rows((P1 + P2 + P3 + owners - 1) // owners)
     bits = [1 << k for k in range(owners.bit_length() - 1)]
     orders = [bits, [bits[1], bits[0], *bits[2:]]]
-    window = lax.axis_index("tm")
-    odd = lax.rem(window, 2) == 1
     meet = [[p for i in range(k, windows - 1, 2) for p in ((i, i + 1), (i + 1, i))] for k in range(2)]
     first, second = (lax.ppermute(source, "tm", pairs) for pairs in meet)
     taps = jnp.pad(band_taps.astype(F32).reshape(2 * BANDS, 1, TAPS), ((0, 0), (0, 0), (0, 256 - TAPS)))
@@ -479,22 +508,22 @@
     kept, sent = (jnp.concatenate([parts[b][k] for b in range(BANDS)], axis=0) for k in range(2))
     own = added(form, kept, swap(sent, owners, bits[-1]))
 
-    lag = lag_sums(form, own)
+    lag = [lag_sums(form, band, own) for band in range(BANDS)]
     freq, edge, column = spectra(form, own)
     arrived = swap(own, owners, bits[-1])
     held = [jnp.stack([own[b], arrived[b]]) for b in range(BANDS)]
+    held, lag[0] = lax.optimization_barrier((held, lag[0]))
     halves = [None, None]
     for step in range(len(bits) - 2, -1, -1):
         arrived = [swap(held[b], owners, orders[b][step]) for b in range(BANDS)]
         halves = [(held[b], arrived[b]) for b in range(BANDS)]
         if step:
             held = [jnp.concatenate(pair, axis=0) for pair in halves]
-    whole = jnp.stack([jnp.concatenate(pair, axis=0) for pair in halves])
-    early, late = whole[..., :LAG], whole[..., t_dev - LAG :]
-    first = lax.ppermute(jnp.where(odd, early, late), "tm", meet[0])
-    second = lax.ppermute(jnp.where(odd, late, early), "tm", meet[1])
+    first, second = margins(form, owners, *halves[0], *halves[1])
+    first = lax.ppermute(first, "tm", meet[0])
+    second = lax.ppermute(second, "tm", meet[1])
     turned = [order[::-1] for order in orders]
-    done = coupling(form, owners, turned, lag, freq, edge, column, *halves[0], *halves[1], first, second)
+    done = coupling(form, owners, turned, *lag, freq, edge, column, *halves[0], *halves[1], first, second)
     return done.transpose(1, 0, 2)[None]
 
 

time: 106 us -> 89.3 us (0.84)
  local copies, waits for them, and re-layouts: 16 us -> 3.27 us
  Pallas kernels: 40.7 us -> 36.9 us
  other arithmetic: 2.06 us -> 0.53 us
  waiting for transfers between devices: 24.5 us -> 25.6 us
    unnamed x24 -> x14, local copies, waits for them, and re-layouts: 8.99 us -> 1.74 us
    ppermute x2 -> x0, local copies, waits for them, and re-layouts: 2.93 us -> none  [the longest x1 1.49 us: local(): first = lax.ppermute(jnp.where(odd, early, late), 'tm', meet[0])]
    select_n x2 -> x0, local copies, waits for them, and re-layouts: 2.61 us -> none  [the longest x1 1.47 us: local(): second = lax.ppermute(jnp.where(odd, late, early), 'tm', meet[1])]
    pallas_call x1, Pallas kernels: 27.1 us -> 25.1 us  [coupling(): pl.pallas_call(partial(coupling_kernel, form, owners, orders), out_shape=...]
    pallas_call x1 -> x3, Pallas kernels: 6.09 us -> 4.26 us  [the longest x2 3.87 us: lag_sums(): pl.pallas_call(partial(lag_sums_kernel, form, band), out_shape=jax.ShapeD...]
    select_n x1 -> x0, other arithmetic: 1.4 us -> none  [local(): second = lax.ppermute(jnp.where(odd, late, early), 'tm', meet[1])]
  transfers between devices with their start and end apart: 14 -> 14, of which waited for: 11 -> 11; matrix products, arithmetic and copies ran while one was open for 3% -> 2% of each run, Pallas kernels for 8% -> 7%
where the time goes in v4:
time: 89.3 us; the launch traced here: 89.1 us
  Pallas kernels  36.9 us (41%)
  waiting for transfers between devices  25.6 us (29%)
  starting transfers between devices  22.5 us (25%)
  local copies, waits for them, and re-layouts  3.27 us (4%)
    pallas_call x1, Pallas kernels, coupling(): pl.pallas_call(partial(coupling_kernel, form, owners, orders), out_shape=...  25.1 us
    ppermute x10, waiting for transfers between devices, swap(): return lax.ppermute(cells, 'vert', [(i, i ^ bit) for i in range(owners)])  20.5 us
    ppermute x10, starting transfers between devices, swap(): return lax.ppermute(cells, 'vert', [(i, i ^ bit) for i in range(owners)])  11.1 us
    ppermute x1, starting transfers between devices, local(): second = lax.ppermute(second, 'tm', meet[1])  7.65 us
    pallas_call x1, Pallas kernels, front(): pl.pallas_call(partial(front_kernel, form, owners, orders), out_shape=[sh...  4.78 us
    ppermute x2, waiting for transfers between devices, local(): first, second = (lax.ppermute(source, 'tm', pairs) for pairs in meet)  4.2 us
    pallas_call x2, Pallas kernels, lag_sums(): pl.pallas_call(partial(lag_sums_kernel, form, band), out_shape=jax.ShapeD...  3.87 us
    ppermute x2, starting transfers between devices, local(): first, second = (lax.ppermute(source, 'tm', pairs) for pairs in meet)  3.7 us
  transfers between devices with their start and end apart: 14, of which 11 were waited for; matrix products, arithmetic and copies ran while one was open for 2% of the time, Pallas kernels for 7%

profile of v4, /device:TPU:9, one launch (start us, length us, event | category | flops | bytes accessed | tf_op | source)
XLA Modules:
  0.0 89.1 jit_solution(4736959356228343360)
XLA Ops:
  0.0 0.7 collective-permute-start
  0.7 3.0 %collective-permute-start.1 = (bf16[1280,128]{1,0:T(8,128)(2,1)}, bf16[1280,128]{1,0:T(8,128)(2,1)S(1)}, u32[]{:S(2)}, u32[]{:S(2)}) collective-permute-start(bf16[1280,128]{1,0:T(8,128)(2,1)} %middle_ref.1), channel_id=1, source_target_pairs={{1,2},{2,1},{5,6},{6,5},{9,10},{10,9},{13,14},{14,13},{17,18},{18,... | collective-permute-start | bytes 983048 | tf_op jit(solution)/shard_map/ppermute | solution.py:498
  3.7 0.7 copy.10
  4.4 0.7 copy.9
  5.1 4.2 %collective-permute-done.1.second_ref = bf16[1280,128]{1,0:T(8,128)(2,1)S(1)} collective-permute-done((bf16[1280,128]{1,0:T(8,128)(2,1)}, bf16[1280,128]{1,0:T(8,128)(2,1)S(1)}, u32[]{:S(2)}, u32[]{:S(2)}) %collective-permute-start.1) | collective-permute-done | bytes 327712 | tf_op jit(solution)/shard_map/ppermute | solution.py:498
  9.3 1.0 %copy-done = bf16[1280,128]{1,0:T(8,128)(2,1)S(1)} copy-done((bf16[1280,128]{1,0:T(8,128)(2,1)S(1)}, bf16[1280,128]{1,0:T(8,128)(2,1)}, u32[]{:S(2)}) %copy-start) | copy-done | bytes 327704
  10.2 0.7 copy-done.1
  11.0 4.8 %envelope_sums.1 = (bf16[4,208,128]{2,1,0:T(8,128)(2,1)S(1)}, bf16[4,208,128]{2,1,0:T(8,128)(2,1)S(1)}, bf16[4,208,128]{2,1,0:T(8,128)(2,1)S(1)}, bf16[4,208,128]{2,1,0:T(8,128)(2,1)S(1)}) custom-call(bf16[1280,128]{1,0:T(8,128)(2,1)S(1)} %copy-done, bf16[1280,128]{1,0:T(8,128)(2,1)S(1)} %collective-permute-done.first_ref, ...), custom_call_target="tpu_custom_call" | custom-call | flops 3000000000 | bytes 2000000 | tf_op jit(solution)/shard_map/envelope_sums/pallas_call | solution.py:176
  15.8 1.3 %collective-permute-start.2 = (bf16[4,208,128]{2,1,0:T(8,128)(2,1)S(1)}, bf16[4,208,128]{2,1,0:T(8,128)(2,1)S(1)}, u32[]{:S(2)}, u32[]{:S(2)}) collective-permute-start(bf16[4,208,128]{2,1,0:T(8,128)(2,1)S(1)} %get-tuple-element.18), channel_id=1, source_target_pairs={{0,4},{4,0},{8,12},{12,8},{16,20},{20,16},{24,28},{28,24},{1,5},{5... | collective-permute-start | bytes 638984 | tf_op jit(solution)/shard_map/ppermute | solution.py:488
  17.2 3.8 %collective-permute-done.2 = bf16[4,208,128]{2,1,0:T(8,128)(2,1)S(1)} collective-permute-done((bf16[4,208,128]{2,1,0:T(8,128)(2,1)S(1)}, bf16[4,208,128]{2,1,0:T(8,128)(2,1)S(1)}, u32[]{:S(2)}, u32[]{:S(2)}) %collective-permute-start.2) | collective-permute-done | bytes 213024 | tf_op jit(solution)/shard_map/ppermute | solution.py:488
  21.1 1.8 %collective-permute-done.4 = bf16[4,208,128]{2,1,0:T(8,128)(2,1)S(1)} collective-permute-done((bf16[4,208,128]{2,1,0:T(8,128)(2,1)S(1)}, bf16[4,208,128]{2,1,0:T(8,128)(2,1)S(1)}, u32[]{:S(2)}, u32[]{:S(2)}) %collective-permute-start.4) | collective-permute-done | bytes 213024 | tf_op jit(solution)/shard_map/ppermute | solution.py:488
  23.7 3.0 %collective-permute-done.3 = bf16[2,208,128]{2,1,0:T(8,128)(2,1)S(1)} collective-permute-done((bf16[2,208,128]{2,1,0:T(8,128)(2,1)S(1)}, bf16[2,208,128]{2,1,0:T(8,128)(2,1)S(1)}, u32[]{:S(2)}, u32[]{:S(2)}) %collective-permute-start.3) | collective-permute-done | bytes 106528 | tf_op jit(solution)/shard_map/ppermute | solution.py:488
  27.5 2.4 %collective-permute-start.6 = (bf16[2,208,128]{2,1,0:T(8,128)(2,1)S(1)}, bf16[2,208,128]{2,1,0:T(8,128)(2,1)S(1)}, u32[]{:S(2)}, u32[]{:S(2)}) collective-permute-start(bf16[2,208,128]{2,1,0:T(8,128)(2,1)S(1)} %pad_maximum_fusion.4), channel_id=1, source_target_pairs={{0,16},{4,20},{8,24},{12,28},{16,0},{20,4},{24,8},{28,12},{1,17},{... | collective-permute-start | bytes 319496 | tf_op jit(solution)/shard_map/ppermute | solution.py:488
  29.9 2.2 %collective-permute-done.6 = bf16[2,208,128]{2,1,0:T(8,128)(2,1)S(1)} collective-permute-done((bf16[2,208,128]{2,1,0:T(8,128)(2,1)S(1)}, bf16[2,208,128]{2,1,0:T(8,128)(2,1)S(1)}, u32[]{:S(2)}, u32[]{:S(2)}) %collective-permute-start.6) | collective-permute-done | bytes 106528 | tf_op jit(solution)/shard_map/ppermute | solution.py:488
  32.3 4.6 %collective-permute-start.7 = (bf16[2,208,128]{2,1,0:T(8,128)(2,1)S(1)}, bf16[2,208,128]{2,1,0:T(8,128)(2,1)S(1)}, u32[]{:S(2)}, u32[]{:S(2)}) collective-permute-start(bf16[2,208,128]{2,1,0:T(8,128)(2,1)S(1)} %pad_maximum_fusion.5.own_ref), channel_id=1, source_target_pairs={{0,16},{4,20},{8,24},{12,28},{16,0},{20,4},{24,8},{28,12},{1,17},{... | collective-permute-start | bytes 319496 | tf_op jit(solution)/shard_map/ppermute | solution.py:488
  36.8 1.9 %lag_sums.2.lag_0 = bf16[192,8192]{1,0:T(8,128)(2,1)S(1)} custom-call(bf16[2,208,128]{2,1,0:T(8,128)(2,1)S(1)} %pad_maximum_fusion.5.own_ref), custom_call_target="tpu_custom_call" | custom-call | flops 2000000000 | bytes 3000000 | tf_op jit(solution)/shard_map/lag_sums/pallas_call | solution.py:234
  39.1 1.9 %collective-permute-start.8 = (bf16[2,208,128]{2,1,0:T(8,128)(2,1)S(1)}, bf16[2,208,128]{2,1,0:T(8,128)(2,1)S(1)}, u32[]{:S(2)}, u32[]{:S(2)}) collective-permute-start(bf16[2,208,128]{2,1,0:T(8,128)(2,1)S(1)} %pad_maximum_fusion.6), channel_id=1, source_target_pairs={{0,8},{4,12},{8,0},{12,4},{16,24},{20,28},{24,16},{28,20},{1,9},{5... | collective-permute-start | bytes 319496 | tf_op jit(solution)/shard_map/ppermute | solution.py:488
  41.1 3.5 %collective-permute-done.10 = bf16[2,208,128]{2,1,0:T(8,128)(2,1)S(1)} collective-permute-done((bf16[2,208,128]{2,1,0:T(8,128)(2,1)S(1)}, bf16[2,208,128]{2,1,0:T(8,128)(2,1)S(1)}, u32[]{:S(2)}, u32[]{:S(2)}) %collective-permute-start.10) | collective-permute-done | bytes 106528 | tf_op jit(solution)/shard_map/ppermute | solution.py:488
  44.8 5.2 %collective-permute-done.11.refs_3_.far_1 = bf16[4,208,128]{2,1,0:T(8,128)(2,1)S(1)} collective-permute-done((bf16[4,208,128]{2,1,0:T(8,128)(2,1)S(1)}, bf16[4,208,128]{2,1,0:T(8,128)(2,1)S(1)}, u32[]{:S(2)}, u32[]{:S(2)}) %collective-permute-start.11) | collective-permute-done | bytes 213024 | tf_op jit(solution)/shard_map/ppermute | solution.py:488
  50.7 7.6 %collective-permute-start.13 = (bf16[8,208,128]{2,1,0:T(8,128)(2,1)S(1)}, bf16[8,208,128]{2,1,0:T(8,128)(2,1)S(1)}, u32[]{:S(2)}, u32[]{:S(2)}) collective-permute-start(bf16[8,208,128]{2,1,0:T(8,128)(2,1)S(1)} %get-tuple-element.28), channel_id=1, source_target_pairs={{1,2},{2,1},{5,6},{6,5},{9,10},{10,9},{13,14},{14,13},{17,18},{18,... | collective-permute-start | bytes 1277960 | tf_op jit(solution)/shard_map/ppermute | solution.py:524
  58.3 1.9 %lag_sums.3.lag_1 = bf16[192,8192]{1,0:T(8,128)(2,1)S(1)} custom-call(bf16[2,208,128]{2,1,0:T(8,128)(2,1)S(1)} %pad_maximum_fusion.5.own_ref), custom_call_target="tpu_custom_call" | custom-call | flops 2000000000 | bytes 3000000 | tf_op jit(solution)/shard_map/lag_sums/pallas_call | solution.py:234
  60.3 2.7 %row_spectra.1 = (bf16[2,192,512]{2,1,0:T(8,128)(2,1)S(1)}, bf16[2,192,256]{2,1,0:T(8,128)(2,1)S(1)}, f32[2,192,128]{2,1,0:T(8,128)S(1)}) custom-call(bf16[2,208,128]{2,1,0:T(8,128)(2,1)S(1)} %pad_maximum_fusion.5.own_ref, f32[256,256]{1,0:T(8,128)S(1)} %copy-done.5, f32[256,256]{1,0:T(8,128)S(1)} %copy-done.4, f32[256,256]{1,0:T(8,128)S(1)} %copy-done.3), custom_call_target="tpu_custom_call" | custom-call | flops 2000000000 | bytes 2000000 | tf_op jit(solution)/shard_map/row_spectra/pallas_call | solution.py:286
  63.0 0.9 %collective-permute-done.13.second_ref = bf16[8,208,128]{2,1,0:T(8,128)(2,1)S(1)} collective-permute-done((bf16[8,208,128]{2,1,0:T(8,128)(2,1)S(1)}, bf16[8,208,128]{2,1,0:T(8,128)(2,1)S(1)}, u32[]{:S(2)}, u32[]{:S(2)}) %collective-permute-start.13) | collective-permute-done | bytes 426016 | tf_op jit(solution)/shard_map/ppermute | solution.py:524
  63.9 25.1 %coupling.1 = f32[188,2,1504]{2,1,0:T(2,128)} custom-call(bf16[192,8192]{1,0:T(8,128)(2,1)S(1)} %lag_sums.2.lag_0, bf16[192,8192]{1,0:T(8,128)(2,1)S(1)} %lag_sums.3.lag_1, bf16[2,192,512]{2,1,0:T(8,128)(2,1)S(1)} %get-tuple-element.22.freq_ref, bf16[2,192,256]{2,1,0:T(8,128)(2,1)S(1)} %get-tuple-element.23.edge_ref, ...), custom_call_target="tpu_custom_call" | custom-call | flops 16000000000 | bytes 10000000 | tf_op jit(solution)/shard_map/coupling/pallas_call | solution.py:466
  (57 shorter events, 3.1 us)
Async XLA Ops:
  0.0 5.1 %collective-permute-start = (bf16[1280,128]{1,0:T(8,128)(2,1)}, bf16[1280,128]{1,0:T(8,128)(2,1)S(1)}, u32[]{:S(2)}, u32[]{:S(2)}) collective-permute-start(bf16[1280,128]{1,0:T(8,128)(2,1)} %middle_ref.1), channel_id=1, source_target_pairs={{0,1},{1,0},{2,3},{3,2},{4,5},{5,4},{6,7},{7,6},{8,9},{9,8},{10,11... | collective-permute-start | bytes 983048 | tf_op jit(solution)/shard_map/ppermute | solution.py:498
  0.7 8.6 %collective-permute-start.1 = (bf16[1280,128]{1,0:T(8,128)(2,1)}, bf16[1280,128]{1,0:T(8,128)(2,1)S(1)}, u32[]{:S(2)}, u32[]{:S(2)}) collective-permute-start(bf16[1280,128]{1,0:T(8,128)(2,1)} %middle_ref.1), channel_id=1, source_target_pairs={{1,2},{2,1},{5,6},{6,5},{9,10},{10,9},{13,14},{14,13},{17,18},{18,... | collective-permute-start | bytes 983048 | tf_op jit(solution)/shard_map/ppermute | solution.py:498
  9.3 1.0 %copy-start = (bf16[1280,128]{1,0:T(8,128)(2,1)S(1)}, bf16[1280,128]{1,0:T(8,128)(2,1)}, u32[]{:S(2)}) copy-start(bf16[1280,128]{1,0:T(8,128)(2,1)} %middle_ref.1) | copy-start | bytes 983044
  10.2 0.7 copy-start.1
  15.8 5.2 %collective-permute-start.2 = (bf16[4,208,128]{2,1,0:T(8,128)(2,1)S(1)}, bf16[4,208,128]{2,1,0:T(8,128)(2,1)S(1)}, u32[]{:S(2)}, u32[]{:S(2)}) collective-permute-start(bf16[4,208,128]{2,1,0:T(8,128)(2,1)S(1)} %get-tuple-element.18), channel_id=1, source_target_pairs={{0,4},{4,0},{8,12},{12,8},{16,20},{20,16},{24,28},{28,24},{1,5},{5... | collective-permute-start | bytes 638984 | tf_op jit(solution)/shard_map/ppermute | solution.py:488
  17.0 5.8 %collective-permute-start.4 = (bf16[4,208,128]{2,1,0:T(8,128)(2,1)S(1)}, bf16[4,208,128]{2,1,0:T(8,128)(2,1)S(1)}, u32[]{:S(2)}, u32[]{:S(2)}) collective-permute-start(bf16[4,208,128]{2,1,0:T(8,128)(2,1)S(1)} %get-tuple-element.20), channel_id=1, source_target_pairs={{0,8},{4,12},{8,0},{12,4},{16,24},{20,28},{24,16},{28,20},{1,9},{5... | collective-permute-start | bytes 638984 | tf_op jit(solution)/shard_map/ppermute | solution.py:488
  23.1 3.6 %collective-permute-start.3 = (bf16[2,208,128]{2,1,0:T(8,128)(2,1)S(1)}, bf16[2,208,128]{2,1,0:T(8,128)(2,1)S(1)}, u32[]{:S(2)}, u32[]{:S(2)}) collective-permute-start(bf16[2,208,128]{2,1,0:T(8,128)(2,1)S(1)} %slice.117), channel_id=1, source_target_pairs={{0,8},{4,12},{8,0},{12,4},{16,24},{20,28},{24,16},{28,20},{1,9},{5... | collective-permute-start | bytes 319496 | tf_op jit(solution)/shard_map/ppermute | solution.py:488
  23.4 3.9 %collective-permute-start.5 = (bf16[2,208,128]{2,1,0:T(8,128)(2,1)S(1)}, bf16[2,208,128]{2,1,0:T(8,128)(2,1)S(1)}, u32[]{:S(2)}, u32[]{:S(2)}) collective-permute-start(bf16[2,208,128]{2,1,0:T(8,128)(2,1)S(1)} %slice.126), channel_id=1, source_target_pairs={{0,4},{4,0},{8,12},{12,8},{16,20},{20,16},{24,28},{28,24},{1,5},{5... | collective-permute-start | bytes 319496 | tf_op jit(solution)/shard_map/ppermute | solution.py:488
  27.5 4.6 %collective-permute-start.6 = (bf16[2,208,128]{2,1,0:T(8,128)(2,1)S(1)}, bf16[2,208,128]{2,1,0:T(8,128)(2,1)S(1)}, u32[]{:S(2)}, u32[]{:S(2)}) collective-permute-start(bf16[2,208,128]{2,1,0:T(8,128)(2,1)S(1)} %pad_maximum_fusion.4), channel_id=1, source_target_pairs={{0,16},{4,20},{8,24},{12,28},{16,0},{20,4},{24,8},{28,12},{1,17},{... | collective-permute-start | bytes 319496 | tf_op jit(solution)/shard_map/ppermute | solution.py:488
  32.3 6.8 %collective-permute-start.7 = (bf16[2,208,128]{2,1,0:T(8,128)(2,1)S(1)}, bf16[2,208,128]{2,1,0:T(8,128)(2,1)S(1)}, u32[]{:S(2)}, u32[]{:S(2)}) collective-permute-start(bf16[2,208,128]{2,1,0:T(8,128)(2,1)S(1)} %pad_maximum_fusion.5.own_ref), channel_id=1, source_target_pairs={{0,16},{4,20},{8,24},{12,28},{16,0},{20,4},{24,8},{28,12},{1,17},{... | collective-permute-start | bytes 319496 | tf_op jit(solution)/shard_map/ppermute | solution.py:488
  39.1 5.6 %collective-permute-start.8 = (bf16[2,208,128]{2,1,0:T(8,128)(2,1)S(1)}, bf16[2,208,128]{2,1,0:T(8,128)(2,1)S(1)}, u32[]{:S(2)}, u32[]{:S(2)}) collective-permute-start(bf16[2,208,128]{2,1,0:T(8,128)(2,1)S(1)} %pad_maximum_fusion.6), channel_id=1, source_target_pairs={{0,8},{4,12},{8,0},{12,4},{16,24},{20,28},{24,16},{28,20},{1,9},{5... | collective-permute-start | bytes 319496 | tf_op jit(solution)/shard_map/ppermute | solution.py:488
  41.0 3.6 %collective-permute-start.10 = (bf16[2,208,128]{2,1,0:T(8,128)(2,1)S(1)}, bf16[2,208,128]{2,1,0:T(8,128)(2,1)S(1)}, u32[]{:S(2)}, u32[]{:S(2)}) collective-permute-start(bf16[2,208,128]{2,1,0:T(8,128)(2,1)S(1)} %pad_maximum_fusion.7), channel_id=1, source_target_pairs={{0,4},{4,0},{8,12},{12,8},{16,20},{20,16},{24,28},{28,24},{1,5},{5... | collective-permute-start | bytes 319496 | tf_op jit(solution)/shard_map/ppermute | solution.py:488
  44.6 5.4 %collective-permute-start.11 = (bf16[4,208,128]{2,1,0:T(8,128)(2,1)S(1)}, bf16[4,208,128]{2,1,0:T(8,128)(2,1)S(1)}, u32[]{:S(2)}, u32[]{:S(2)}) collective-permute-start(bf16[4,208,128]{2,1,0:T(8,128)(2,1)S(1)} %constant_dynamic-update-slice_fusion.2.refs_2_.near_1), channel_id=1, source_target_pairs={{0,8},{4,12},{8,0},{12,4},{16,24},{20,28},{24,16},{28,20},{1,9},{5... | collective-permute-start | bytes 638984 | tf_op jit(solution)/shard_map/ppermute | solution.py:488
  44.8 5.4 %collective-permute-start.9 = (bf16[4,208,128]{2,1,0:T(8,128)(2,1)S(1)}, bf16[4,208,128]{2,1,0:T(8,128)(2,1)S(1)}, u32[]{:S(2)}, u32[]{:S(2)}) collective-permute-start(bf16[4,208,128]{2,1,0:T(8,128)(2,1)S(1)} %constant_dynamic-update-slice_fusion.refs_0_.near_0), channel_id=1, source_target_pairs={{0,4},{4,0},{8,12},{12,8},{16,20},{20,16},{24,28},{28,24},{1,5},{5... | collective-permute-start | bytes 638984 | tf_op jit(solution)/shard_map/ppermute | solution.py:488
  50.5 12.5 %collective-permute-start.12 = (bf16[8,208,128]{2,1,0:T(8,128)(2,1)S(1)}, bf16[8,208,128]{2,1,0:T(8,128)(2,1)S(1)}, u32[]{:S(2)}, u32[]{:S(2)}) collective-permute-start(bf16[8,208,128]{2,1,0:T(8,128)(2,1)S(1)} %get-tuple-element.27), channel_id=1, source_target_pairs={{0,1},{1,0},{2,3},{3,2},{4,5},{5,4},{6,7},{7,6},{8,9},{9,8},{10,11... | collective-permute-start | bytes 1277960 | tf_op jit(solution)/shard_map/ppermute | solution.py:523
  50.6 9.6 %copy-start.3 = (f32[256,256]{1,0:T(8,128)S(1)}, f32[256,256]{1,0:T(8,128)}, u32[]{:S(2)}) copy-start(f32[256,256]{1,0:T(8,128)} %constant.22.clone.inverse_ref) | copy-start | bytes 786436
  50.6 9.6 %copy-start.4 = (f32[256,256]{1,0:T(8,128)S(1)}, f32[256,256]{1,0:T(8,128)}, u32[]{:S(2)}) copy-start(f32[256,256]{1,0:T(8,128)} %constant.21.clone.to_weights_ref) | copy-start | bytes 786436
  50.6 9.6 %copy-start.5 = (f32[256,256]{1,0:T(8,128)S(1)}, f32[256,256]{1,0:T(8,128)}, u32[]{:S(2)}) copy-start(f32[256,256]{1,0:T(8,128)} %constant.20.clone.forward_ref) | copy-start | bytes 786436
  50.7 13.3 %collective-permute-start.13 = (bf16[8,208,128]{2,1,0:T(8,128)(2,1)S(1)}, bf16[8,208,128]{2,1,0:T(8,128)(2,1)S(1)}, u32[]{:S(2)}, u32[]{:S(2)}) collective-permute-start(bf16[8,208,128]{2,1,0:T(8,128)(2,1)S(1)} %get-tuple-element.28), channel_id=1, source_target_pairs={{1,2},{2,1},{5,6},{6,5},{9,10},{10,9},{13,14},{14,13},{17,18},{18,... | collective-permute-start | bytes 1277960 | tf_op jit(solution)/shard_map/ppermute | solution.py:524
  60.3 3.6 %copy-start.2 = (bf16[1024,256]{1,0:T(8,128)(2,1)S(1)}, bf16[1024,256]{1,0:T(8,128)(2,1)}, u32[]{:S(2)}) copy-start(bf16[1024,256]{1,0:T(8,128)(2,1)} %constant.23.clone.factor_ref) | copy-start | bytes 1572868

commit v5 on v4

--- a/solution.py
+++ b/solution.py
@@ -22,6 +22,7 @@
 GROUP = (SPLIT + 127) // 128 * 128
 TILE = 256
 PERIOD = 127
+LAGS = 64 * 128
 HIGH = lax.Precision.HIGHEST
 BF16 = jnp.bfloat16
 F32 = jnp.float32
@@ -50,7 +51,7 @@
     high = factors.astype(np.float32).astype(jnp.bfloat16)
     low = (factors - high.astype(np.float64)).astype(np.float32).astype(jnp.bfloat16)
     f32 = lambda cells: cells.astype(np.float32)
-    return f32(forward), f32(to_weights), f32(inverse), np.concatenate([high, low], axis=0)
+    return f32(forward), f32(to_weights), f32(inverse), np.concatenate([high, low], axis=1)
 
 
 FORWARD, TO_WEIGHTS, INVERSE, FACTORS = fourier_constants()
@@ -96,22 +97,40 @@
     return tail[...].astype(BF16)
 
 
-def front_kernel(
-    form, owners, orders, middle_ref, first_ref, second_ref, taps_ref, smooth_ref, ids_ref, *rest
-):
+def prepare_kernel(form, owners, middle_ref, taps_ref, smooth_ref, ids_ref, source_ref, filter_ref, smoother_ref, hits_ref):
+    me = lax.axis_index("vert")
+    source_ref[...] = middle_ref[...]
+    for k in range(2 * BANDS):
+        taps = jnp.broadcast_to(taps_ref[k], (256, 256))
+        filter_ref[k] = pltpu.roll(taps, 192, 1, stride=1, stride_axis=0).astype(BF16)
+    for k in range(BANDS):
+        taps = jnp.broadcast_to(smooth_ref[k], (128, 256))
+        smoother_ref[k] = pltpu.roll(taps, 0, 1, stride=1, stride_axis=0).astype(BF16)
+    offsets = (0, P1, SPLIT)
+    ids = [ids_ref[r : r + 1] + offsets[r] for r in range(3)]
+    for k in range(owners):
+        wanted = iota((form.padded, 1), 0) + (me ^ k) * form.rows
+        hits = (wanted == ids[0]) | (wanted == ids[1]) | (wanted == ids[2])
+        hits_ref[k] = jnp.where(hits, 1.0, 0.0).astype(BF16)
+
+
+def prepare(form, owners, source, taps, smooths, ids):
+    shapes = [source.shape, (2 * BANDS, 256, 256), (BANDS, 128, 256), (owners, form.padded, source.shape[0])]
+    return pl.pallas_call(
+        partial(prepare_kernel, form, owners),
+        out_shape=[jax.ShapeDtypeStruct(shape, BF16) for shape in shapes],
+        in_specs=[VMEM] * 4,
+        out_specs=[VMEM] * 4,
+        compiler_params=params(16),
+        cost_estimate=cost(2 * 10**9, 5 * 10**6),
+        name="prepare",
+    )(source, taps, smooths, ids)
+
+
+def front_kernel(form, owners, orders, first_ref, second_ref, middle_ref, filter_ref, smoother_ref, hits_ref, *rest):
     outs, (env, tail) = rest[: 2 * BANDS], rest[2 * BANDS :]
-    me = lax.axis_index("vert")
-    shape = (256, 256)
-    filters = [
-        pltpu.roll(jnp.broadcast_to(taps_ref[k], shape), 192, 1, stride=1, stride_axis=0).astype(BF16)
-        for k in range(2 * BANDS)
-    ]
-    smooths = [
-        pltpu.roll(
-            jnp.broadcast_to(smooth_ref[k], (128, 256)), 0, 1, stride=1, stride_axis=0
-        ).astype(BF16)
-        for k in range(BANDS)
-    ]
+    filters = [filter_ref[k] for k in range(2 * BANDS)]
+    smooths = [smoother_ref[k] for k in range(BANDS)]
     turned = (((1,), (1,)), ((), ()))
     vertices = middle_ref.shape[0]
     step = 256
@@ -128,18 +147,12 @@
             power = (one * one + two * two).astype(BF16)
             smooth = lax.dot_general(power, smooths[band], turned, preferred_element_type=F32)
             env[cut, band * 128 : (band + 1) * 128] = smooth.astype(BF16)
-    offsets = (0, P1, SPLIT)
-    ids = [ids_ref[r : r + 1] + offsets[r] for r in range(3)]
     height = form.padded
     lane = iota((64, 128), 1)
     row = iota((64, 128), 0)
     diagonal = lax.rem(lane, 64) == row
     for k in range(owners):
-        owner = me ^ k
-        wanted = iota((height, 1), 0) + owner * form.rows
-        hits = (wanted == ids[0]) | (wanted == ids[1]) | (wanted == ids[2])
-        hits = jnp.where(hits, 1.0, 0.0).astype(BF16)
-        sums = jnp.dot(hits, env[...], preferred_element_type=F32)
+        sums = jnp.dot(hits_ref[k], env[...], preferred_element_type=F32)
         for band in range(BANDS):
             cells = sums[:, band * 128 : (band + 1) * 128]
             mean = jnp.mean(cells, axis=1, keepdims=True)
@@ -170,9 +183,9 @@
     return sum((1 if k & bit else 0) << j for j, bit in enumerate(order))
 
 
-def front(form, owners, orders, middle, first, second, taps, smooths, ids):
+def front(form, owners, orders, first, second, middle, *prepared):
     shape = jax.ShapeDtypeStruct((owners // 2, form.height, 128), BF16)
-    operands = (middle, first, second, taps, smooths, ids)
+    operands = (first, second, middle, *prepared)
     return pl.pallas_call(
         partial(front_kernel, form, owners, orders),
         out_shape=[shape] * (2 * BANDS),
@@ -213,8 +226,8 @@
     return middle * power, rest
 
 
-def lag_sums_kernel(form, band, own_ref, out_ref):
-    middle = own_rows(form, own_ref, band)[0]
+def row_weights_kernel(form, band, own_ref, forward_ref, to_weights_ref, inverse_ref, out_ref, column_ref):
+    middle, rest = own_rows(form, own_ref, band)
     lane = iota((1, 128), 1)
     row = iota((128, 128), 0)
     col = iota((128, 128), 1)
@@ -229,29 +242,10 @@
         out_ref[:, d * 128 : (d + 1) * 128] = sums.astype(BF16)
         turned = further
 
-
-def lag_sums(form, band, own):
-    return pl.pallas_call(
-        partial(lag_sums_kernel, form, band),
-        out_shape=jax.ShapeDtypeStruct((form.padded, 64 * 128), BF16),
-        in_specs=[VMEM],
-        out_specs=VMEM,
-        compiler_params=params(12),
-        cost_estimate=cost(2 * 10**9, 3 * 10**6),
-        name="lag_sums",
-    )(own)
-
-
-def spectra_kernel(form, own_ref, forward_ref, to_weights_ref, inverse_ref, freq_ref, edge_ref, column_ref):
     window, windows = lax.axis_index("tm"), lax.axis_size("tm")
-    rows = [own_rows(form, own_ref, band) for band in range(BANDS)]
-    middle = jnp.concatenate([cells for cells, _ in rows], axis=0)
-    rest = jnp.concatenate([left for _, left in rows], axis=0)
     dot = partial(jnp.dot, precision=HIGH, preferred_element_type=F32)
-    forward = forward_ref[...]
     spectrum = dot(middle, forward_ref[0:128])
     low, high = spectrum[:, :128], spectrum[:, 128:]
-    lane = iota(low.shape, 1)
     inner = jnp.where(lane == 0, 0.0, high)
     last = jnp.where(lane == 0, high, 0.0)
     strength = jnp.concatenate([low * low + inner * inner, last * last], axis=1)
@@ -264,33 +258,31 @@
     outside = jnp.where(outside, 1.0, 0.0).astype(BF16)
     sums = jnp.dot(middle.astype(BF16), outside, preferred_element_type=F32)
     edge_sum = jnp.sum(sums * sums, axis=1, keepdims=True)
-    other = dot(sums, forward)
+    other = dot(sums, forward_ref[...])
     other_low, other_high = other[:, :128], other[:, 128:]
     cross = other_high * high
     real = other_low * low - jnp.where(lane == 0, 0.0, cross)
     imag = jnp.where(lane == 0, cross, other_low * high + other_high * low)
     edge = dot(jnp.concatenate([real, imag], axis=1), inverse_ref[...])
+    big = weights.astype(BF16)
+    out_ref[:, LAGS : LAGS + 256] = big
+    out_ref[:, LAGS + 256 : LAGS + 512] = (weights - big.astype(F32)).astype(BF16)
+    out_ref[:, LAGS + 512 : LAGS + 768] = big
+    out_ref[:, LAGS + 768 : LAGS + 1024] = edge.astype(BF16)
     factor = rest * (1.0 / (128 * 128 * NLAG))
-    column = jnp.where(lane == 0, edge_sum, jnp.where(lane == 1, factor, 0.0))
-    for band in range(BANDS):
-        cut = slice(band * form.padded, (band + 1) * form.padded)
-        big = weights[cut].astype(BF16)
-        freq_ref[band, :, 0:256] = big
-        freq_ref[band, :, 256:512] = (weights[cut] - big.astype(F32)).astype(BF16)
-        edge_ref[band] = edge[cut].astype(BF16)
-        column_ref[band] = column[cut]
-
-
-def spectra(form, own):
-    shapes = [((BANDS, form.padded, 512), BF16), ((BANDS, form.padded, 256), BF16), ((BANDS, form.padded, 128), F32)]
+    column_ref[...] = jnp.where(lane == 0, edge_sum, jnp.where(lane == 1, factor, 0.0))
+
+
+def row_weights(form, band, own):
+    shapes = [((form.padded, LAGS + 1024), BF16), ((form.padded, 128), F32)]
     return pl.pallas_call(
-        partial(spectra_kernel, form),
+        partial(row_weights_kernel, form, band),
         out_shape=[jax.ShapeDtypeStruct(*shape) for shape in shapes],
         in_specs=[VMEM] * 4,
-        out_specs=[VMEM] * 3,
+        out_specs=[VMEM] * 2,
         compiler_params=params(12),
-        cost_estimate=cost(2 * 10**9, 2 * 10**6),
-        name="row_spectra",
+        cost_estimate=cost(3 * 10**9, 4 * 10**6),
+        name="row_weights",
     )(own, jnp.asarray(FORWARD), jnp.asarray(TO_WEIGHTS), jnp.asarray(INVERSE))
 
 
@@ -304,23 +296,84 @@
     return jnp.sum(jnp.where(own, spread, 0.0), axis=1, keepdims=True)
 
 
-def margins_kernel(form, owners, *refs):
-    halves, outs = refs[: 2 * BANDS], refs[2 * BANDS :]
+def pieces(form, owners, owner):
+    at = owner * form.rows
+    found = []
+    for lo, hi, gap in ((0, SPLIT, 0), (SPLIT, owners * form.rows, GROUP - SPLIT)):
+        start, stop = max(lo, at), min(hi, at + form.rows)
+        if start < stop:
+            found.append((slice(start - at, stop - at), slice(start + gap, stop + gap)))
+    return found
+
+
+def stands(order, k):
+    return sum(lax.rem(k // bit, 2) << j for j, bit in enumerate(order))
+
+
+def gaps(form, owners):
+    end = GROUP + owners * form.rows - SPLIT
+    return (slice(SPLIT, GROUP), slice(end, columns_of(form, owners)))
+
+
+def columns_of(form, owners):
+    return GROUP + (owners * form.rows - SPLIT + TILE - 1) // TILE * TILE
+
+
+def scaled_rows_kernel(form, owners, orders, near_0, far_0, near_1, far_1, middle_ref, extra_ref, blocks):
+    me = lax.axis_index("vert")
+    window, windows = lax.axis_index("tm"), lax.axis_size("tm")
+    edge = (window == 0) | (window == windows - 1)
+    half = owners // 2
+    lane = iota((1, 128), 1)
+    for band, (low, high) in enumerate(((near_0, far_0), (near_1, far_1))):
+        blocks[0:half] = low[...]
+        blocks[half:owners] = high[...]
+        for cut in gaps(form, owners):
+            middle_ref[band, cut] = jnp.zeros((cut.stop - cut.start, 128), F32)
+            extra_ref[band, cut] = jnp.zeros((cut.stop - cut.start, 128), F32)
+        for owner in range(owners):
+            block = blocks[stands(orders[band], me ^ owner)]
+            middle = block[0 : form.padded].astype(F32)
+            mean = mean_column(form, block)
+            power, left_over = scales_of(middle)
+            mu = jnp.where(edge, mean.astype(BF16).astype(F32) * power, 0.0)
+            scaled = middle * power
+            extra = jnp.where(lane == 0, mu, jnp.where(lane == 1, left_over, jnp.where(lane == 2, power, mean)))
+            for cut, put in pieces(form, owners, owner):
+                middle_ref[band, put] = scaled[cut]
+                extra_ref[band, put] = extra[cut]
+
+
+def scaled_rows(form, owners, orders, *halves):
+    shape = jax.ShapeDtypeStruct((BANDS, columns_of(form, owners), 128), F32)
+    return pl.pallas_call(
+        partial(scaled_rows_kernel, form, owners, orders),
+        out_shape=[shape] * 2,
+        in_specs=[VMEM] * len(halves),
+        out_specs=[VMEM] * 2,
+        scratch_shapes=[pltpu.VMEM((owners, form.height, 128), BF16)],
+        compiler_params=params(12),
+        cost_estimate=cost(10**9, 4 * 10**6),
+        name="scaled_rows",
+    )(*halves)
+
+
+def margins_kernel(owners, *refs):
+    halves, outs = refs[:BANDS], refs[BANDS:]
     odd = lax.rem(lax.axis_index("tm"), 2) == 1
     is_low = iota((1, 128), 1) < LAG
-    half = owners // 2
     for n in range(owners):
-        zero, one = (halves[2 * band + n // half][n % half].astype(F32) for band in range(BANDS))
+        zero, one = (halves[band][n].astype(F32) for band in range(BANDS))
         early = jnp.where(is_low, zero, pltpu.roll(one, 64, 1)).astype(BF16)
         late = jnp.where(is_low, pltpu.roll(zero, 64, 1), one).astype(BF16)
         outs[0][n] = jnp.where(odd, early, late)
         outs[1][n] = jnp.where(odd, late, early)
 
 
-def margins(form, owners, *halves):
+def margins(*halves):
     return pl.pallas_call(
-        partial(margins_kernel, form, owners),
-        out_shape=[jax.ShapeDtypeStruct((owners, form.height, 128), BF16)] * 2,
+        partial(margins_kernel, halves[0].shape[0]),
+        out_shape=[jax.ShapeDtypeStruct(halves[0].shape, BF16)] * 2,
         in_specs=[VMEM] * len(halves),
         out_specs=[VMEM] * 2,
         compiler_params=params(8),
@@ -330,55 +383,43 @@
 
 
 def coupling_kernel(
-    form, owners, orders, lag_0, lag_1, freq_ref, edge_ref, column_ref, near_0, far_0, near_1, far_1,
-    first_ref, second_ref, factor_ref, out_ref, result, blocks, rows, near, far, near_turn, far_turn, change
+    form, owners, orders, lag_0, lag_1, column_0, column_1, middle_ref, extra_ref,
+    first_0, second_0, first_1, second_1, factor_ref, out_ref, result, first_ref, second_ref, around_rows, near, far, near_turn, far_turn, change
 ):
     me = lax.axis_index("vert")
     window, windows = lax.axis_index("tm"), lax.axis_size("tm")
     odd = lax.rem(window, 2) == 1
     half = owners // 2
-    for band, (low, high) in enumerate(((near_0, far_0), (near_1, far_1))):
-        blocks[band, 0:half] = low[...]
-        blocks[band, half:owners] = high[...]
+    for whole, low, high in ((first_ref, first_0, first_1), (second_ref, second_0, second_1)):
+        whole[0:half] = low[...]
+        whole[half:owners] = high[...]
     result[...] = jnp.zeros_like(result)
-    gaps = ((SPLIT, GROUP), (GROUP + owners * form.rows - SPLIT, rows.shape[1]))
-    for start, stop in gaps:
-        rows[:, start:stop] = jnp.zeros((BANDS, stop - start, 384), F32)
+    for cut in gaps(form, owners):
+        around_rows[:, cut] = jnp.zeros((BANDS, cut.stop - cut.start, 128), F32)
     lane = iota((1, 128), 1)
     is_left = lane < LAG
     first_window, last_window = window == 0, window == windows - 1
     outside = (first_window & is_left) | (last_window & ~is_left)
+    begin = me * form.rows
+    end = jnp.minimum(begin + form.rows, SPLIT + P3)
+    coarse, fine = begin < SPLIT, end > SPLIT
     for band in range(BANDS):
         for owner in range(owners):
-            k = me ^ owner
-            p = sum(lax.rem(k // bit, 2) << j for j, bit in enumerate(orders[band]))
-            block = blocks[band, p]
-            middle = block[0 : form.padded].astype(F32)
-            mean = mean_column(form, block)
+            p = stands(orders[band], me ^ owner)
             one, two = first_ref[p], second_ref[p]
             left, right = jnp.where(odd, one, two), jnp.where(odd, two, one)
-            shift_left = mean_column(form, left, band * 64) - mean
-            shift_right = mean_column(form, right, band * 64) - mean
+            shift_left = mean_column(form, left, band * 64)
+            shift_right = mean_column(form, right, band * 64)
             left, right = (cells[0 : form.padded].astype(F32) for cells in (left, right))
             if band == 0:
                 right = pltpu.roll(right, 64, 1)
             else:
                 left = pltpu.roll(left, 64, 1)
-            around = jnp.where(is_left, left, right)
-            around = (around + jnp.where(is_left, shift_left, shift_right)).astype(BF16).astype(F32)
-            around = jnp.where(outside, 0.0, around)
-            power, left_over = scales_of(middle)
-            mu = jnp.where(first_window | last_window, mean.astype(BF16).astype(F32) * power, 0.0)
-            extra = jnp.where(lane == 0, mu, jnp.where(lane == 1, left_over, 0.0))
-            begin = owner * form.rows
-            for lo, hi, gap in ((0, SPLIT, 0), (SPLIT, owners * form.rows, GROUP - SPLIT)):
-                start, stop = max(lo, begin), min(hi, begin + form.rows)
-                if start < stop:
-                    cut = slice(start - begin, stop - begin)
-                    put = slice(start + gap, stop + gap)
-                    rows[band, put, 0:128] = (middle * power)[cut]
-                    rows[band, put, 128:256] = (around * power)[cut]
-                    rows[band, put, 256:384] = extra[cut]
+            around = jnp.where(is_left, left + shift_left, right + shift_right)
+            for cut, put in pieces(form, owners, owner):
+                extra = extra_ref[band, put]
+                shifted = (around[cut] - extra[:, 3:4]).astype(BF16).astype(F32) * extra[:, 2:3]
+                around_rows[band, put] = jnp.where(outside, 0.0, shifted)
 
     own_parcel = iota((form.padded, 1), 0) + me * form.rows
     own_level = level_of(own_parcel)
@@ -388,8 +429,10 @@
         lag_ref = (lag_0, lag_1)[band]
         rows_of = slice(start, start + height)
         first = pl.multiple_of(step * TILE, TILE)
-        columns = rows[band, pl.ds(first, TILE), :].T
-        narrow = columns[0:256].astype(BF16)
+        tile_of = pl.ds(first, TILE)
+        columns = jnp.concatenate([middle_ref[band, tile_of].T, around_rows[band, tile_of].T], axis=0)
+        constants = extra_ref[band, tile_of].T
+        narrow = columns.astype(BF16)
         near[0:64] = columns[128:192]
         near[64:127] = columns[0:63]
         near[127:191] = columns[128:192]
@@ -397,6 +440,20 @@
         far[63:127] = columns[192:256]
         far[127:190] = columns[65:128]
         far[190:191] = columns[192:193]
+        twice = jnp.concatenate([narrow, narrow], axis=0)
+        spectra = jnp.dot(factor_ref[...], twice, preferred_element_type=F32)
+        low_a, high_a, low_c, high_c = (spectra[128 * k : 128 * (k + 1)] for k in range(4))
+        at_zero = iota((128, TILE), 0) == 0
+        cross = high_a * high_c
+        real = low_a * low_c + jnp.where(at_zero, 0.0, cross)
+        imag = jnp.where(at_zero, cross, low_a * high_c - high_a * low_c)
+        both = jnp.concatenate([real, imag], axis=0)
+        big = both.astype(BF16)
+        small = (both - big.astype(F32)).astype(BF16)
+        mu, other_factor = constants[0:1], constants[1:2]
+        mixed = (columns * (-2.0 * mu)).astype(BF16)
+        for n, part in enumerate((big, big, small, mixed)):
+            change[LAGS + 256 * n : LAGS + 256 * (n + 1)] = part
         for r in range(16):
             near_turn[r] = near[r : r + 176].astype(BF16)
             far_turn[r] = far[r : r + 176].astype(BF16)
@@ -407,26 +464,9 @@
                 - near_turn[0, 0:128] * near_turn[r, 16 * a : 16 * a + 128]
             )
         total = jnp.dot(lag_ref[rows_of], change[...], preferred_element_type=F32)
-        spectra = jnp.dot(factor_ref[0:512], narrow, preferred_element_type=F32) + jnp.dot(
-            factor_ref[512:1024], narrow, preferred_element_type=F32
-        )
-        low_a, high_a, low_c, high_c = (spectra[128 * k : 128 * (k + 1)] for k in range(4))
-        at_zero = iota((128, TILE), 0) == 0
-        cross = high_a * high_c
-        real = low_a * low_c + jnp.where(at_zero, 0.0, cross)
-        imag = jnp.where(at_zero, cross, low_a * high_c - high_a * low_c)
-        both = jnp.concatenate([real, imag], axis=0)
-        big = both.astype(BF16)
-        small = (both - big.astype(F32)).astype(BF16)
-        weights = freq_ref[band, rows_of]
-        total += jnp.dot(weights[:, 0:256], big, preferred_element_type=F32)
-        total += jnp.dot(weights[:, 256:512], big, preferred_element_type=F32)
-        total += jnp.dot(weights[:, 0:256], small, preferred_element_type=F32)
-        mixed = jnp.dot(edge_ref[band, rows_of], narrow, preferred_element_type=F32)
-        mu, other_factor = columns[256:257], columns[257:258]
-        factors = column_ref[band, rows_of]
+        factors = (column_0, column_1)[band][rows_of]
         edge_sum, own_factor = factors[:, 0:1], factors[:, 1:2]
-        total += mu * (mu * edge_sum - 2.0 * mixed)
+        total += mu * mu * edge_sum
         column = iota((1, TILE), 1) + first
         parcel = jnp.where(column < GROUP, column, column - (GROUP - SPLIT))
         gap = (column >= SPLIT) & (column < GROUP)
@@ -436,11 +476,8 @@
         result[band, rows_of, pl.ds(first, TILE)] = jnp.where(same, scaled, 0.0)
         return carry
 
-    begin = me * form.rows
-    end = jnp.minimum(begin + form.rows, SPLIT + P3)
     tiles = result.shape[2] // TILE
     fold = GROUP // TILE
-    coarse, fine = begin < SPLIT, end > SPLIT
     for band in range(BANDS):
         run = lambda lo, hi, start, height: lax.fori_loop(
             lo, hi, partial(tile, band, start, height), 0
@@ -461,7 +498,7 @@
 
 def coupling(form, owners, orders, *operands):
     total = owners * form.rows
-    width = GROUP + (total - SPLIT + TILE - 1) // TILE * TILE
+    width = columns_of(form, owners)
     operands = (*operands, jnp.asarray(FACTORS))
     return pl.pallas_call(
         partial(coupling_kernel, form, owners, orders),
@@ -470,13 +507,14 @@
         out_specs=VMEM,
         scratch_shapes=[
             pltpu.VMEM((BANDS, form.padded, width), F32),
-            pltpu.VMEM((BANDS, owners, form.height, 128), BF16),
-            pltpu.VMEM((BANDS, width, 384), F32),
+            pltpu.VMEM((owners, form.height, 128), BF16),
+            pltpu.VMEM((owners, form.height, 128), BF16),
+            pltpu.VMEM((BANDS, width, 128), F32),
             pltpu.VMEM((192, TILE), F32),
             pltpu.VMEM((192, TILE), F32),
             pltpu.VMEM((16, 176, TILE), BF16),
             pltpu.VMEM((16, 176, TILE), BF16),
-            pltpu.VMEM((64 * 128, TILE), BF16),
+            pltpu.VMEM((LAGS + 1024, TILE), BF16),
         ],
         compiler_params=params(24),
         cost_estimate=cost(16 * 10**9, 10**7),
@@ -498,7 +536,8 @@
     first, second = (lax.ppermute(source, "tm", pairs) for pairs in meet)
     taps = jnp.pad(band_taps.astype(F32).reshape(2 * BANDS, 1, TAPS), ((0, 0), (0, 0), (0, 256 - TAPS)))
     smooths = jnp.pad(smooth_taps.astype(F32)[:, None, :], ((0, 0), (0, 0), (0, 256 - TAPS)))
-    parts = front(form, owners, orders, source, first, second, taps, smooths, parcel_ids)
+    prepared = prepare(form, owners, source, taps, smooths, parcel_ids)
+    parts = front(form, owners, orders, first, second, *prepared)
     parts = [parts[0:2], parts[2:4]]
     for step in range(len(bits) - 1):
         arrived = [swap(parts[b][1], owners, orders[b][step]) for b in range(BANDS)]
@@ -506,24 +545,32 @@
         half = sums[0].shape[0] // 2
         parts = [(cells[:half], cells[half:]) for cells in sums]
     kept, sent = (jnp.concatenate([parts[b][k] for b in range(BANDS)], axis=0) for k in range(2))
-    own = added(form, kept, swap(sent, owners, bits[-1]))
-
-    lag = [lag_sums(form, band, own) for band in range(BANDS)]
-    freq, edge, column = spectra(form, own)
-    arrived = swap(own, owners, bits[-1])
-    held = [jnp.stack([own[b], arrived[b]]) for b in range(BANDS)]
-    held, lag[0] = lax.optimization_barrier((held, lag[0]))
-    halves = [None, None]
+    theirs = swap(jnp.concatenate([kept, sent], axis=0), owners, bits[-1])
+    both = added(form, jnp.concatenate([kept, sent], axis=0), jnp.concatenate([theirs[BANDS:], theirs[:BANDS]], axis=0))
+    own = both[:BANDS]
+    held = [jnp.stack([both[b], both[BANDS + b]]) for b in range(BANDS)]
+    weights = [row_weights(form, 0, own), None]
+    sides = []
+
+    def send_margins(packed):
+        sides.append([lax.ppermute(cells, "tm", pairs) for cells, pairs in zip(packed, meet)])
+
     for step in range(len(bits) - 2, -1, -1):
         arrived = [swap(held[b], owners, orders[b][step]) for b in range(BANDS)]
-        halves = [(held[b], arrived[b]) for b in range(BANDS)]
         if step:
-            held = [jnp.concatenate(pair, axis=0) for pair in halves]
-    first, second = margins(form, owners, *halves[0], *halves[1])
-    first = lax.ppermute(first, "tm", meet[0])
-    second = lax.ppermute(second, "tm", meet[1])
+            held = [jnp.concatenate([held[b], arrived[b]], axis=0) for b in range(BANDS)]
+            if step == 1:
+                held, weights[0] = lax.optimization_barrier((held, weights[0]))
+        else:
+            packed, own = lax.optimization_barrier((margins(*held), own))
+            send_margins(packed)
+            weights[1] = row_weights(form, 1, own)
+            arrived, weights[1] = lax.optimization_barrier((arrived, weights[1]))
+            send_margins(margins(*arrived))
     turned = [order[::-1] for order in orders]
-    done = coupling(form, owners, turned, *lag, freq, edge, column, *halves[0], *halves[1], first, second)
+    middle, extra = scaled_rows(form, owners, turned, held[0], arrived[0], held[1], arrived[1])
+    lag, column = zip(*weights)
+    done = coupling(form, owners, turned, *lag, *column, middle, extra, *sides[0], *sides[1])
     return done.transpose(1, 0, 2)[None]
 
 

time: 89.3 us -> 83.3 us (0.933)
  waiting for transfers between devices: 25.6 us -> 20.9 us
  starting transfers between devices: 22.5 us -> 19.6 us
  Pallas kernels: 36.9 us -> 38.3 us
    ppermute x2, waiting for transfers between devices: 4.2 us -> 0.01 us  [local(): first, second = (lax.ppermute(source, 'tm', pairs) for pairs in meet)]
    pallas_call x4 -> x6, Pallas kernels: 6.97 us -> 11.1 us  [the longest x2 6.54 us: row_weights(): pl.pallas_call(partial(row_weights_kernel, form, band), out_shape=[jax.Sh...]
    ppermute x10 -> x9, starting transfers between devices: 11.1 us -> 8.63 us  [swap(): return lax.ppermute(cells, 'vert', [(i, i ^ bit) for i in range(owners)])]
    ppermute x10 -> x9, waiting for transfers between devices: 20.5 us -> 18.2 us  [swap(): return lax.ppermute(cells, 'vert', [(i, i ^ bit) for i in range(owners)])]
    ppermute x2 -> x4, waiting for transfers between devices: 0.91 us -> 2.71 us  [send_margins(): lax.ppermute(cells, 'tm', pairs)]
    pallas_call x1, Pallas kernels: 4.78 us -> 3.41 us  [front(): pl.pallas_call(partial(front_kernel, form, owners, orders), out_shape=[sh...]
    pallas_call x1, Pallas kernels: 25.1 us -> 23.8 us  [coupling(): pl.pallas_call(partial(coupling_kernel, form, owners, orders), out_shape=...]
    ppermute x2 -> x4, starting transfers between devices: 7.72 us -> 7.23 us  [send_margins(): lax.ppermute(cells, 'tm', pairs)]
  transfers between devices with their start and end apart: 14 -> 15, of which waited for: 11 -> 6; matrix products, arithmetic and copies ran while one was open for 2% -> 2% of each run, Pallas kernels for 7% -> 13%
where the time goes in v5:
time: 83.3 us; the launch traced here: 83 us
  Pallas kernels  38.3 us (46%)
  waiting for transfers between devices  20.9 us (25%)
  starting transfers between devices  19.6 us (24%)
  local copies, waits for them, and re-layouts  3.25 us (4%)
    pallas_call x1, Pallas kernels, coupling(): pl.pallas_call(partial(coupling_kernel, form, owners, orders), out_shape=...  23.8 us
    ppermute x9, waiting for transfers between devices, swap(): return lax.ppermute(cells, 'vert', [(i, i ^ bit) for i in range(owners)])  18.2 us
    ppermute x9, starting transfers between devices, swap(): return lax.ppermute(cells, 'vert', [(i, i ^ bit) for i in range(owners)])  8.63 us
    ppermute x4, starting transfers between devices, send_margins(): lax.ppermute(cells, 'tm', pairs)  7.23 us
    pallas_call x2, Pallas kernels, row_weights(): pl.pallas_call(partial(row_weights_kernel, form, band), out_shape=[jax.Sh...  6.54 us
    ppermute x2, starting transfers between devices, local(): first, second = (lax.ppermute(source, 'tm', pairs) for pairs in meet)  3.7 us
    pallas_call x1, Pallas kernels, front(): pl.pallas_call(partial(front_kernel, form, owners, orders), out_shape=[sh...  3.41 us
    pallas_call x1, Pallas kernels, prepare(): pl.pallas_call(partial(prepare_kernel, form, owners), out_shape=[jax.Shap...  2.74 us
  transfers between devices with their start and end apart: 15, of which 6 were waited for; matrix products, arithmetic and copies ran while one was open for 2% of the time, Pallas kernels for 13%

profile of v5, /device:TPU:9, one launch (start us, length us, event | category | flops | bytes accessed | tf_op | source)
XLA Modules:
  0.0 83.0 jit_solution(7290794249011569561)
XLA Ops:
  0.0 0.7 collective-permute-start
  0.7 3.0 %collective-permute-start.1 = (bf16[1280,128]{1,0:T(8,128)(2,1)}, bf16[1280,128]{1,0:T(8,128)(2,1)S(1)}, u32[]{:S(2)}, u32[]{:S(2)}) collective-permute-start(bf16[1280,128]{1,0:T(8,128)(2,1)} %middle_ref.1), channel_id=1, source_target_pairs={{1,2},{2,1},{5,6},{6,5},{9,10},{10,9},{13,14},{14,13},{17,18},{18,... | collective-permute-start | bytes 983048 | tf_op jit(solution)/shard_map/ppermute | solution.py:536
  4.4 0.7 copy.9
  5.1 1.0 %copy-done = bf16[1280,128]{1,0:T(8,128)(2,1)S(1)} copy-done((bf16[1280,128]{1,0:T(8,128)(2,1)S(1)}, bf16[1280,128]{1,0:T(8,128)(2,1)}, u32[]{:S(2)}) %copy-start) | copy-done | bytes 327704
  6.0 0.7 copy-done.1
  6.8 2.7 %prepare.1 = (bf16[1280,128]{1,0:T(8,128)(2,1)S(1)}, bf16[4,256,256]{2,1,0:T(8,128)(2,1)S(1)}, bf16[2,128,256]{2,1,0:T(8,128)(2,1)S(1)}, bf16[8,192,1280]{2,1,0:T(8,128)(2,1)S(1)}) custom-call(bf16[1280,128]{1,0:T(8,128)(2,1)S(1)} %copy-done, f32[4,1,256]{2,1,0:T(1,128)S(1)} %pad_convert_fusion.taps_ref, f32[2,1,256]{2,1,0:T(1,128)S(1)} %pad_convert_fusion.1.smooth_ref, ...), custom_call_target="tpu_custom_call" | custom-call | flops 2000000000 | bytes 5000000 | tf_op jit(solution)/shard_map/prepare/pallas_call | solution.py:119
  9.5 3.4 %envelope_sums.1 = (bf16[4,208,128]{2,1,0:T(8,128)(2,1)S(1)}, bf16[4,208,128]{2,1,0:T(8,128)(2,1)S(1)}, bf16[4,208,128]{2,1,0:T(8,128)(2,1)S(1)}, bf16[4,208,128]{2,1,0:T(8,128)(2,1)S(1)}) custom-call(bf16[1280,128]{1,0:T(8,128)(2,1)S(1)} %collective-permute-done.first_ref, bf16[1280,128]{1,0:T(8,128)(2,1)S(1)} %collective-permute-done.1.second_ref, ...), custom_call_target="tpu_custom_call" | custom-call | flops 3000000000 | bytes 2000000 | tf_op jit(solution)/shard_map/envelope_sums/pallas_call | solution.py:189
  13.0 1.3 %collective-permute-start.2 = (bf16[4,208,128]{2,1,0:T(8,128)(2,1)S(1)}, bf16[4,208,128]{2,1,0:T(8,128)(2,1)S(1)}, u32[]{:S(2)}, u32[]{:S(2)}) collective-permute-start(bf16[4,208,128]{2,1,0:T(8,128)(2,1)S(1)} %get-tuple-element.39), channel_id=1, source_target_pairs={{0,4},{4,0},{8,12},{12,8},{16,20},{20,16},{24,28},{28,24},{1,5},{5... | collective-permute-start | bytes 638984 | tf_op jit(solution)/shard_map/ppermute | solution.py:526
  14.4 3.8 %collective-permute-done.2 = bf16[4,208,128]{2,1,0:T(8,128)(2,1)S(1)} collective-permute-done((bf16[4,208,128]{2,1,0:T(8,128)(2,1)S(1)}, bf16[4,208,128]{2,1,0:T(8,128)(2,1)S(1)}, u32[]{:S(2)}, u32[]{:S(2)}) %collective-permute-start.2) | collective-permute-done | bytes 213024 | tf_op jit(solution)/shard_map/ppermute | solution.py:526
  18.3 1.3 %collective-permute-done.4 = bf16[4,208,128]{2,1,0:T(8,128)(2,1)S(1)} collective-permute-done((bf16[4,208,128]{2,1,0:T(8,128)(2,1)S(1)}, bf16[4,208,128]{2,1,0:T(8,128)(2,1)S(1)}, u32[]{:S(2)}, u32[]{:S(2)}) %collective-permute-start.4) | collective-permute-done | bytes 213024 | tf_op jit(solution)/shard_map/ppermute | solution.py:526
  20.3 4.1 %collective-permute-done.3 = bf16[2,208,128]{2,1,0:T(8,128)(2,1)S(1)} collective-permute-done((bf16[2,208,128]{2,1,0:T(8,128)(2,1)S(1)}, bf16[2,208,128]{2,1,0:T(8,128)(2,1)S(1)}, u32[]{:S(2)}, u32[]{:S(2)}) %collective-permute-start.3) | collective-permute-done | bytes 106528 | tf_op jit(solution)/shard_map/ppermute | solution.py:526
  24.9 2.4 %collective-permute-start.6 = (bf16[4,208,128]{2,1,0:T(8,128)(2,1)S(1)}, bf16[4,208,128]{2,1,0:T(8,128)(2,1)S(1)}, u32[]{:S(2)}, u32[]{:S(2)}) collective-permute-start(bf16[4,208,128]{2,1,0:T(8,128)(2,1)S(1)} %pad_maximum_fusion.2), channel_id=1, source_target_pairs={{0,16},{4,20},{8,24},{12,28},{16,0},{20,4},{24,8},{28,12},{1,17},{... | collective-permute-start | bytes 638984 | tf_op jit(solution)/shard_map/ppermute | solution.py:526
  27.3 8.8 %collective-permute-done.6 = bf16[4,208,128]{2,1,0:T(8,128)(2,1)S(1)} collective-permute-done((bf16[4,208,128]{2,1,0:T(8,128)(2,1)S(1)}, bf16[4,208,128]{2,1,0:T(8,128)(2,1)S(1)}, u32[]{:S(2)}, u32[]{:S(2)}) %collective-permute-start.6) | collective-permute-done | bytes 213024 | tf_op jit(solution)/shard_map/ppermute | solution.py:526
  36.3 2.8 %collective-permute-start.7 = (bf16[2,208,128]{2,1,0:T(8,128)(2,1)S(1)}, bf16[2,208,128]{2,1,0:T(8,128)(2,1)S(1)}, u32[]{:S(2)}, u32[]{:S(2)}) collective-permute-start(bf16[2,208,128]{2,1,0:T(8,128)(2,1)S(1)} %pad_maximum_fusion.8), channel_id=1, source_target_pairs={{0,8},{4,12},{8,0},{12,4},{16,24},{20,28},{24,16},{28,20},{1,9},{5... | collective-permute-start | bytes 319496 | tf_op jit(solution)/shard_map/ppermute | solution.py:526
  39.5 3.3 %row_weights.2 = (bf16[192,9216]{1,0:T(8,128)(2,1)S(1)}, f32[192,128]{1,0:T(8,128)S(1)}) custom-call(bf16[2,208,128]{2,1,0:T(8,128)(2,1)S(1)} %slice.154.own_ref, f32[256,256]{1,0:T(8,128)S(1)} %copy-done.5, f32[256,256]{1,0:T(8,128)S(1)} %copy-done.4, f32[256,256]{1,0:T(8,128)S(1)} %copy-done.3), custom_call_target="tpu_custom_call" | custom-call | flops 3000000000 | bytes 4000000 | tf_op jit(solution)/shard_map/row_weights/pallas_call | solution.py:278
  42.8 1.3 %collective-permute-start.9 = (bf16[4,208,128]{2,1,0:T(8,128)(2,1)S(1)}, bf16[4,208,128]{2,1,0:T(8,128)(2,1)S(1)}, u32[]{:S(2)}, u32[]{:S(2)}) collective-permute-start(bf16[4,208,128]{2,1,0:T(8,128)(2,1)S(1)} %pad_maximum_fusion.4.refs_0_.near_0), channel_id=1, source_target_pairs={{0,4},{4,0},{8,12},{12,8},{16,20},{20,16},{24,28},{28,24},{1,5},{5... | collective-permute-start | bytes 638984 | tf_op jit(solution)/shard_map/ppermute | solution.py:526
  44.4 1.4 %collective-permute-start.11 = (bf16[4,208,128]{2,1,0:T(8,128)(2,1)S(1)}, bf16[4,208,128]{2,1,0:T(8,128)(2,1)S(1)}, u32[]{:S(2)}, u32[]{:S(2)}) collective-permute-start(bf16[4,208,128]{2,1,0:T(8,128)(2,1)S(1)} %get-tuple-element.59), channel_id=1, source_target_pairs={{0,1},{1,0},{2,3},{3,2},{4,5},{5,4},{6,7},{7,6},{8,9},{9,8},{10,11... | collective-permute-start | bytes 638984 | tf_op jit(solution)/shard_map/ppermute | solution.py:556
  45.8 2.1 %collective-permute-start.12 = (bf16[4,208,128]{2,1,0:T(8,128)(2,1)S(1)}, bf16[4,208,128]{2,1,0:T(8,128)(2,1)S(1)}, u32[]{:S(2)}, u32[]{:S(2)}) collective-permute-start(bf16[4,208,128]{2,1,0:T(8,128)(2,1)S(1)} %get-tuple-element.60), channel_id=1, source_target_pairs={{1,2},{2,1},{5,6},{6,5},{9,10},{10,9},{13,14},{14,13},{17,18},{18,... | collective-permute-start | bytes 638984 | tf_op jit(solution)/shard_map/ppermute | solution.py:556
  47.9 3.3 %row_weights.3 = (bf16[192,9216]{1,0:T(8,128)(2,1)S(1)}, f32[192,128]{1,0:T(8,128)S(1)}) custom-call(bf16[2,208,128]{2,1,0:T(8,128)(2,1)S(1)} %slice.154.own_ref, f32[256,256]{1,0:T(8,128)S(1)} %copy-done.5, f32[256,256]{1,0:T(8,128)S(1)} %copy-done.4, f32[256,256]{1,0:T(8,128)S(1)} %copy-done.3), custom_call_target="tpu_custom_call" | custom-call | flops 3000000000 | bytes 4000000 | tf_op jit(solution)/shard_map/row_weights/pallas_call | solution.py:278
  51.4 0.7 collective-permute-start.13
  52.1 3.1 %collective-permute-start.14 = (bf16[4,208,128]{2,1,0:T(8,128)(2,1)S(1)}, bf16[4,208,128]{2,1,0:T(8,128)(2,1)S(1)}, u32[]{:S(2)}, u32[]{:S(2)}) collective-permute-start(bf16[4,208,128]{2,1,0:T(8,128)(2,1)S(1)} %get-tuple-element.62), channel_id=1, source_target_pairs={{1,2},{2,1},{5,6},{6,5},{9,10},{10,9},{13,14},{14,13},{17,18},{18,... | collective-permute-start | bytes 638984 | tf_op jit(solution)/shard_map/ppermute | solution.py:556
  55.2 1.3 %scaled_rows.1 = (f32[2,1536,128]{2,1,0:T(8,128)S(1)}, f32[2,1536,128]{2,1,0:T(8,128)S(1)}) custom-call(bf16[4,208,128]{2,1,0:T(8,128)(2,1)S(1)} %pad_maximum_fusion.4.refs_0_.near_0, bf16[4,208,128]{2,1,0:T(8,128)(2,1)S(1)} %collective-permute-done.9.far_0.refs_0_, bf16[4,208,128]{2,1,0:T(8,128)(2,1)S(1)} %pad_maximum_fusion.5.refs_1_.near_1, ...), custom_call_target="tpu_custom_call" | custom-call | flops 1000000000 | bytes 4000000 | tf_op jit(solution)/shard_map/scaled_rows/pallas_call | solution.py:349
  56.5 2.7 %collective-permute-done.14.second_1 = bf16[4,208,128]{2,1,0:T(8,128)(2,1)S(1)} collective-permute-done((bf16[4,208,128]{2,1,0:T(8,128)(2,1)S(1)}, bf16[4,208,128]{2,1,0:T(8,128)(2,1)S(1)}, u32[]{:S(2)}, u32[]{:S(2)}) %collective-permute-start.14) | collective-permute-done | bytes 213024 | tf_op jit(solution)/shard_map/ppermute | solution.py:556
  59.2 23.8 %coupling.1 = f32[188,2,1504]{2,1,0:T(2,128)} custom-call(bf16[192,9216]{1,0:T(8,128)(2,1)S(1)} %get-tuple-element.44.lag_0, bf16[192,9216]{1,0:T(8,128)(2,1)S(1)} %get-tuple-element.52.lag_1, f32[192,128]{1,0:T(8,128)S(1)} %get-tuple-element.53.column_0, f32[192,128]{1,0:T(8,128)S(1)} %get-tuple-element.54.column_1, ...), custom_call_target="tpu_custom_call" | custom-call | flops 16000000000 | bytes 10000000 | tf_op jit(solution)/shard_map/coupling/pallas_call | solution.py:503
  (60 shorter events, 3.1 us)
Async XLA Ops:
  0.0 9.5 %collective-permute-start = (bf16[1280,128]{1,0:T(8,128)(2,1)}, bf16[1280,128]{1,0:T(8,128)(2,1)S(1)}, u32[]{:S(2)}, u32[]{:S(2)}) collective-permute-start(bf16[1280,128]{1,0:T(8,128)(2,1)} %middle_ref.1), channel_id=1, source_target_pairs={{0,1},{1,0},{2,3},{3,2},{4,5},{5,4},{6,7},{7,6},{8,9},{9,8},{10,11... | collective-permute-start | bytes 983048 | tf_op jit(solution)/shard_map/ppermute | solution.py:536
  0.7 8.9 %collective-permute-start.1 = (bf16[1280,128]{1,0:T(8,128)(2,1)}, bf16[1280,128]{1,0:T(8,128)(2,1)S(1)}, u32[]{:S(2)}, u32[]{:S(2)}) collective-permute-start(bf16[1280,128]{1,0:T(8,128)(2,1)} %middle_ref.1), channel_id=1, source_target_pairs={{1,2},{2,1},{5,6},{6,5},{9,10},{10,9},{13,14},{14,13},{17,18},{18,... | collective-permute-start | bytes 983048 | tf_op jit(solution)/shard_map/ppermute | solution.py:536
  5.1 1.0 %copy-start = (bf16[1280,128]{1,0:T(8,128)(2,1)S(1)}, bf16[1280,128]{1,0:T(8,128)(2,1)}, u32[]{:S(2)}) copy-start(bf16[1280,128]{1,0:T(8,128)(2,1)} %middle_ref.1) | copy-start | bytes 983044
  6.0 0.7 copy-start.1
  13.0 5.3 %collective-permute-start.2 = (bf16[4,208,128]{2,1,0:T(8,128)(2,1)S(1)}, bf16[4,208,128]{2,1,0:T(8,128)(2,1)S(1)}, u32[]{:S(2)}, u32[]{:S(2)}) collective-permute-start(bf16[4,208,128]{2,1,0:T(8,128)(2,1)S(1)} %get-tuple-element.39), channel_id=1, source_target_pairs={{0,4},{4,0},{8,12},{12,8},{16,20},{20,16},{24,28},{28,24},{1,5},{5... | collective-permute-start | bytes 638984 | tf_op jit(solution)/shard_map/ppermute | solution.py:526
  14.2 5.4 %collective-permute-start.4 = (bf16[4,208,128]{2,1,0:T(8,128)(2,1)S(1)}, bf16[4,208,128]{2,1,0:T(8,128)(2,1)S(1)}, u32[]{:S(2)}, u32[]{:S(2)}) collective-permute-start(bf16[4,208,128]{2,1,0:T(8,128)(2,1)S(1)} %get-tuple-element.41), channel_id=1, source_target_pairs={{0,8},{4,12},{8,0},{12,4},{16,24},{20,28},{24,16},{28,20},{1,9},{5... | collective-permute-start | bytes 638984 | tf_op jit(solution)/shard_map/ppermute | solution.py:526
  19.8 19.7 %copy-start.3 = (f32[256,256]{1,0:T(8,128)S(1)}, f32[256,256]{1,0:T(8,128)}, u32[]{:S(2)}) copy-start(f32[256,256]{1,0:T(8,128)} %constant.22.clone.inverse_ref) | copy-start | bytes 786436
  19.8 19.7 %copy-start.4 = (f32[256,256]{1,0:T(8,128)S(1)}, f32[256,256]{1,0:T(8,128)}, u32[]{:S(2)}) copy-start(f32[256,256]{1,0:T(8,128)} %constant.21.clone.to_weights_ref) | copy-start | bytes 786436
  19.8 19.7 %copy-start.5 = (f32[256,256]{1,0:T(8,128)S(1)}, f32[256,256]{1,0:T(8,128)}, u32[]{:S(2)}) copy-start(f32[256,256]{1,0:T(8,128)} %constant.20.clone.forward_ref) | copy-start | bytes 786436
  19.9 4.5 %collective-permute-start.3 = (bf16[2,208,128]{2,1,0:T(8,128)(2,1)S(1)}, bf16[2,208,128]{2,1,0:T(8,128)(2,1)S(1)}, u32[]{:S(2)}, u32[]{:S(2)}) collective-permute-start(bf16[2,208,128]{2,1,0:T(8,128)(2,1)S(1)} %slice.129), channel_id=1, source_target_pairs={{0,8},{4,12},{8,0},{12,4},{16,24},{20,28},{24,16},{28,20},{1,9},{5... | collective-permute-start | bytes 319496 | tf_op jit(solution)/shard_map/ppermute | solution.py:526
  20.1 4.5 %collective-permute-start.5 = (bf16[2,208,128]{2,1,0:T(8,128)(2,1)S(1)}, bf16[2,208,128]{2,1,0:T(8,128)(2,1)S(1)}, u32[]{:S(2)}, u32[]{:S(2)}) collective-permute-start(bf16[2,208,128]{2,1,0:T(8,128)(2,1)S(1)} %slice.138), channel_id=1, source_target_pairs={{0,4},{4,0},{8,12},{12,8},{16,20},{20,16},{24,28},{28,24},{1,5},{5... | collective-permute-start | bytes 319496 | tf_op jit(solution)/shard_map/ppermute | solution.py:526
  24.9 11.2 %collective-permute-start.6 = (bf16[4,208,128]{2,1,0:T(8,128)(2,1)S(1)}, bf16[4,208,128]{2,1,0:T(8,128)(2,1)S(1)}, u32[]{:S(2)}, u32[]{:S(2)}) collective-permute-start(bf16[4,208,128]{2,1,0:T(8,128)(2,1)S(1)} %pad_maximum_fusion.2), channel_id=1, source_target_pairs={{0,16},{4,20},{8,24},{12,28},{16,0},{20,4},{24,8},{28,12},{1,17},{... | collective-permute-start | bytes 638984 | tf_op jit(solution)/shard_map/ppermute | solution.py:526
  36.3 6.4 %collective-permute-start.7 = (bf16[2,208,128]{2,1,0:T(8,128)(2,1)S(1)}, bf16[2,208,128]{2,1,0:T(8,128)(2,1)S(1)}, u32[]{:S(2)}, u32[]{:S(2)}) collective-permute-start(bf16[2,208,128]{2,1,0:T(8,128)(2,1)S(1)} %pad_maximum_fusion.8), channel_id=1, source_target_pairs={{0,8},{4,12},{8,0},{12,4},{16,24},{20,28},{24,16},{28,20},{1,9},{5... | collective-permute-start | bytes 319496 | tf_op jit(solution)/shard_map/ppermute | solution.py:526
  39.2 3.6 %collective-permute-start.8 = (bf16[2,208,128]{2,1,0:T(8,128)(2,1)S(1)}, bf16[2,208,128]{2,1,0:T(8,128)(2,1)S(1)}, u32[]{:S(2)}, u32[]{:S(2)}) collective-permute-start(bf16[2,208,128]{2,1,0:T(8,128)(2,1)S(1)} %pad_maximum_fusion.9), channel_id=1, source_target_pairs={{0,4},{4,0},{8,12},{12,8},{16,20},{20,16},{24,28},{28,24},{1,5},{5... | collective-permute-start | bytes 319496 | tf_op jit(solution)/shard_map/ppermute | solution.py:526
  42.8 8.4 %collective-permute-start.9 = (bf16[4,208,128]{2,1,0:T(8,128)(2,1)S(1)}, bf16[4,208,128]{2,1,0:T(8,128)(2,1)S(1)}, u32[]{:S(2)}, u32[]{:S(2)}) collective-permute-start(bf16[4,208,128]{2,1,0:T(8,128)(2,1)S(1)} %pad_maximum_fusion.4.refs_0_.near_0), channel_id=1, source_target_pairs={{0,4},{4,0},{8,12},{12,8},{16,20},{20,16},{24,28},{28,24},{1,5},{5... | collective-permute-start | bytes 638984 | tf_op jit(solution)/shard_map/ppermute | solution.py:526
  44.1 7.1 %collective-permute-start.10 = (bf16[4,208,128]{2,1,0:T(8,128)(2,1)S(1)}, bf16[4,208,128]{2,1,0:T(8,128)(2,1)S(1)}, u32[]{:S(2)}, u32[]{:S(2)}) collective-permute-start(bf16[4,208,128]{2,1,0:T(8,128)(2,1)S(1)} %pad_maximum_fusion.5.refs_1_.near_1), channel_id=1, source_target_pairs={{0,8},{4,12},{8,0},{12,4},{16,24},{20,28},{24,16},{28,20},{1,9},{5... | collective-permute-start | bytes 638984 | tf_op jit(solution)/shard_map/ppermute | solution.py:526
  44.4 12.1 %collective-permute-start.11 = (bf16[4,208,128]{2,1,0:T(8,128)(2,1)S(1)}, bf16[4,208,128]{2,1,0:T(8,128)(2,1)S(1)}, u32[]{:S(2)}, u32[]{:S(2)}) collective-permute-start(bf16[4,208,128]{2,1,0:T(8,128)(2,1)S(1)} %get-tuple-element.59), channel_id=1, source_target_pairs={{0,1},{1,0},{2,3},{3,2},{4,5},{5,4},{6,7},{7,6},{8,9},{9,8},{10,11... | collective-permute-start | bytes 638984 | tf_op jit(solution)/shard_map/ppermute | solution.py:556
  45.8 10.7 %collective-permute-start.12 = (bf16[4,208,128]{2,1,0:T(8,128)(2,1)S(1)}, bf16[4,208,128]{2,1,0:T(8,128)(2,1)S(1)}, u32[]{:S(2)}, u32[]{:S(2)}) collective-permute-start(bf16[4,208,128]{2,1,0:T(8,128)(2,1)S(1)} %get-tuple-element.60), channel_id=1, source_target_pairs={{1,2},{2,1},{5,6},{6,5},{9,10},{10,9},{13,14},{14,13},{17,18},{18,... | collective-permute-start | bytes 638984 | tf_op jit(solution)/shard_map/ppermute | solution.py:556
  51.2 8.1 %copy-start.2 = (bf16[512,512]{1,0:T(8,128)(2,1)S(1)}, bf16[512,512]{1,0:T(8,128)(2,1)}, u32[]{:S(2)}) copy-start(bf16[512,512]{1,0:T(8,128)(2,1)} %constant.23.clone.factor_ref) | copy-start | bytes 1572868
  51.4 5.1 %collective-permute-start.13 = (bf16[4,208,128]{2,1,0:T(8,128)(2,1)S(1)}, bf16[4,208,128]{2,1,0:T(8,128)(2,1)S(1)}, u32[]{:S(2)}, u32[]{:S(2)}) collective-permute-start(bf16[4,208,128]{2,1,0:T(8,128)(2,1)S(1)} %get-tuple-element.61), channel_id=1, source_target_pairs={{0,1},{1,0},{2,3},{3,2},{4,5},{5,4},{6,7},{7,6},{8,9},{9,8},{10,11... | collective-permute-start | bytes 638984 | tf_op jit(solution)/shard_map/ppermute | solution.py:556
  52.1 7.2 %collective-permute-start.14 = (bf16[4,208,128]{2,1,0:T(8,128)(2,1)S(1)}, bf16[4,208,128]{2,1,0:T(8,128)(2,1)S(1)}, u32[]{:S(2)}, u32[]{:S(2)}) collective-permute-start(bf16[4,208,128]{2,1,0:T(8,128)(2,1)S(1)} %get-tuple-element.62), channel_id=1, source_target_pairs={{1,2},{2,1},{5,6},{6,5},{9,10},{10,9},{13,14},{14,13},{17,18},{18,... | collective-permute-start | bytes 638984 | tf_op jit(solution)/shard_map/ppermute | solution.py:556

commit v6 on v5

--- a/solution.py
+++ b/solution.py
@@ -97,14 +97,14 @@
     return tail[...].astype(BF16)
 
 
-def prepare_kernel(form, owners, middle_ref, taps_ref, smooth_ref, ids_ref, source_ref, filter_ref, smoother_ref, hits_ref):
+def prepare_kernel(form, owners, middle_ref, taps_ref, ids_ref, source_ref, filter_ref, smoother_ref, hits_ref):
     me = lax.axis_index("vert")
     source_ref[...] = middle_ref[...]
     for k in range(2 * BANDS):
-        taps = jnp.broadcast_to(taps_ref[k], (256, 256))
+        taps = jnp.broadcast_to(taps_ref[k : k + 1], (256, 256))
         filter_ref[k] = pltpu.roll(taps, 192, 1, stride=1, stride_axis=0).astype(BF16)
     for k in range(BANDS):
-        taps = jnp.broadcast_to(smooth_ref[k], (128, 256))
+        taps = jnp.broadcast_to(taps_ref[4 + k : 5 + k], (128, 256))
         smoother_ref[k] = pltpu.roll(taps, 0, 1, stride=1, stride_axis=0).astype(BF16)
     offsets = (0, P1, SPLIT)
     ids = [ids_ref[r : r + 1] + offsets[r] for r in range(3)]
@@ -114,17 +114,17 @@
         hits_ref[k] = jnp.where(hits, 1.0, 0.0).astype(BF16)
 
 
-def prepare(form, owners, source, taps, smooths, ids):
+def prepare(form, owners, source, taps, ids):
     shapes = [source.shape, (2 * BANDS, 256, 256), (BANDS, 128, 256), (owners, form.padded, source.shape[0])]
     return pl.pallas_call(
         partial(prepare_kernel, form, owners),
         out_shape=[jax.ShapeDtypeStruct(shape, BF16) for shape in shapes],
-        in_specs=[VMEM] * 4,
+        in_specs=[VMEM] * 3,
         out_specs=[VMEM] * 4,
         compiler_params=params(16),
         cost_estimate=cost(2 * 10**9, 5 * 10**6),
         name="prepare",
-    )(source, taps, smooths, ids)
+    )(source, taps, ids)
 
 
 def front_kernel(form, owners, orders, first_ref, second_ref, middle_ref, filter_ref, smoother_ref, hits_ref, *rest):
@@ -226,8 +226,8 @@
     return middle * power, rest
 
 
-def row_weights_kernel(form, band, own_ref, forward_ref, to_weights_ref, inverse_ref, out_ref, column_ref):
-    middle, rest = own_rows(form, own_ref, band)
+def lag_sums_kernel(form, band, own_ref, out_ref):
+    middle = own_rows(form, own_ref, band)[0]
     lane = iota((1, 128), 1)
     row = iota((128, 128), 0)
     col = iota((128, 128), 1)
@@ -242,10 +242,29 @@
         out_ref[:, d * 128 : (d + 1) * 128] = sums.astype(BF16)
         turned = further
 
+
+def lag_sums(form, band, own):
+    return pl.pallas_call(
+        partial(lag_sums_kernel, form, band),
+        out_shape=jax.ShapeDtypeStruct((form.padded, 64 * 128), BF16),
+        in_specs=[VMEM],
+        out_specs=VMEM,
+        compiler_params=params(12),
+        cost_estimate=cost(2 * 10**9, 3 * 10**6),
+        name="lag_sums",
+    )(own)
+
+
+def spectra_kernel(form, own_ref, forward_ref, to_weights_ref, inverse_ref, freq_ref, column_ref):
     window, windows = lax.axis_index("tm"), lax.axis_size("tm")
+    rows = [own_rows(form, own_ref, band) for band in range(BANDS)]
+    middle = jnp.concatenate([cells for cells, _ in rows], axis=0)
+    rest = jnp.concatenate([left for _, left in rows], axis=0)
     dot = partial(jnp.dot, precision=HIGH, preferred_element_type=F32)
+    forward = forward_ref[...]
     spectrum = dot(middle, forward_ref[0:128])
     low, high = spectrum[:, :128], spectrum[:, 128:]
+    lane = iota(low.shape, 1)
     inner = jnp.where(lane == 0, 0.0, high)
     last = jnp.where(lane == 0, high, 0.0)
     strength = jnp.concatenate([low * low + inner * inner, last * last], axis=1)
@@ -258,31 +277,34 @@
     outside = jnp.where(outside, 1.0, 0.0).astype(BF16)
     sums = jnp.dot(middle.astype(BF16), outside, preferred_element_type=F32)
     edge_sum = jnp.sum(sums * sums, axis=1, keepdims=True)
-    other = dot(sums, forward_ref[...])
+    other = dot(sums, forward)
     other_low, other_high = other[:, :128], other[:, 128:]
     cross = other_high * high
     real = other_low * low - jnp.where(lane == 0, 0.0, cross)
     imag = jnp.where(lane == 0, cross, other_low * high + other_high * low)
     edge = dot(jnp.concatenate([real, imag], axis=1), inverse_ref[...])
-    big = weights.astype(BF16)
-    out_ref[:, LAGS : LAGS + 256] = big
-    out_ref[:, LAGS + 256 : LAGS + 512] = (weights - big.astype(F32)).astype(BF16)
-    out_ref[:, LAGS + 512 : LAGS + 768] = big
-    out_ref[:, LAGS + 768 : LAGS + 1024] = edge.astype(BF16)
     factor = rest * (1.0 / (128 * 128 * NLAG))
-    column_ref[...] = jnp.where(lane == 0, edge_sum, jnp.where(lane == 1, factor, 0.0))
-
-
-def row_weights(form, band, own):
-    shapes = [((form.padded, LAGS + 1024), BF16), ((form.padded, 128), F32)]
+    column = jnp.where(lane == 0, edge_sum, jnp.where(lane == 1, factor, 0.0))
+    for band in range(BANDS):
+        cut = slice(band * form.padded, (band + 1) * form.padded)
+        big = weights[cut].astype(BF16)
+        freq_ref[band, :, 0:256] = big
+        freq_ref[band, :, 256:512] = (weights[cut] - big.astype(F32)).astype(BF16)
+        freq_ref[band, :, 512:768] = big
+        freq_ref[band, :, 768:1024] = edge[cut].astype(BF16)
+        column_ref[band] = column[cut]
+
+
+def spectra(form, own):
+    shapes = [((BANDS, form.padded, 1024), BF16), ((BANDS, form.padded, 128), F32)]
     return pl.pallas_call(
-        partial(row_weights_kernel, form, band),
+        partial(spectra_kernel, form),
         out_shape=[jax.ShapeDtypeStruct(*shape) for shape in shapes],
         in_specs=[VMEM] * 4,
         out_specs=[VMEM] * 2,
         compiler_params=params(12),
-        cost_estimate=cost(3 * 10**9, 4 * 10**6),
-        name="row_weights",
+        cost_estimate=cost(2 * 10**9, 2 * 10**6),
+        name="row_spectra",
     )(own, jnp.asarray(FORWARD), jnp.asarray(TO_WEIGHTS), jnp.asarray(INVERSE))
 
 
@@ -383,7 +405,7 @@
 
 
 def coupling_kernel(
-    form, owners, orders, lag_0, lag_1, column_0, column_1, middle_ref, extra_ref,
+    form, owners, orders, lag_0, lag_1, freq_ref, column_ref, middle_ref, extra_ref,
     first_0, second_0, first_1, second_1, factor_ref, out_ref, result, first_ref, second_ref, around_rows, near, far, near_turn, far_turn, change
 ):
     me = lax.axis_index("vert")
@@ -463,8 +485,9 @@
                 far_turn[0, 0:128] * far_turn[r, 16 * a : 16 * a + 128]
                 - near_turn[0, 0:128] * near_turn[r, 16 * a : 16 * a + 128]
             )
-        total = jnp.dot(lag_ref[rows_of], change[...], preferred_element_type=F32)
-        factors = (column_0, column_1)[band][rows_of]
+        weights = jnp.concatenate([lag_ref[rows_of], freq_ref[band, rows_of]], axis=1)
+        total = jnp.dot(weights, change[...], preferred_element_type=F32)
+        factors = column_ref[band, rows_of]
         edge_sum, own_factor = factors[:, 0:1], factors[:, 1:2]
         total += mu * mu * edge_sum
         column = iota((1, TILE), 1) + first
@@ -534,9 +557,9 @@
     orders = [bits, [bits[1], bits[0], *bits[2:]]]
     meet = [[p for i in range(k, windows - 1, 2) for p in ((i, i + 1), (i + 1, i))] for k in range(2)]
     first, second = (lax.ppermute(source, "tm", pairs) for pairs in meet)
-    taps = jnp.pad(band_taps.astype(F32).reshape(2 * BANDS, 1, TAPS), ((0, 0), (0, 0), (0, 256 - TAPS)))
-    smooths = jnp.pad(smooth_taps.astype(F32)[:, None, :], ((0, 0), (0, 0), (0, 256 - TAPS)))
-    prepared = prepare(form, owners, source, taps, smooths, parcel_ids)
+    taps = jnp.concatenate([band_taps.reshape(2 * BANDS, TAPS), smooth_taps], axis=0).astype(F32)
+    taps = jnp.pad(taps, ((0, 8 - 3 * BANDS), (0, 256 - TAPS)))
+    prepared = prepare(form, owners, source, taps, parcel_ids)
     parts = front(form, owners, orders, first, second, *prepared)
     parts = [parts[0:2], parts[2:4]]
     for step in range(len(bits) - 1):
@@ -549,7 +572,7 @@
     both = added(form, jnp.concatenate([kept, sent], axis=0), jnp.concatenate([theirs[BANDS:], theirs[:BANDS]], axis=0))
     own = both[:BANDS]
     held = [jnp.stack([both[b], both[BANDS + b]]) for b in range(BANDS)]
-    weights = [row_weights(form, 0, own), None]
+    lag = [lag_sums(form, 0, own), None]
     sides = []
 
     def send_margins(packed):
@@ -560,17 +583,18 @@
         if step:
             held = [jnp.concatenate([held[b], arrived[b]], axis=0) for b in range(BANDS)]
             if step == 1:
-                held, weights[0] = lax.optimization_barrier((held, weights[0]))
+                held, lag[0] = lax.optimization_barrier((held, lag[0]))
         else:
             packed, own = lax.optimization_barrier((margins(*held), own))
             send_margins(packed)
-            weights[1] = row_weights(form, 1, own)
-            arrived, weights[1] = lax.optimization_barrier((arrived, weights[1]))
-            send_margins(margins(*arrived))
+            lag[1] = lag_sums(form, 1, own)
+            arrived, lag[1] = lax.optimization_barrier((arrived, lag[1]))
+            packed, own = lax.optimization_barrier((margins(*arrived), own))
+            send_margins(packed)
+    freq, column = spectra(form, own)
     turned = [order[::-1] for order in orders]
     middle, extra = scaled_rows(form, owners, turned, held[0], arrived[0], held[1], arrived[1])
-    lag, column = zip(*weights)
-    done = coupling(form, owners, turned, *lag, *column, middle, extra, *sides[0], *sides[1])
+    done = coupling(form, owners, turned, *lag, freq, column, middle, extra, *sides[0], *sides[1])
     return done.transpose(1, 0, 2)[None]
 
 

time: 83.3 us -> 81.5 us (0.978)
  local copies, waits for them, and re-layouts: 3.25 us -> 1.91 us
    ppermute x4, waiting for transfers between devices: 2.71 us -> 0.56 us  [send_margins(): lax.ppermute(cells, 'tm', pairs)]
    ppermute x9, waiting for transfers between devices: 18.2 us -> 19.2 us  [swap(): return lax.ppermute(cells, 'vert', [(i, i ^ bit) for i in range(owners)])]
    ppermute x9, starting transfers between devices: 8.63 us -> 7.77 us  [swap(): return lax.ppermute(cells, 'vert', [(i, i ^ bit) for i in range(owners)])]
    pallas_call x2 -> x3, Pallas kernels: 6.54 us -> 6.58 us  [the longest x2 3.87 us: lag_sums(): pl.pallas_call(partial(lag_sums_kernel, form, band), out_shape=jax.ShapeD...]
  transfers between devices with their start and end apart: 15 -> 15, of which waited for: 6 -> 9; matrix products, arithmetic and copies ran while one was open for 2% -> 1% of each run, Pallas kernels for 13% -> 14%
where the time goes in v6:
time: 81.5 us; the launch traced here: 81.2 us
  Pallas kernels  38.3 us (47%)
  waiting for transfers between devices  20.2 us (25%)
  starting transfers between devices  19.2 us (24%)
  local copies, waits for them, and re-layouts  1.91 us (2%)
  other arithmetic  1.35 us (2%)
    pallas_call x1, Pallas kernels, coupling(): pl.pallas_call(partial(coupling_kernel, form, owners, orders), out_shape=...  23.8 us
    ppermute x9, waiting for transfers between devices, swap(): return lax.ppermute(cells, 'vert', [(i, i ^ bit) for i in range(owners)])  19.2 us
    ppermute x9, starting transfers between devices, swap(): return lax.ppermute(cells, 'vert', [(i, i ^ bit) for i in range(owners)])  7.77 us
    ppermute x4, starting transfers between devices, send_margins(): lax.ppermute(cells, 'tm', pairs)  7.72 us
    pallas_call x2, Pallas kernels, lag_sums(): pl.pallas_call(partial(lag_sums_kernel, form, band), out_shape=jax.ShapeD...  3.87 us
    ppermute x2, starting transfers between devices, local(): first, second = (lax.ppermute(source, 'tm', pairs) for pairs in meet)  3.7 us
    pallas_call x1, Pallas kernels, front(): pl.pallas_call(partial(front_kernel, form, owners, orders), out_shape=[sh...  3.4 us
    pallas_call x1, Pallas kernels, prepare(): pl.pallas_call(partial(prepare_kernel, form, owners), out_shape=[jax.Shap...  2.74 us
  transfers between devices with their start and end apart: 15, of which 9 were waited for; matrix products, arithmetic and copies ran while one was open for 1% of the time, Pallas kernels for 14%

profile of v6, /device:TPU:9, one launch (start us, length us, event | category | flops | bytes accessed | tf_op | source)
XLA Modules:
  0.0 81.2 jit_solution(4106300183689720956)
XLA Ops:
  0.0 0.7 collective-permute-start
  0.7 3.0 %collective-permute-start.1 = (bf16[1280,128]{1,0:T(8,128)(2,1)}, bf16[1280,128]{1,0:T(8,128)(2,1)S(1)}, u32[]{:S(2)}, u32[]{:S(2)}) collective-permute-start(bf16[1280,128]{1,0:T(8,128)(2,1)} %middle_ref.1), channel_id=1, source_target_pairs={{1,2},{2,1},{5,6},{6,5},{9,10},{10,9},{13,14},{14,13},{17,18},{18,... | collective-permute-start | bytes 983048 | tf_op jit(solution)/shard_map/ppermute | solution.py:559
  3.7 0.7 fusion.21.taps_ref
  4.4 1.0 %copy-done = bf16[1280,128]{1,0:T(8,128)(2,1)S(1)} copy-done((bf16[1280,128]{1,0:T(8,128)(2,1)S(1)}, bf16[1280,128]{1,0:T(8,128)(2,1)}, u32[]{:S(2)}) %copy-start) | copy-done | bytes 327704
  5.4 0.7 copy-done.1
  6.1 2.7 %prepare.1 = (bf16[1280,128]{1,0:T(8,128)(2,1)S(1)}, bf16[4,256,256]{2,1,0:T(8,128)(2,1)S(1)}, bf16[2,128,256]{2,1,0:T(8,128)(2,1)S(1)}, bf16[8,192,1280]{2,1,0:T(8,128)(2,1)S(1)}) custom-call(bf16[1280,128]{1,0:T(8,128)(2,1)S(1)} %copy-done, f32[8,256]{1,0:T(8,128)S(1)} %fusion.21.taps_ref, s32[3,1280]{1,0:T(4,128)S(1)} %copy-done.1), custom_call_target="tpu_custom_call" | custom-call | flops 2000000000 | bytes 5000000 | tf_op jit(solution)/shard_map/prepare/pallas_call | solution.py:119
  9.3 3.4 %envelope_sums.1 = (bf16[4,208,128]{2,1,0:T(8,128)(2,1)S(1)}, bf16[4,208,128]{2,1,0:T(8,128)(2,1)S(1)}, bf16[4,208,128]{2,1,0:T(8,128)(2,1)S(1)}, bf16[4,208,128]{2,1,0:T(8,128)(2,1)S(1)}) custom-call(bf16[1280,128]{1,0:T(8,128)(2,1)S(1)} %collective-permute-done.first_ref, bf16[1280,128]{1,0:T(8,128)(2,1)S(1)} %collective-permute-done.1.second_ref, ...), custom_call_target="tpu_custom_call" | custom-call | flops 3000000000 | bytes 2000000 | tf_op jit(solution)/shard_map/envelope_sums/pallas_call | solution.py:189
  12.7 1.3 %collective-permute-start.2 = (bf16[4,208,128]{2,1,0:T(8,128)(2,1)S(1)}, bf16[4,208,128]{2,1,0:T(8,128)(2,1)S(1)}, u32[]{:S(2)}, u32[]{:S(2)}) collective-permute-start(bf16[4,208,128]{2,1,0:T(8,128)(2,1)S(1)} %get-tuple-element.38), channel_id=1, source_target_pairs={{0,4},{4,0},{8,12},{12,8},{16,20},{20,16},{24,28},{28,24},{1,5},{5... | collective-permute-start | bytes 638984 | tf_op jit(solution)/shard_map/ppermute | solution.py:549
  14.1 3.3 %collective-permute-done.2 = bf16[4,208,128]{2,1,0:T(8,128)(2,1)S(1)} collective-permute-done((bf16[4,208,128]{2,1,0:T(8,128)(2,1)S(1)}, bf16[4,208,128]{2,1,0:T(8,128)(2,1)S(1)}, u32[]{:S(2)}, u32[]{:S(2)}) %collective-permute-start.2) | collective-permute-done | bytes 213024 | tf_op jit(solution)/shard_map/ppermute | solution.py:549
  17.5 1.4 %collective-permute-done.4 = bf16[4,208,128]{2,1,0:T(8,128)(2,1)S(1)} collective-permute-done((bf16[4,208,128]{2,1,0:T(8,128)(2,1)S(1)}, bf16[4,208,128]{2,1,0:T(8,128)(2,1)S(1)}, u32[]{:S(2)}, u32[]{:S(2)}) %collective-permute-start.4) | collective-permute-done | bytes 213024 | tf_op jit(solution)/shard_map/ppermute | solution.py:549
  19.6 3.7 %collective-permute-done.3 = bf16[2,208,128]{2,1,0:T(8,128)(2,1)S(1)} collective-permute-done((bf16[2,208,128]{2,1,0:T(8,128)(2,1)S(1)}, bf16[2,208,128]{2,1,0:T(8,128)(2,1)S(1)}, u32[]{:S(2)}, u32[]{:S(2)}) %collective-permute-start.3) | collective-permute-done | bytes 106528 | tf_op jit(solution)/shard_map/ppermute | solution.py:549
  23.8 2.4 %collective-permute-start.6 = (bf16[4,208,128]{2,1,0:T(8,128)(2,1)S(1)}, bf16[4,208,128]{2,1,0:T(8,128)(2,1)S(1)}, u32[]{:S(2)}, u32[]{:S(2)}) collective-permute-start(bf16[4,208,128]{2,1,0:T(8,128)(2,1)S(1)} %pad_maximum_fusion.2), channel_id=1, source_target_pairs={{0,16},{4,20},{8,24},{12,28},{16,0},{20,4},{24,8},{28,12},{1,17},{... | collective-permute-start | bytes 638984 | tf_op jit(solution)/shard_map/ppermute | solution.py:549
  26.2 9.2 %collective-permute-done.6 = bf16[4,208,128]{2,1,0:T(8,128)(2,1)S(1)} collective-permute-done((bf16[4,208,128]{2,1,0:T(8,128)(2,1)S(1)}, bf16[4,208,128]{2,1,0:T(8,128)(2,1)S(1)}, u32[]{:S(2)}, u32[]{:S(2)}) %collective-permute-start.6) | collective-permute-done | bytes 213024 | tf_op jit(solution)/shard_map/ppermute | solution.py:549
  35.6 2.5 %collective-permute-start.7 = (bf16[2,208,128]{2,1,0:T(8,128)(2,1)S(1)}, bf16[2,208,128]{2,1,0:T(8,128)(2,1)S(1)}, u32[]{:S(2)}, u32[]{:S(2)}) collective-permute-start(bf16[2,208,128]{2,1,0:T(8,128)(2,1)S(1)} %pad_maximum_fusion.8), channel_id=1, source_target_pairs={{0,8},{4,12},{8,0},{12,4},{16,24},{20,28},{24,16},{28,20},{1,9},{5... | collective-permute-start | bytes 319496 | tf_op jit(solution)/shard_map/ppermute | solution.py:549
  38.4 1.9 %lag_sums.2.lag_0 = bf16[192,8192]{1,0:T(8,128)(2,1)S(1)} custom-call(bf16[2,208,128]{2,1,0:T(8,128)(2,1)S(1)} %slice.154.own_ref), custom_call_target="tpu_custom_call" | custom-call | flops 2000000000 | bytes 3000000 | tf_op jit(solution)/shard_map/lag_sums/pallas_call | solution.py:247
  40.3 0.8 collective-permute-done.7
  42.8 1.9 %collective-permute-start.11 = (bf16[4,208,128]{2,1,0:T(8,128)(2,1)S(1)}, bf16[4,208,128]{2,1,0:T(8,128)(2,1)S(1)}, u32[]{:S(2)}, u32[]{:S(2)}) collective-permute-start(bf16[4,208,128]{2,1,0:T(8,128)(2,1)S(1)} %get-tuple-element.57), channel_id=1, source_target_pairs={{0,1},{1,0},{2,3},{3,2},{4,5},{5,4},{6,7},{7,6},{8,9},{9,8},{10,11... | collective-permute-start | bytes 638984 | tf_op jit(solution)/shard_map/ppermute | solution.py:579
  44.7 1.9 %collective-permute-start.12 = (bf16[4,208,128]{2,1,0:T(8,128)(2,1)S(1)}, bf16[4,208,128]{2,1,0:T(8,128)(2,1)S(1)}, u32[]{:S(2)}, u32[]{:S(2)}) collective-permute-start(bf16[4,208,128]{2,1,0:T(8,128)(2,1)S(1)} %get-tuple-element.58), channel_id=1, source_target_pairs={{1,2},{2,1},{5,6},{6,5},{9,10},{10,9},{13,14},{14,13},{17,18},{18,... | collective-permute-start | bytes 638984 | tf_op jit(solution)/shard_map/ppermute | solution.py:579
  46.6 1.9 %lag_sums.3.lag_1 = bf16[192,8192]{1,0:T(8,128)(2,1)S(1)} custom-call(bf16[2,208,128]{2,1,0:T(8,128)(2,1)S(1)} %slice.154.own_ref), custom_call_target="tpu_custom_call" | custom-call | flops 2000000000 | bytes 3000000 | tf_op jit(solution)/shard_map/lag_sums/pallas_call | solution.py:247
  48.8 1.4 %collective-permute-start.13 = (bf16[4,208,128]{2,1,0:T(8,128)(2,1)S(1)}, bf16[4,208,128]{2,1,0:T(8,128)(2,1)S(1)}, u32[]{:S(2)}, u32[]{:S(2)}) collective-permute-start(bf16[4,208,128]{2,1,0:T(8,128)(2,1)S(1)} %get-tuple-element.59), channel_id=1, source_target_pairs={{0,1},{1,0},{2,3},{3,2},{4,5},{5,4},{6,7},{7,6},{8,9},{9,8},{10,11... | collective-permute-start | bytes 638984 | tf_op jit(solution)/shard_map/ppermute | solution.py:579
  50.3 2.5 %collective-permute-start.14 = (bf16[4,208,128]{2,1,0:T(8,128)(2,1)S(1)}, bf16[4,208,128]{2,1,0:T(8,128)(2,1)S(1)}, u32[]{:S(2)}, u32[]{:S(2)}) collective-permute-start(bf16[4,208,128]{2,1,0:T(8,128)(2,1)S(1)} %get-tuple-element.60), channel_id=1, source_target_pairs={{1,2},{2,1},{5,6},{6,5},{9,10},{10,9},{13,14},{14,13},{17,18},{18,... | collective-permute-start | bytes 638984 | tf_op jit(solution)/shard_map/ppermute | solution.py:579
  52.8 1.3 %scaled_rows.1 = (f32[2,1536,128]{2,1,0:T(8,128)S(1)}, f32[2,1536,128]{2,1,0:T(8,128)S(1)}) custom-call(bf16[4,208,128]{2,1,0:T(8,128)(2,1)S(1)} %pad_maximum_fusion.4.refs_0_.near_0, bf16[4,208,128]{2,1,0:T(8,128)(2,1)S(1)} %collective-permute-done.9.refs_0_.far_0, bf16[4,208,128]{2,1,0:T(8,128)(2,1)S(1)} %pad_maximum_fusion.5.refs_1_.near_1, ...), custom_call_target="tpu_custom_call" | custom-call | flops 1000000000 | bytes 4000000 | tf_op jit(solution)/shard_map/scaled_rows/pallas_call | solution.py:371
  54.1 2.7 %row_spectra.1 = (bf16[2,192,1024]{2,1,0:T(8,128)(2,1)S(1)}, f32[2,192,128]{2,1,0:T(8,128)S(1)}) custom-call(bf16[2,208,128]{2,1,0:T(8,128)(2,1)S(1)} %slice.154.own_ref, f32[256,256]{1,0:T(8,128)S(1)} %copy-done.5, f32[256,256]{1,0:T(8,128)S(1)} %copy-done.4, f32[256,256]{1,0:T(8,128)S(1)} %copy-done.3), custom_call_target="tpu_custom_call" | custom-call | flops 2000000000 | bytes 2000000 | tf_op jit(solution)/shard_map/row_spectra/pallas_call | solution.py:300
  57.4 23.8 %coupling.1 = f32[188,2,1504]{2,1,0:T(2,128)} custom-call(bf16[192,8192]{1,0:T(8,128)(2,1)S(1)} %lag_sums.2.lag_0, bf16[192,8192]{1,0:T(8,128)(2,1)S(1)} %lag_sums.3.lag_1, bf16[2,192,1024]{2,1,0:T(8,128)(2,1)S(1)} %get-tuple-element.53.freq_ref, f32[2,192,128]{2,1,0:T(8,128)S(1)} %get-tuple-element.54.column_ref, ...), custom_call_target="tpu_custom_call" | custom-call | flops 16000000000 | bytes 10000000 | tf_op jit(solution)/shard_map/coupling/pallas_call | solution.py:526
  (58 shorter events, 4.8 us)
Async XLA Ops:
  0.0 8.9 %collective-permute-start = (bf16[1280,128]{1,0:T(8,128)(2,1)}, bf16[1280,128]{1,0:T(8,128)(2,1)S(1)}, u32[]{:S(2)}, u32[]{:S(2)}) collective-permute-start(bf16[1280,128]{1,0:T(8,128)(2,1)} %middle_ref.1), channel_id=1, source_target_pairs={{0,1},{1,0},{2,3},{3,2},{4,5},{5,4},{6,7},{7,6},{8,9},{9,8},{10,11... | collective-permute-start | bytes 983048 | tf_op jit(solution)/shard_map/ppermute | solution.py:559
  0.7 8.6 %collective-permute-start.1 = (bf16[1280,128]{1,0:T(8,128)(2,1)}, bf16[1280,128]{1,0:T(8,128)(2,1)S(1)}, u32[]{:S(2)}, u32[]{:S(2)}) collective-permute-start(bf16[1280,128]{1,0:T(8,128)(2,1)} %middle_ref.1), channel_id=1, source_target_pairs={{1,2},{2,1},{5,6},{6,5},{9,10},{10,9},{13,14},{14,13},{17,18},{18,... | collective-permute-start | bytes 983048 | tf_op jit(solution)/shard_map/ppermute | solution.py:559
  4.4 1.0 %copy-start = (bf16[1280,128]{1,0:T(8,128)(2,1)S(1)}, bf16[1280,128]{1,0:T(8,128)(2,1)}, u32[]{:S(2)}) copy-start(bf16[1280,128]{1,0:T(8,128)(2,1)} %middle_ref.1) | copy-start | bytes 983044
  5.4 0.7 copy-start.1
  12.7 4.8 %collective-permute-start.2 = (bf16[4,208,128]{2,1,0:T(8,128)(2,1)S(1)}, bf16[4,208,128]{2,1,0:T(8,128)(2,1)S(1)}, u32[]{:S(2)}, u32[]{:S(2)}) collective-permute-start(bf16[4,208,128]{2,1,0:T(8,128)(2,1)S(1)} %get-tuple-element.38), channel_id=1, source_target_pairs={{0,4},{4,0},{8,12},{12,8},{16,20},{20,16},{24,28},{28,24},{1,5},{5... | collective-permute-start | bytes 638984 | tf_op jit(solution)/shard_map/ppermute | solution.py:549
  14.0 5.0 %collective-permute-start.4 = (bf16[4,208,128]{2,1,0:T(8,128)(2,1)S(1)}, bf16[4,208,128]{2,1,0:T(8,128)(2,1)S(1)}, u32[]{:S(2)}, u32[]{:S(2)}) collective-permute-start(bf16[4,208,128]{2,1,0:T(8,128)(2,1)S(1)} %get-tuple-element.40), channel_id=1, source_target_pairs={{0,8},{4,12},{8,0},{12,4},{16,24},{20,28},{24,16},{28,20},{1,9},{5... | collective-permute-start | bytes 638984 | tf_op jit(solution)/shard_map/ppermute | solution.py:549
  19.2 4.1 %collective-permute-start.3 = (bf16[2,208,128]{2,1,0:T(8,128)(2,1)S(1)}, bf16[2,208,128]{2,1,0:T(8,128)(2,1)S(1)}, u32[]{:S(2)}, u32[]{:S(2)}) collective-permute-start(bf16[2,208,128]{2,1,0:T(8,128)(2,1)S(1)} %slice.129), channel_id=1, source_target_pairs={{0,8},{4,12},{8,0},{12,4},{16,24},{20,28},{24,16},{28,20},{1,9},{5... | collective-permute-start | bytes 319496 | tf_op jit(solution)/shard_map/ppermute | solution.py:549
  19.4 4.1 %collective-permute-start.5 = (bf16[2,208,128]{2,1,0:T(8,128)(2,1)S(1)}, bf16[2,208,128]{2,1,0:T(8,128)(2,1)S(1)}, u32[]{:S(2)}, u32[]{:S(2)}) collective-permute-start(bf16[2,208,128]{2,1,0:T(8,128)(2,1)S(1)} %slice.138), channel_id=1, source_target_pairs={{0,4},{4,0},{8,12},{12,8},{16,20},{20,16},{24,28},{28,24},{1,5},{5... | collective-permute-start | bytes 319496 | tf_op jit(solution)/shard_map/ppermute | solution.py:549
  23.8 11.6 %collective-permute-start.6 = (bf16[4,208,128]{2,1,0:T(8,128)(2,1)S(1)}, bf16[4,208,128]{2,1,0:T(8,128)(2,1)S(1)}, u32[]{:S(2)}, u32[]{:S(2)}) collective-permute-start(bf16[4,208,128]{2,1,0:T(8,128)(2,1)S(1)} %pad_maximum_fusion.2), channel_id=1, source_target_pairs={{0,16},{4,20},{8,24},{12,28},{16,0},{20,4},{24,8},{28,12},{1,17},{... | collective-permute-start | bytes 638984 | tf_op jit(solution)/shard_map/ppermute | solution.py:549
  35.6 5.4 %collective-permute-start.7 = (bf16[2,208,128]{2,1,0:T(8,128)(2,1)S(1)}, bf16[2,208,128]{2,1,0:T(8,128)(2,1)S(1)}, u32[]{:S(2)}, u32[]{:S(2)}) collective-permute-start(bf16[2,208,128]{2,1,0:T(8,128)(2,1)S(1)} %pad_maximum_fusion.8), channel_id=1, source_target_pairs={{0,8},{4,12},{8,0},{12,4},{16,24},{20,28},{24,16},{28,20},{1,9},{5... | collective-permute-start | bytes 319496 | tf_op jit(solution)/shard_map/ppermute | solution.py:549
  38.1 3.6 %collective-permute-start.8 = (bf16[2,208,128]{2,1,0:T(8,128)(2,1)S(1)}, bf16[2,208,128]{2,1,0:T(8,128)(2,1)S(1)}, u32[]{:S(2)}, u32[]{:S(2)}) collective-permute-start(bf16[2,208,128]{2,1,0:T(8,128)(2,1)S(1)} %pad_maximum_fusion.9), channel_id=1, source_target_pairs={{0,4},{4,0},{8,12},{12,8},{16,20},{20,16},{24,28},{28,24},{1,5},{5... | collective-permute-start | bytes 319496 | tf_op jit(solution)/shard_map/ppermute | solution.py:549
  41.8 6.8 %collective-permute-start.9 = (bf16[4,208,128]{2,1,0:T(8,128)(2,1)S(1)}, bf16[4,208,128]{2,1,0:T(8,128)(2,1)S(1)}, u32[]{:S(2)}, u32[]{:S(2)}) collective-permute-start(bf16[4,208,128]{2,1,0:T(8,128)(2,1)S(1)} %pad_maximum_fusion.4.refs_0_.near_0), channel_id=1, source_target_pairs={{0,4},{4,0},{8,12},{12,8},{16,20},{20,16},{24,28},{28,24},{1,5},{5... | collective-permute-start | bytes 638984 | tf_op jit(solution)/shard_map/ppermute | solution.py:549
  42.0 6.6 %collective-permute-start.10 = (bf16[4,208,128]{2,1,0:T(8,128)(2,1)S(1)}, bf16[4,208,128]{2,1,0:T(8,128)(2,1)S(1)}, u32[]{:S(2)}, u32[]{:S(2)}) collective-permute-start(bf16[4,208,128]{2,1,0:T(8,128)(2,1)S(1)} %pad_maximum_fusion.5.refs_1_.near_1), channel_id=1, source_target_pairs={{0,8},{4,12},{8,0},{12,4},{16,24},{20,28},{24,16},{28,20},{1,9},{5... | collective-permute-start | bytes 638984 | tf_op jit(solution)/shard_map/ppermute | solution.py:549
  42.8 14.1 %collective-permute-start.11 = (bf16[4,208,128]{2,1,0:T(8,128)(2,1)S(1)}, bf16[4,208,128]{2,1,0:T(8,128)(2,1)S(1)}, u32[]{:S(2)}, u32[]{:S(2)}) collective-permute-start(bf16[4,208,128]{2,1,0:T(8,128)(2,1)S(1)} %get-tuple-element.57), channel_id=1, source_target_pairs={{0,1},{1,0},{2,3},{3,2},{4,5},{5,4},{6,7},{7,6},{8,9},{9,8},{10,11... | collective-permute-start | bytes 638984 | tf_op jit(solution)/shard_map/ppermute | solution.py:579
  44.7 12.2 %collective-permute-start.12 = (bf16[4,208,128]{2,1,0:T(8,128)(2,1)S(1)}, bf16[4,208,128]{2,1,0:T(8,128)(2,1)S(1)}, u32[]{:S(2)}, u32[]{:S(2)}) collective-permute-start(bf16[4,208,128]{2,1,0:T(8,128)(2,1)S(1)} %get-tuple-element.58), channel_id=1, source_target_pairs={{1,2},{2,1},{5,6},{6,5},{9,10},{10,9},{13,14},{14,13},{17,18},{18,... | collective-permute-start | bytes 638984 | tf_op jit(solution)/shard_map/ppermute | solution.py:579
  48.6 5.5 %copy-start.3 = (f32[256,256]{1,0:T(8,128)S(1)}, f32[256,256]{1,0:T(8,128)}, u32[]{:S(2)}) copy-start(f32[256,256]{1,0:T(8,128)} %constant.22.clone.inverse_ref) | copy-start | bytes 786436
  48.6 5.5 %copy-start.4 = (f32[256,256]{1,0:T(8,128)S(1)}, f32[256,256]{1,0:T(8,128)}, u32[]{:S(2)}) copy-start(f32[256,256]{1,0:T(8,128)} %constant.21.clone.to_weights_ref) | copy-start | bytes 786436
  48.6 5.5 %copy-start.5 = (f32[256,256]{1,0:T(8,128)S(1)}, f32[256,256]{1,0:T(8,128)}, u32[]{:S(2)}) copy-start(f32[256,256]{1,0:T(8,128)} %constant.20.clone.forward_ref) | copy-start | bytes 786436
  48.8 8.0 %collective-permute-start.13 = (bf16[4,208,128]{2,1,0:T(8,128)(2,1)S(1)}, bf16[4,208,128]{2,1,0:T(8,128)(2,1)S(1)}, u32[]{:S(2)}, u32[]{:S(2)}) collective-permute-start(bf16[4,208,128]{2,1,0:T(8,128)(2,1)S(1)} %get-tuple-element.59), channel_id=1, source_target_pairs={{0,1},{1,0},{2,3},{3,2},{4,5},{5,4},{6,7},{7,6},{8,9},{9,8},{10,11... | collective-permute-start | bytes 638984 | tf_op jit(solution)/shard_map/ppermute | solution.py:579
  50.3 7.2 %collective-permute-start.14 = (bf16[4,208,128]{2,1,0:T(8,128)(2,1)S(1)}, bf16[4,208,128]{2,1,0:T(8,128)(2,1)S(1)}, u32[]{:S(2)}, u32[]{:S(2)}) collective-permute-start(bf16[4,208,128]{2,1,0:T(8,128)(2,1)S(1)} %get-tuple-element.60), channel_id=1, source_target_pairs={{1,2},{2,1},{5,6},{6,5},{9,10},{10,9},{13,14},{14,13},{17,18},{18,... | collective-permute-start | bytes 638984 | tf_op jit(solution)/shard_map/ppermute | solution.py:579
  54.1 3.3 %copy-start.2 = (bf16[512,512]{1,0:T(8,128)(2,1)S(1)}, bf16[512,512]{1,0:T(8,128)(2,1)}, u32[]{:S(2)}) copy-start(bf16[512,512]{1,0:T(8,128)(2,1)} %constant.23.clone.factor_ref) | copy-start | bytes 1572868

commit v7 on v6

--- a/solution.py
+++ b/solution.py
@@ -479,12 +479,14 @@
         for r in range(16):
             near_turn[r] = near[r : r + 176].astype(BF16)
             far_turn[r] = far[r : r + 176].astype(BF16)
-        for d in range(64):
-            a, r = divmod(d, 16)
-            change[d * 128 : (d + 1) * 128] = (
-                far_turn[0, 0:128] * far_turn[r, 16 * a : 16 * a + 128]
-                - near_turn[0, 0:128] * near_turn[r, 16 * a : 16 * a + 128]
-            )
+        for h in (0, 64):
+            far_0, near_0 = far_turn[0, h : h + 64], near_turn[0, h : h + 64]
+            for d in range(64):
+                a, r = divmod(d, 16)
+                shift = slice(16 * a + h, 16 * a + h + 64)
+                change[d * 128 + h : d * 128 + h + 64] = (
+                    far_0 * far_turn[r, shift] - near_0 * near_turn[r, shift]
+                )
         weights = jnp.concatenate([lag_ref[rows_of], freq_ref[band, rows_of]], axis=1)
         total = jnp.dot(weights, change[...], preferred_element_type=F32)
         factors = column_ref[band, rows_of]
@@ -507,10 +509,11 @@
         )
         low, high = jnp.where(coarse, 0, fold), jnp.where(fine, tiles, fold)
         cut = SPLIT % form.rows
-        if form.padded - 128 <= cut <= 128:
+        if form.padded > 128 and cut:
             mixed = coarse & fine
-            run(0, jnp.where(mixed, fold, 0), 0, 128)
-            run(jnp.where(mixed, fold, tiles), tiles, form.padded - 128, 128)
+            run(0, jnp.where(mixed, fold, 0), 0, (cut + 31) // 32 * 32)
+            upper = cut // 32 * 32
+            run(jnp.where(mixed, fold, tiles), tiles, upper, form.padded - upper)
             low = jnp.where(mixed, high, low)
         run(low, high, 0, form.padded)
     total = owners * form.rows

time: 81.5 us -> 81.4 us (level)
  no operation moved by 1% of the time
where the time goes in v7:
time: 81.4 us; the launch traced here: 81.1 us
  Pallas kernels  38.2 us (47%)
  waiting for transfers between devices  20.2 us (25%)
  starting transfers between devices  19.2 us (24%)
  local copies, waits for them, and re-layouts  1.91 us (2%)
  other arithmetic  1.35 us (2%)
    pallas_call x1, Pallas kernels, coupling(): pl.pallas_call(partial(coupling_kernel, form, owners, orders), out_shape=...  23.7 us
    ppermute x9, waiting for transfers between devices, swap(): return lax.ppermute(cells, 'vert', [(i, i ^ bit) for i in range(owners)])  19.2 us
    ppermute x9, starting transfers between devices, swap(): return lax.ppermute(cells, 'vert', [(i, i ^ bit) for i in range(owners)])  7.77 us
    ppermute x4, starting transfers between devices, send_margins(): lax.ppermute(cells, 'tm', pairs)  7.72 us
    pallas_call x2, Pallas kernels, lag_sums(): pl.pallas_call(partial(lag_sums_kernel, form, band), out_shape=jax.ShapeD...  3.87 us
    ppermute x2, starting transfers between devices, local(): first, second = (lax.ppermute(source, 'tm', pairs) for pairs in meet)  3.7 us
    pallas_call x1, Pallas kernels, front(): pl.pallas_call(partial(front_kernel, form, owners, orders), out_shape=[sh...  3.4 us
    pallas_call x1, Pallas kernels, prepare(): pl.pallas_call(partial(prepare_kernel, form, owners), out_shape=[jax.Shap...  2.74 us
  transfers between devices with their start and end apart: 15, of which 9 were waited for; matrix products, arithmetic and copies ran while one was open for 1% of the time, Pallas kernels for 14%

profile of v7, /device:TPU:9, one launch (start us, length us, event | category | flops | bytes accessed | tf_op | source)
XLA Modules:
  0.0 81.1 jit_solution(18166184143976031693)
XLA Ops:
  0.0 0.7 collective-permute-start
  0.7 3.0 %collective-permute-start.1 = (bf16[1280,128]{1,0:T(8,128)(2,1)}, bf16[1280,128]{1,0:T(8,128)(2,1)S(1)}, u32[]{:S(2)}, u32[]{:S(2)}) collective-permute-start(bf16[1280,128]{1,0:T(8,128)(2,1)} %middle_ref.1), channel_id=1, source_target_pairs={{1,2},{2,1},{5,6},{6,5},{9,10},{10,9},{13,14},{14,13},{17,18},{18,... | collective-permute-start | bytes 983048 | tf_op jit(solution)/shard_map/ppermute | solution.py:562
  3.7 0.7 fusion.21.taps_ref
  4.4 1.0 %copy-done = bf16[1280,128]{1,0:T(8,128)(2,1)S(1)} copy-done((bf16[1280,128]{1,0:T(8,128)(2,1)S(1)}, bf16[1280,128]{1,0:T(8,128)(2,1)}, u32[]{:S(2)}) %copy-start) | copy-done | bytes 327704
  5.4 0.7 copy-done.1
  6.1 2.7 %prepare.1 = (bf16[1280,128]{1,0:T(8,128)(2,1)S(1)}, bf16[4,256,256]{2,1,0:T(8,128)(2,1)S(1)}, bf16[2,128,256]{2,1,0:T(8,128)(2,1)S(1)}, bf16[8,192,1280]{2,1,0:T(8,128)(2,1)S(1)}) custom-call(bf16[1280,128]{1,0:T(8,128)(2,1)S(1)} %copy-done, f32[8,256]{1,0:T(8,128)S(1)} %fusion.21.taps_ref, s32[3,1280]{1,0:T(4,128)S(1)} %copy-done.1), custom_call_target="tpu_custom_call" | custom-call | flops 2000000000 | bytes 5000000 | tf_op jit(solution)/shard_map/prepare/pallas_call | solution.py:119
  9.3 3.4 %envelope_sums.1 = (bf16[4,208,128]{2,1,0:T(8,128)(2,1)S(1)}, bf16[4,208,128]{2,1,0:T(8,128)(2,1)S(1)}, bf16[4,208,128]{2,1,0:T(8,128)(2,1)S(1)}, bf16[4,208,128]{2,1,0:T(8,128)(2,1)S(1)}) custom-call(bf16[1280,128]{1,0:T(8,128)(2,1)S(1)} %collective-permute-done.first_ref, bf16[1280,128]{1,0:T(8,128)(2,1)S(1)} %collective-permute-done.1.second_ref, ...), custom_call_target="tpu_custom_call" | custom-call | flops 3000000000 | bytes 2000000 | tf_op jit(solution)/shard_map/envelope_sums/pallas_call | solution.py:189
  12.7 1.3 %collective-permute-start.2 = (bf16[4,208,128]{2,1,0:T(8,128)(2,1)S(1)}, bf16[4,208,128]{2,1,0:T(8,128)(2,1)S(1)}, u32[]{:S(2)}, u32[]{:S(2)}) collective-permute-start(bf16[4,208,128]{2,1,0:T(8,128)(2,1)S(1)} %get-tuple-element.38), channel_id=1, source_target_pairs={{0,4},{4,0},{8,12},{12,8},{16,20},{20,16},{24,28},{28,24},{1,5},{5... | collective-permute-start | bytes 638984 | tf_op jit(solution)/shard_map/ppermute | solution.py:552
  14.1 3.3 %collective-permute-done.2 = bf16[4,208,128]{2,1,0:T(8,128)(2,1)S(1)} collective-permute-done((bf16[4,208,128]{2,1,0:T(8,128)(2,1)S(1)}, bf16[4,208,128]{2,1,0:T(8,128)(2,1)S(1)}, u32[]{:S(2)}, u32[]{:S(2)}) %collective-permute-start.2) | collective-permute-done | bytes 213024 | tf_op jit(solution)/shard_map/ppermute | solution.py:552
  17.5 1.4 %collective-permute-done.4 = bf16[4,208,128]{2,1,0:T(8,128)(2,1)S(1)} collective-permute-done((bf16[4,208,128]{2,1,0:T(8,128)(2,1)S(1)}, bf16[4,208,128]{2,1,0:T(8,128)(2,1)S(1)}, u32[]{:S(2)}, u32[]{:S(2)}) %collective-permute-start.4) | collective-permute-done | bytes 213024 | tf_op jit(solution)/shard_map/ppermute | solution.py:552
  19.6 3.7 %collective-permute-done.3 = bf16[2,208,128]{2,1,0:T(8,128)(2,1)S(1)} collective-permute-done((bf16[2,208,128]{2,1,0:T(8,128)(2,1)S(1)}, bf16[2,208,128]{2,1,0:T(8,128)(2,1)S(1)}, u32[]{:S(2)}, u32[]{:S(2)}) %collective-permute-start.3) | collective-permute-done | bytes 106528 | tf_op jit(solution)/shard_map/ppermute | solution.py:552
  23.8 2.4 %collective-permute-start.6 = (bf16[4,208,128]{2,1,0:T(8,128)(2,1)S(1)}, bf16[4,208,128]{2,1,0:T(8,128)(2,1)S(1)}, u32[]{:S(2)}, u32[]{:S(2)}) collective-permute-start(bf16[4,208,128]{2,1,0:T(8,128)(2,1)S(1)} %pad_maximum_fusion.2), channel_id=1, source_target_pairs={{0,16},{4,20},{8,24},{12,28},{16,0},{20,4},{24,8},{28,12},{1,17},{... | collective-permute-start | bytes 638984 | tf_op jit(solution)/shard_map/ppermute | solution.py:552
  26.2 9.2 %collective-permute-done.6 = bf16[4,208,128]{2,1,0:T(8,128)(2,1)S(1)} collective-permute-done((bf16[4,208,128]{2,1,0:T(8,128)(2,1)S(1)}, bf16[4,208,128]{2,1,0:T(8,128)(2,1)S(1)}, u32[]{:S(2)}, u32[]{:S(2)}) %collective-permute-start.6) | collective-permute-done | bytes 213024 | tf_op jit(solution)/shard_map/ppermute | solution.py:552
  35.6 2.5 %collective-permute-start.7 = (bf16[2,208,128]{2,1,0:T(8,128)(2,1)S(1)}, bf16[2,208,128]{2,1,0:T(8,128)(2,1)S(1)}, u32[]{:S(2)}, u32[]{:S(2)}) collective-permute-start(bf16[2,208,128]{2,1,0:T(8,128)(2,1)S(1)} %pad_maximum_fusion.8), channel_id=1, source_target_pairs={{0,8},{4,12},{8,0},{12,4},{16,24},{20,28},{24,16},{28,20},{1,9},{5... | collective-permute-start | bytes 319496 | tf_op jit(solution)/shard_map/ppermute | solution.py:552
  38.4 1.9 %lag_sums.2.lag_0 = bf16[192,8192]{1,0:T(8,128)(2,1)S(1)} custom-call(bf16[2,208,128]{2,1,0:T(8,128)(2,1)S(1)} %slice.154.own_ref), custom_call_target="tpu_custom_call" | custom-call | flops 2000000000 | bytes 3000000 | tf_op jit(solution)/shard_map/lag_sums/pallas_call | solution.py:247
  40.3 0.8 collective-permute-done.7
  42.8 1.9 %collective-permute-start.11 = (bf16[4,208,128]{2,1,0:T(8,128)(2,1)S(1)}, bf16[4,208,128]{2,1,0:T(8,128)(2,1)S(1)}, u32[]{:S(2)}, u32[]{:S(2)}) collective-permute-start(bf16[4,208,128]{2,1,0:T(8,128)(2,1)S(1)} %get-tuple-element.57), channel_id=1, source_target_pairs={{0,1},{1,0},{2,3},{3,2},{4,5},{5,4},{6,7},{7,6},{8,9},{9,8},{10,11... | collective-permute-start | bytes 638984 | tf_op jit(solution)/shard_map/ppermute | solution.py:582
  44.7 1.9 %collective-permute-start.12 = (bf16[4,208,128]{2,1,0:T(8,128)(2,1)S(1)}, bf16[4,208,128]{2,1,0:T(8,128)(2,1)S(1)}, u32[]{:S(2)}, u32[]{:S(2)}) collective-permute-start(bf16[4,208,128]{2,1,0:T(8,128)(2,1)S(1)} %get-tuple-element.58), channel_id=1, source_target_pairs={{1,2},{2,1},{5,6},{6,5},{9,10},{10,9},{13,14},{14,13},{17,18},{18,... | collective-permute-start | bytes 638984 | tf_op jit(solution)/shard_map/ppermute | solution.py:582
  46.6 1.9 %lag_sums.3.lag_1 = bf16[192,8192]{1,0:T(8,128)(2,1)S(1)} custom-call(bf16[2,208,128]{2,1,0:T(8,128)(2,1)S(1)} %slice.154.own_ref), custom_call_target="tpu_custom_call" | custom-call | flops 2000000000 | bytes 3000000 | tf_op jit(solution)/shard_map/lag_sums/pallas_call | solution.py:247
  48.8 1.4 %collective-permute-start.13 = (bf16[4,208,128]{2,1,0:T(8,128)(2,1)S(1)}, bf16[4,208,128]{2,1,0:T(8,128)(2,1)S(1)}, u32[]{:S(2)}, u32[]{:S(2)}) collective-permute-start(bf16[4,208,128]{2,1,0:T(8,128)(2,1)S(1)} %get-tuple-element.59), channel_id=1, source_target_pairs={{0,1},{1,0},{2,3},{3,2},{4,5},{5,4},{6,7},{7,6},{8,9},{9,8},{10,11... | collective-permute-start | bytes 638984 | tf_op jit(solution)/shard_map/ppermute | solution.py:582
  50.3 2.5 %collective-permute-start.14 = (bf16[4,208,128]{2,1,0:T(8,128)(2,1)S(1)}, bf16[4,208,128]{2,1,0:T(8,128)(2,1)S(1)}, u32[]{:S(2)}, u32[]{:S(2)}) collective-permute-start(bf16[4,208,128]{2,1,0:T(8,128)(2,1)S(1)} %get-tuple-element.60), channel_id=1, source_target_pairs={{1,2},{2,1},{5,6},{6,5},{9,10},{10,9},{13,14},{14,13},{17,18},{18,... | collective-permute-start | bytes 638984 | tf_op jit(solution)/shard_map/ppermute | solution.py:582
  52.8 1.3 %scaled_rows.1 = (f32[2,1536,128]{2,1,0:T(8,128)S(1)}, f32[2,1536,128]{2,1,0:T(8,128)S(1)}) custom-call(bf16[4,208,128]{2,1,0:T(8,128)(2,1)S(1)} %pad_maximum_fusion.4.refs_0_.near_0, bf16[4,208,128]{2,1,0:T(8,128)(2,1)S(1)} %collective-permute-done.9.refs_0_.far_0, bf16[4,208,128]{2,1,0:T(8,128)(2,1)S(1)} %pad_maximum_fusion.5.refs_1_.near_1, ...), custom_call_target="tpu_custom_call" | custom-call | flops 1000000000 | bytes 4000000 | tf_op jit(solution)/shard_map/scaled_rows/pallas_call | solution.py:371
  54.1 2.7 %row_spectra.1 = (bf16[2,192,1024]{2,1,0:T(8,128)(2,1)S(1)}, f32[2,192,128]{2,1,0:T(8,128)S(1)}) custom-call(bf16[2,208,128]{2,1,0:T(8,128)(2,1)S(1)} %slice.154.own_ref, f32[256,256]{1,0:T(8,128)S(1)} %copy-done.5, f32[256,256]{1,0:T(8,128)S(1)} %copy-done.4, f32[256,256]{1,0:T(8,128)S(1)} %copy-done.3), custom_call_target="tpu_custom_call" | custom-call | flops 2000000000 | bytes 2000000 | tf_op jit(solution)/shard_map/row_spectra/pallas_call | solution.py:300
  57.4 23.7 %coupling.1 = f32[188,2,1504]{2,1,0:T(2,128)} custom-call(bf16[192,8192]{1,0:T(8,128)(2,1)S(1)} %lag_sums.2.lag_0, bf16[192,8192]{1,0:T(8,128)(2,1)S(1)} %lag_sums.3.lag_1, bf16[2,192,1024]{2,1,0:T(8,128)(2,1)S(1)} %get-tuple-element.53.freq_ref, f32[2,192,128]{2,1,0:T(8,128)S(1)} %get-tuple-element.54.column_ref, ...), custom_call_target="tpu_custom_call" | custom-call | flops 16000000000 | bytes 10000000 | tf_op jit(solution)/shard_map/coupling/pallas_call | solution.py:529
  (58 shorter events, 4.8 us)
Async XLA Ops:
  0.0 8.9 %collective-permute-start = (bf16[1280,128]{1,0:T(8,128)(2,1)}, bf16[1280,128]{1,0:T(8,128)(2,1)S(1)}, u32[]{:S(2)}, u32[]{:S(2)}) collective-permute-start(bf16[1280,128]{1,0:T(8,128)(2,1)} %middle_ref.1), channel_id=1, source_target_pairs={{0,1},{1,0},{2,3},{3,2},{4,5},{5,4},{6,7},{7,6},{8,9},{9,8},{10,11... | collective-permute-start | bytes 983048 | tf_op jit(solution)/shard_map/ppermute | solution.py:562
  0.7 8.6 %collective-permute-start.1 = (bf16[1280,128]{1,0:T(8,128)(2,1)}, bf16[1280,128]{1,0:T(8,128)(2,1)S(1)}, u32[]{:S(2)}, u32[]{:S(2)}) collective-permute-start(bf16[1280,128]{1,0:T(8,128)(2,1)} %middle_ref.1), channel_id=1, source_target_pairs={{1,2},{2,1},{5,6},{6,5},{9,10},{10,9},{13,14},{14,13},{17,18},{18,... | collective-permute-start | bytes 983048 | tf_op jit(solution)/shard_map/ppermute | solution.py:562
  4.4 1.0 %copy-start = (bf16[1280,128]{1,0:T(8,128)(2,1)S(1)}, bf16[1280,128]{1,0:T(8,128)(2,1)}, u32[]{:S(2)}) copy-start(bf16[1280,128]{1,0:T(8,128)(2,1)} %middle_ref.1) | copy-start | bytes 983044
  5.4 0.7 copy-start.1
  12.7 4.8 %collective-permute-start.2 = (bf16[4,208,128]{2,1,0:T(8,128)(2,1)S(1)}, bf16[4,208,128]{2,1,0:T(8,128)(2,1)S(1)}, u32[]{:S(2)}, u32[]{:S(2)}) collective-permute-start(bf16[4,208,128]{2,1,0:T(8,128)(2,1)S(1)} %get-tuple-element.38), channel_id=1, source_target_pairs={{0,4},{4,0},{8,12},{12,8},{16,20},{20,16},{24,28},{28,24},{1,5},{5... | collective-permute-start | bytes 638984 | tf_op jit(solution)/shard_map/ppermute | solution.py:552
  14.0 5.0 %collective-permute-start.4 = (bf16[4,208,128]{2,1,0:T(8,128)(2,1)S(1)}, bf16[4,208,128]{2,1,0:T(8,128)(2,1)S(1)}, u32[]{:S(2)}, u32[]{:S(2)}) collective-permute-start(bf16[4,208,128]{2,1,0:T(8,128)(2,1)S(1)} %get-tuple-element.40), channel_id=1, source_target_pairs={{0,8},{4,12},{8,0},{12,4},{16,24},{20,28},{24,16},{28,20},{1,9},{5... | collective-permute-start | bytes 638984 | tf_op jit(solution)/shard_map/ppermute | solution.py:552
  19.2 4.1 %collective-permute-start.3 = (bf16[2,208,128]{2,1,0:T(8,128)(2,1)S(1)}, bf16[2,208,128]{2,1,0:T(8,128)(2,1)S(1)}, u32[]{:S(2)}, u32[]{:S(2)}) collective-permute-start(bf16[2,208,128]{2,1,0:T(8,128)(2,1)S(1)} %slice.129), channel_id=1, source_target_pairs={{0,8},{4,12},{8,0},{12,4},{16,24},{20,28},{24,16},{28,20},{1,9},{5... | collective-permute-start | bytes 319496 | tf_op jit(solution)/shard_map/ppermute | solution.py:552
  19.4 4.1 %collective-permute-start.5 = (bf16[2,208,128]{2,1,0:T(8,128)(2,1)S(1)}, bf16[2,208,128]{2,1,0:T(8,128)(2,1)S(1)}, u32[]{:S(2)}, u32[]{:S(2)}) collective-permute-start(bf16[2,208,128]{2,1,0:T(8,128)(2,1)S(1)} %slice.138), channel_id=1, source_target_pairs={{0,4},{4,0},{8,12},{12,8},{16,20},{20,16},{24,28},{28,24},{1,5},{5... | collective-permute-start | bytes 319496 | tf_op jit(solution)/shard_map/ppermute | solution.py:552
  23.8 11.6 %collective-permute-start.6 = (bf16[4,208,128]{2,1,0:T(8,128)(2,1)S(1)}, bf16[4,208,128]{2,1,0:T(8,128)(2,1)S(1)}, u32[]{:S(2)}, u32[]{:S(2)}) collective-permute-start(bf16[4,208,128]{2,1,0:T(8,128)(2,1)S(1)} %pad_maximum_fusion.2), channel_id=1, source_target_pairs={{0,16},{4,20},{8,24},{12,28},{16,0},{20,4},{24,8},{28,12},{1,17},{... | collective-permute-start | bytes 638984 | tf_op jit(solution)/shard_map/ppermute | solution.py:552
  35.6 5.4 %collective-permute-start.7 = (bf16[2,208,128]{2,1,0:T(8,128)(2,1)S(1)}, bf16[2,208,128]{2,1,0:T(8,128)(2,1)S(1)}, u32[]{:S(2)}, u32[]{:S(2)}) collective-permute-start(bf16[2,208,128]{2,1,0:T(8,128)(2,1)S(1)} %pad_maximum_fusion.8), channel_id=1, source_target_pairs={{0,8},{4,12},{8,0},{12,4},{16,24},{20,28},{24,16},{28,20},{1,9},{5... | collective-permute-start | bytes 319496 | tf_op jit(solution)/shard_map/ppermute | solution.py:552
  38.1 3.6 %collective-permute-start.8 = (bf16[2,208,128]{2,1,0:T(8,128)(2,1)S(1)}, bf16[2,208,128]{2,1,0:T(8,128)(2,1)S(1)}, u32[]{:S(2)}, u32[]{:S(2)}) collective-permute-start(bf16[2,208,128]{2,1,0:T(8,128)(2,1)S(1)} %pad_maximum_fusion.9), channel_id=1, source_target_pairs={{0,4},{4,0},{8,12},{12,8},{16,20},{20,16},{24,28},{28,24},{1,5},{5... | collective-permute-start | bytes 319496 | tf_op jit(solution)/shard_map/ppermute | solution.py:552
  41.8 6.8 %collective-permute-start.9 = (bf16[4,208,128]{2,1,0:T(8,128)(2,1)S(1)}, bf16[4,208,128]{2,1,0:T(8,128)(2,1)S(1)}, u32[]{:S(2)}, u32[]{:S(2)}) collective-permute-start(bf16[4,208,128]{2,1,0:T(8,128)(2,1)S(1)} %pad_maximum_fusion.4.refs_0_.near_0), channel_id=1, source_target_pairs={{0,4},{4,0},{8,12},{12,8},{16,20},{20,16},{24,28},{28,24},{1,5},{5... | collective-permute-start | bytes 638984 | tf_op jit(solution)/shard_map/ppermute | solution.py:552
  42.0 6.6 %collective-permute-start.10 = (bf16[4,208,128]{2,1,0:T(8,128)(2,1)S(1)}, bf16[4,208,128]{2,1,0:T(8,128)(2,1)S(1)}, u32[]{:S(2)}, u32[]{:S(2)}) collective-permute-start(bf16[4,208,128]{2,1,0:T(8,128)(2,1)S(1)} %pad_maximum_fusion.5.refs_1_.near_1), channel_id=1, source_target_pairs={{0,8},{4,12},{8,0},{12,4},{16,24},{20,28},{24,16},{28,20},{1,9},{5... | collective-permute-start | bytes 638984 | tf_op jit(solution)/shard_map/ppermute | solution.py:552
  42.8 14.1 %collective-permute-start.11 = (bf16[4,208,128]{2,1,0:T(8,128)(2,1)S(1)}, bf16[4,208,128]{2,1,0:T(8,128)(2,1)S(1)}, u32[]{:S(2)}, u32[]{:S(2)}) collective-permute-start(bf16[4,208,128]{2,1,0:T(8,128)(2,1)S(1)} %get-tuple-element.57), channel_id=1, source_target_pairs={{0,1},{1,0},{2,3},{3,2},{4,5},{5,4},{6,7},{7,6},{8,9},{9,8},{10,11... | collective-permute-start | bytes 638984 | tf_op jit(solution)/shard_map/ppermute | solution.py:582
  44.7 12.2 %collective-permute-start.12 = (bf16[4,208,128]{2,1,0:T(8,128)(2,1)S(1)}, bf16[4,208,128]{2,1,0:T(8,128)(2,1)S(1)}, u32[]{:S(2)}, u32[]{:S(2)}) collective-permute-start(bf16[4,208,128]{2,1,0:T(8,128)(2,1)S(1)} %get-tuple-element.58), channel_id=1, source_target_pairs={{1,2},{2,1},{5,6},{6,5},{9,10},{10,9},{13,14},{14,13},{17,18},{18,... | collective-permute-start | bytes 638984 | tf_op jit(solution)/shard_map/ppermute | solution.py:582
  48.6 5.5 %copy-start.3 = (f32[256,256]{1,0:T(8,128)S(1)}, f32[256,256]{1,0:T(8,128)}, u32[]{:S(2)}) copy-start(f32[256,256]{1,0:T(8,128)} %constant.22.clone.inverse_ref) | copy-start | bytes 786436
  48.6 5.5 %copy-start.4 = (f32[256,256]{1,0:T(8,128)S(1)}, f32[256,256]{1,0:T(8,128)}, u32[]{:S(2)}) copy-start(f32[256,256]{1,0:T(8,128)} %constant.21.clone.to_weights_ref) | copy-start | bytes 786436
  48.6 5.5 %copy-start.5 = (f32[256,256]{1,0:T(8,128)S(1)}, f32[256,256]{1,0:T(8,128)}, u32[]{:S(2)}) copy-start(f32[256,256]{1,0:T(8,128)} %constant.20.clone.forward_ref) | copy-start | bytes 786436
  48.8 8.0 %collective-permute-start.13 = (bf16[4,208,128]{2,1,0:T(8,128)(2,1)S(1)}, bf16[4,208,128]{2,1,0:T(8,128)(2,1)S(1)}, u32[]{:S(2)}, u32[]{:S(2)}) collective-permute-start(bf16[4,208,128]{2,1,0:T(8,128)(2,1)S(1)} %get-tuple-element.59), channel_id=1, source_target_pairs={{0,1},{1,0},{2,3},{3,2},{4,5},{5,4},{6,7},{7,6},{8,9},{9,8},{10,11... | collective-permute-start | bytes 638984 | tf_op jit(solution)/shard_map/ppermute | solution.py:582
  50.3 7.2 %collective-permute-start.14 = (bf16[4,208,128]{2,1,0:T(8,128)(2,1)S(1)}, bf16[4,208,128]{2,1,0:T(8,128)(2,1)S(1)}, u32[]{:S(2)}, u32[]{:S(2)}) collective-permute-start(bf16[4,208,128]{2,1,0:T(8,128)(2,1)S(1)} %get-tuple-element.60), channel_id=1, source_target_pairs={{1,2},{2,1},{5,6},{6,5},{9,10},{10,9},{13,14},{14,13},{17,18},{18,... | collective-permute-start | bytes 638984 | tf_op jit(solution)/shard_map/ppermute | solution.py:582
  54.1 3.3 %copy-start.2 = (bf16[512,512]{1,0:T(8,128)(2,1)S(1)}, bf16[512,512]{1,0:T(8,128)(2,1)}, u32[]{:S(2)}) copy-start(bf16[512,512]{1,0:T(8,128)(2,1)} %constant.23.clone.factor_ref) | copy-start | bytes 1572868
